TPU v7x, 256 devices: a whole 4x4x8 slice. The times are simulated.
256 devices in a mesh: lat: 32 (over y, x, core), tok: 8 (over z).
Axes of the slice: x: 4, y: 4, z: 8, core: 2. Of those that a mesh axis runs over, the one named last changes fastest.
Arguments:
- acts_early: bfloat16 [512, 3584], P(('lat', 'tok')), may hold values from -6 to 6
- acts_late: bfloat16 [512, 3584], P(('lat', 'tok')), may hold values from -6 to 6
- enc_early: bfloat16 [3584, 131072], P(None, ('lat', 'tok')), may hold values from -0.09375 to 0.09375
- enc_late: bfloat16 [3584, 131072], P(None, ('lat', 'tok')), may hold values from -0.09375 to 0.09375
- bias_early: float32 [131072], P(('lat', 'tok')), may hold values from -3 to 3
- bias_late: float32 [131072], P(('lat', 'tok')), may hold values from -3 to 3
- thresh_early: float32 [131072], P(('lat', 'tok')), may hold values from 0.1 to 2
- thresh_late: float32 [131072], P(('lat', 'tok')), may hold values from 0.1 to 2
- pair_blocks: int32 [4096, 2], P('lat'), may hold values from 0 to 1023, as said below
- live_pairs: int32 [32], P('lat'), may hold values from 32 to 128, as said below
Outputs:
- gram_tiles: float32 [4096, 128, 128], P(('lat', 'tok'))
Inputs may be any that keep to these rules, and one draw needn't show every extreme that they name: `pair_blocks`: block numbers count blocks of 128 latents; latent group g holds blocks g * 32 to g * 32 + 31. In each column, the 128 rows of one owner name every latent group exactly 4 times. `live_pairs`: some owner has all 128 slots live.
All inputs are finite; a program needn't handle non-finite values.
Results may differ from a plain program's by a relative error of at most 0.00035.
Values may be sent and summed in bfloat16 or wider, within the bound.
No kernel may reach another device: no remote copies, remote signals or barrier semaphores. Data moves between devices by JAX's collectives and lax.ppermute only.
A program may use at most 64 MiB of HBM per device.

v0:
```python
import jax
import jax.numpy as jnp
from jax import lax
from jax.sharding import PartitionSpec as P

BLOCK = 128
FROM_GROUP = 4


def soft_jump(preact, thresh):
    return preact * jnp.clip(2.0 * preact / thresh - 1.0, 0.0, 1.0)


def slot_ranking(source):
    width = source.shape[-1]
    same_src = source[..., :, None] == source[..., None, :]
    before = jnp.arange(width)[None, :] < jnp.arange(width)[:, None]
    return jnp.sum(same_src & before, axis=-1)


def encode(acts, weight, bias_vec, thresh):
    preact = (
        jnp.dot(
            lax.all_gather(acts, ("lat", "tok"), axis=0, tiled=True),
            weight,
            preferred_element_type=jnp.float32,
        )
        + bias_vec
    )
    return soft_jump(preact, thresh).astype(jnp.bfloat16)


def regroup(codes):
    return lax.all_to_all(codes, "tok", split_axis=0, concat_axis=1, tiled=True)


def outgoing(column, is_live, local_codes, my_group, group_blocks):
    source = column // group_blocks
    within = column % group_blocks
    ranking = slot_ranking(source)
    chosen = is_live & (source == my_group)
    by_rank = ((ranking[..., None] == jnp.arange(FROM_GROUP)) & chosen[..., None]).astype(
        jnp.float32
    )
    by_block = (within[..., None] == jnp.arange(group_blocks)).astype(jnp.float32)
    selector = jnp.einsum("gsm,gsb->gmb", by_rank, by_block).astype(jnp.bfloat16)
    stacked = local_codes.reshape(local_codes.shape[0], group_blocks, BLOCK)
    return jnp.einsum(
        "gmb,tbc->gmtc", selector, stacked, preferred_element_type=jnp.float32
    ).astype(jnp.bfloat16)


def incoming(column, live_count, received, group_blocks):
    slot_count = column.shape[0]
    source = column // group_blocks
    flat_slot = source * FROM_GROUP + slot_ranking(source)
    is_live = jnp.arange(slot_count) < live_count
    targets = jnp.arange(received.shape[0] * FROM_GROUP)
    picker = ((flat_slot[:, None] == targets[None, :]) & is_live[:, None]).astype(jnp.bfloat16)
    row_table = received.reshape(
        received.shape[0] * FROM_GROUP, received.shape[2] * received.shape[3]
    )
    picked = jnp.dot(picker, row_table, preferred_element_type=jnp.float32).astype(jnp.bfloat16)
    return picked.reshape(slot_count, received.shape[2], received.shape[3])


def shards(
    acts_early,
    acts_late,
    enc_early,
    enc_late,
    bias_early,
    bias_late,
    thresh_early,
    thresh_late,
    pair_blocks,
    live_pairs,
):
    rank_count = lax.axis_size("tok")
    my_group = lax.axis_index("lat")
    codes_early = encode(acts_early, enc_early, bias_early, thresh_early)
    local_early = regroup(codes_early)
    codes_late = encode(acts_late, enc_late, bias_late, thresh_late)
    local_late = regroup(codes_late)
    group_blocks = local_early.shape[1] // BLOCK
    all_pairs, all_counts = (
        lax.all_gather(pair_blocks, "lat", axis=0, tiled=True),
        lax.all_gather(live_pairs, "lat", axis=0, tiled=True),
    )
    group_count = all_counts.shape[0]
    slot_count = pair_blocks.shape[0]
    pair_table = all_pairs.reshape(group_count, slot_count, 2)
    is_live = jnp.arange(slot_count)[None, :] < all_counts[:, None]
    send_early = outgoing(pair_table[:, :, 0], is_live, local_early, my_group, group_blocks)
    send_late = outgoing(pair_table[:, :, 1], is_live, local_late, my_group, group_blocks)
    recv_early, recv_late = (
        lax.all_to_all(send_early, "lat", split_axis=0, concat_axis=0, tiled=True),
        lax.all_to_all(send_late, "lat", split_axis=0, concat_axis=0, tiled=True),
    )
    slot_early = incoming(pair_blocks[:, 0], live_pairs[0], recv_early, group_blocks)
    slot_late = incoming(pair_blocks[:, 1], live_pairs[0], recv_late, group_blocks)
    tok_rows = local_early.shape[0]
    gram_sums = lax.psum_scatter(
        jnp.einsum("ktc,ktd->kcd", slot_early, slot_late, preferred_element_type=jnp.float32),
        "tok",
        scatter_dimension=0,
        tiled=True,
    )
    return gram_sums / (tok_rows * rank_count)


def solution(mesh):
    in_specs = (
        P(("lat", "tok"), None),
        P(("lat", "tok"), None),
        P(None, ("lat", "tok")),
        P(None, ("lat", "tok")),
        P(("lat", "tok")),
        P(("lat", "tok")),
        P(("lat", "tok")),
        P(("lat", "tok")),
        P("lat", None),
        P("lat"),
    )
    out_specs = P(("lat", "tok"), None, None)
    return jax.shard_map(shards, mesh=mesh, in_specs=in_specs, out_specs=out_specs, check_vma=False)
```

profile of v0, /device:TPU:1, one launch (start us, length us, event | category | flops | bytes accessed | tf_op | source)
XLA Modules:
  0.0 458.4 jit_solution(14923905379886875757)
XLA Ops:
  6.5 0.7 all-gather.5.cloned.1.call-update
  7.3 0.7 all-gather.7.cloned.1.call-update
  8.7 25.8 %all_gather.12 = s32[4096,2]{0,1:T(2,128)S(1)} all-gather(s32[128,2]{0,1:T(2,128)} %param.18), channel_id=1, replica_groups=mesh['lat'=32,'tok'=8] {'lat'}, dimensions={0}, use_global_device_ids=true | all-gather | bytes 33792 | tf_op jit(solution)/shard_map/all_gather | solution.py:87
  34.4 1.3 dynamic-slice
  35.7 0.8 dynamic-update-slice
  36.5 11.3 %all-reduce = s32[32]{0:T(128)S(1)} all-reduce(s32[32]{0:T(128)S(1)} %dynamic-update-slice), channel_id=1, replica_groups=mesh['lat'=32,'tok'=8] {'lat'}, use_global_device_ids=true, to_apply=%add | all-reduce | flops 32 | bytes 256
  47.8 81.9 %all-gather.5.cloned.1.call-done = bf16[256,2,3584]{2,1,0:T(2,128)(2,1)} async-done(((bf16[1,2,3584]{2,1,0:T(2,128)(2,1)}), bf16[256,2,3584]{2,1,0:T(2,128)(2,1)}) %all-gather.5.cloned.1.call-update) | async-done | bytes 3670032 | tf_op jit(solution)/shard_map/all_gather | solution.py:24
  129.7 8.4 %reshape.215 = bf16[512,3584]{1,0:T(8,128)(2,1)} reshape(bf16[256,2,3584]{2,1,0:T(2,128)(2,1)} %all-gather.5.cloned.1.call-done) | data formatting | bytes 7340032
  138.1 6.1 %multiply_convert_fusion.1 = bf16[512,512]{1,0:T(8,128)(2,1)} fusion(bf16[512,3584]{1,0:T(8,128)(2,1)} %reshape.215, bf16[3584,512]{1,0:T(8,128)(2,1)} %param.12, f32[512]{0:T(512)S(1)} %copy-done.1, f32[512]{0:T(512)S(1)} %copy-done.2), kind=kOutput, calls=%fused_computation.19 | convolution fusion | flops 1880883200 | bytes 7868416 | tf_op jit(solution)/shard_map/dot_general | solution.py:23
  144.2 4.2 all-to-all-start
  148.5 98.3 %all-gather.7.cloned.1.call-done = bf16[256,2,3584]{2,1,0:T(2,128)(2,1)} async-done(((bf16[1,2,3584]{2,1,0:T(2,128)(2,1)}), bf16[256,2,3584]{2,1,0:T(2,128)(2,1)}) %all-gather.7.cloned.1.call-update) | async-done | bytes 3670032 | tf_op jit(solution)/shard_map/all_gather | solution.py:24
  246.8 8.4 %reshape.217 = bf16[512,3584]{1,0:T(8,128)(2,1)} reshape(bf16[256,2,3584]{2,1,0:T(2,128)(2,1)} %all-gather.7.cloned.1.call-done) | data formatting | bytes 7340032
  255.2 6.1 %multiply_convert_fusion = bf16[512,512]{1,0:T(8,128)(2,1)} fusion(bf16[512,3584]{1,0:T(8,128)(2,1)} %reshape.217, bf16[3584,512]{1,0:T(8,128)(2,1)} %param.13, f32[512]{0:T(512)S(1)} %copy-done.3, f32[512]{0:T(512)S(1)} %copy-done.4), kind=kOutput, calls=%fused_computation.18 | convolution fusion | flops 1880883200 | bytes 7868416 | tf_op jit(solution)/shard_map/dot_general | solution.py:23
  261.3 4.2 all-to-all-start.2
  265.6 2.6 convert_reduce_fusion
  268.7 0.3 reshape.221
  269.0 0.7 convolution_convert_fusion.3
  269.7 2.1 copy.25
  271.9 11.6 %all-to-all-done.2 = bf16[8,64,512]{2,1,0:T(8,128)(2,1)S(1)} async-done(((bf16[8,64,512]{2,1,0:T(8,128)(2,1)}), bf16[8,64,512]{2,1,0:T(8,128)(2,1)S(1)}, u32[]{:S(2)}, u32[]{:S(2)}) %all-to-all-start.2) | async-done | bytes 524320 | tf_op jit(solution)/shard_map/all_to_all | solution.py:34
  283.5 6.1 %all-to-all-start.1 = ((bf16[32,4,64,128]{3,2,1,0:T(8,128)(2,1)}), bf16[32,4,64,128]{3,2,1,0:T(8,128)(2,1)S(1)}, u32[]{:S(2)}, u32[]{:S(2)}) async-start(bf16[32,4,64,128]{3,2,1,0:T(8,128)(2,1)} %copy.25), calls=%async_computation.1 | async-start | bytes 4194304 | tf_op jit(solution)/shard_map/all_to_all | solution.py:97
  290.5 0.7 convolution_convert_fusion.2
  291.2 2.1 copy.28
  293.4 24.1 %all-to-all-done.1 = bf16[32,4,64,128]{3,2,1,0:T(8,128)(2,1)S(1)} async-done(((bf16[32,4,64,128]{3,2,1,0:T(8,128)(2,1)}), bf16[32,4,64,128]{3,2,1,0:T(8,128)(2,1)S(1)}, u32[]{:S(2)}, u32[]{:S(2)}) %all-to-all-start.1) | async-done | bytes 2097184 | tf_op jit(solution)/shard_map/all_to_all | solution.py:97
  317.5 6.9 %all-to-all-start.3 = ((bf16[32,4,64,128]{3,2,1,0:T(8,128)(2,1)}), bf16[32,4,64,128]{3,2,1,0:T(8,128)(2,1)}, u32[]{:S(2)}, u32[]{:S(2)}) async-start(bf16[32,4,64,128]{3,2,1,0:T(8,128)(2,1)} %copy.28), calls=%async_computation.3 | async-start | bytes 4194304 | tf_op jit(solution)/shard_map/all_to_all | solution.py:98
  324.9 1.6 fusion.4
  326.5 0.6 copy.37
  327.2 25.2 %all-to-all-done.3 = bf16[32,4,64,128]{3,2,1,0:T(8,128)(2,1)} async-done(((bf16[32,4,64,128]{3,2,1,0:T(8,128)(2,1)}), bf16[32,4,64,128]{3,2,1,0:T(8,128)(2,1)}, u32[]{:S(2)}, u32[]{:S(2)}) %all-to-all-start.3) | async-done | bytes 2097184 | tf_op jit(solution)/shard_map/all_to_all | solution.py:98
  352.4 3.2 fusion.7
  355.6 0.6 copy.39
  356.2 4.6 fusion.54
  360.8 88.8 %reduce-scatter.2.cloned.1.call-done = f32[16,128,128]{2,1,0:T(8,128)} async-done(((f32[128,128,128]{2,1,0:T(8,128)}), f32[16,128,128]{2,1,0:T(8,128)}) %reduce-scatter.2.cloned.1.call-update) | async-done | bytes 1048592 | tf_op jit(solution)/shard_map/reduce_scatter | solution.py:103
  449.6 2.3 broadcast_multiply_fusion
  (33 shorter events, 2.1 us)
Async XLA Ops:
  6.5 123.2 %all-gather.5.cloned.1.call-start = ((), (), s32[]{:S(2)}) async-start(), calls=%async_computation.6 | async-start | bytes 3684352 | tf_op jit(solution)/shard_map/all_gather | solution.py:24
  7.3 239.6 %all-gather.7.cloned.1.call-start = ((), (), s32[]{:S(2)}) async-start(), calls=%async_computation.7 | async-start | bytes 3684352 | tf_op jit(solution)/shard_map/all_gather | solution.py:24
  47.8 90.4 %copy-start.1 = (f32[512]{0:T(512)S(1)}, f32[512]{0:T(512)}, u32[]{:S(2)}) copy-start(f32[512]{0:T(512)} %param.16) | copy-start | bytes 6148
  47.8 90.3 %copy-start.2 = (f32[512]{0:T(512)S(1)}, f32[512]{0:T(512)}, u32[]{:S(2)}) copy-start(f32[512]{0:T(512)} %param.14) | copy-start | bytes 6148
  144.2 117.1 %all-to-all-start = ((bf16[8,64,512]{2,1,0:T(8,128)(2,1)}), bf16[8,64,512]{2,1,0:T(8,128)(2,1)S(1)}, u32[]{:S(2)}, u32[]{:S(2)}) async-start(bf16[8,64,512]{2,1,0:T(8,128)(2,1)} %bitcast.12), calls=%async_computation | async-start | bytes 1048576 | tf_op jit(solution)/shard_map/all_to_all | solution.py:34
  148.5 106.7 %copy-start.3 = (f32[512]{0:T(512)S(1)}, f32[512]{0:T(512)}, u32[]{:S(2)}) copy-start(f32[512]{0:T(512)} %param.17) | copy-start | bytes 6148
  148.5 106.7 %copy-start.4 = (f32[512]{0:T(512)S(1)}, f32[512]{0:T(512)}, u32[]{:S(2)}) copy-start(f32[512]{0:T(512)} %param.15) | copy-start | bytes 6148
  261.3 22.2 %all-to-all-start.2 = ((bf16[8,64,512]{2,1,0:T(8,128)(2,1)}), bf16[8,64,512]{2,1,0:T(8,128)(2,1)S(1)}, u32[]{:S(2)}, u32[]{:S(2)}) async-start(bf16[8,64,512]{2,1,0:T(8,128)(2,1)} %bitcast.24), calls=%async_computation.2 | async-start | bytes 1048576 | tf_op jit(solution)/shard_map/all_to_all | solution.py:34
  283.5 34.0 %all-to-all-start.1 = ((bf16[32,4,64,128]{3,2,1,0:T(8,128)(2,1)}), bf16[32,4,64,128]{3,2,1,0:T(8,128)(2,1)S(1)}, u32[]{:S(2)}, u32[]{:S(2)}) async-start(bf16[32,4,64,128]{3,2,1,0:T(8,128)(2,1)} %copy.25), calls=%async_computation.1 | async-start | bytes 4194304 | tf_op jit(solution)/shard_map/all_to_all | solution.py:97
  293.4 31.1 %copy-start = (s32[128,2]{0,1:T(2,128)S(1)}, s32[128,2]{0,1:T(2,128)}, u32[]{:S(2)}) copy-start(s32[128,2]{0,1:T(2,128)} %param.18) | copy-start | bytes 3076
  317.5 34.9 %all-to-all-start.3 = ((bf16[32,4,64,128]{3,2,1,0:T(8,128)(2,1)}), bf16[32,4,64,128]{3,2,1,0:T(8,128)(2,1)}, u32[]{:S(2)}, u32[]{:S(2)}) async-start(bf16[32,4,64,128]{3,2,1,0:T(8,128)(2,1)} %copy.28), calls=%async_computation.3 | async-start | bytes 4194304 | tf_op jit(solution)/shard_map/all_to_all | solution.py:98
  324.4 125.2 %reduce-scatter.2.cloned.1.call-start = ((), (), s32[]{:S(2)}) async-start(), calls=%async_computation.5 | async-start | bytes 9437184 | tf_op jit(solution)/shard_map/reduce_scatter | solution.py:103
Sparse Core Ops, SparseCore 0:
  11.1 118.5 all-gather.4
  133.5 113.2 all-gather.6
  360.9 88.6 reduce-scatter.1
where the time goes:
time: 459 us; the launch traced here: 458 us
  waiting for transfers between devices  331 us (72%)
  blocking collectives  37.1 us (8%)
  local copies, waits for them, and re-layouts  25.5 us (6%)
  matrix products  23.4 us (5%)
  starting transfers between devices  21.6 us (5%)
  between operations  14 us (3%)
  other arithmetic  5.4 us (1%)
    all_gather x2, waiting for transfers between devices, encode(): lax.all_gather(acts, ('lat', 'tok'), axis=0, tiled=True)  180 us
    reduce_scatter x1, waiting for transfers between devices, shards(): lax.psum_scatter(jnp.einsum('ktc,ktd->kcd', slot_early, slot_late, prefer...  88.8 us
    all_gather x1, blocking collectives, shards(): lax.all_gather(pair_blocks, 'lat', axis=0, tiled=True)  25.8 us
    all_to_all x1, waiting for transfers between devices, shards(): lax.all_to_all(send_late, 'lat', split_axis=0, concat_axis=0, tiled=True)  25.2 us
    all_to_all x1, waiting for transfers between devices, shards(): lax.all_to_all(send_early, 'lat', split_axis=0, concat_axis=0, tiled=True)  24.1 us
    unnamed x18, local copies, waits for them, and re-layouts  20 us
    dot_general x2, matrix products, encode(): jnp.dot(lax.all_gather(acts, ('lat', 'tok'), axis=0, tiled=True), weight,...  12.2 us
    all_to_all x2, waiting for transfers between devices, regroup(): return lax.all_to_all(codes, 'tok', split_axis=0, concat_axis=1, tiled=True)  11.6 us
  transfers between devices with their start and end apart: 7, of which 6 were waited for; matrix products, arithmetic and copies ran while one was open for 10% of the time, Pallas kernels for 0%

commit v1 on v0

v1 whole, which is shorter than its diff:
```python
import jax
import jax.numpy as jnp
from jax import lax
from jax.experimental import pallas as pl
from jax.experimental.pallas import tpu as pltpu
from jax.sharding import Mesh, PartitionSpec as P

BLOCK = 128
FROM_GROUP = 4
GROUPS = 32
RANKS = 8
TOKENS = 512
ALL = ("y", "x", "c", "z")
LAT = ("y", "x", "c")
MIB = 1 << 20


def encode_kernel(core_ref, own_ref, other_ref, w_ref, bias_ref, thresh_ref, out_ref):
    core = core_ref[0]
    rows = own_ref.shape[0] // RANKS
    for side, acts_ref in enumerate((own_ref, other_ref)):
        half = core if side == 0 else 1 - core
        at = pl.multiple_of(half * rows, rows)
        preact = jnp.dot(acts_ref[...], w_ref[...], preferred_element_type=jnp.float32) + bias_ref[...]
        codes = preact * jnp.clip(2.0 * preact / thresh_ref[...] - 1.0, 0.0, 1.0)
        codes = codes.astype(jnp.bfloat16)
        for t in range(RANKS):
            for j in range(out_ref.shape[1]):
                out_ref[t, j, pl.ds(at, rows), :] = codes[
                    t * rows : (t + 1) * rows, j * BLOCK : (j + 1) * BLOCK
                ]


def encode(core, own, other, weight, bias_vec, thresh):
    half, depth = own.shape
    width = weight.shape[1]
    step = 256
    return pl.pallas_call(
        encode_kernel,
        grid_spec=pltpu.PrefetchScalarGridSpec(
            num_scalar_prefetch=1,
            grid=(width // step,),
            in_specs=[
                pl.BlockSpec((half, depth), lambda i, s: (0, 0)),
                pl.BlockSpec((half, depth), lambda i, s: (0, 0)),
                pl.BlockSpec((depth, step), lambda i, s: (0, i)),
                pl.BlockSpec((1, step), lambda i, s: (0, i)),
                pl.BlockSpec((1, step), lambda i, s: (0, i)),
            ],
            out_specs=pl.BlockSpec(
                (RANKS, step // BLOCK, 2 * half // RANKS, BLOCK), lambda i, s: (0, i, 0, 0)
            ),
        ),
        out_shape=jax.ShapeDtypeStruct(
            (RANKS, width // BLOCK, 2 * half // RANKS, BLOCK), jnp.bfloat16
        ),
        compiler_params=pltpu.CompilerParams(vmem_limit_bytes=24 * MIB),
        cost_estimate=pl.CostEstimate(
            flops=4 * half * depth * width, bytes_accessed=8 * MIB, transcendentals=0
        ),
        name="encode",
    )(core, own, other, weight, bias_vec[None], thresh[None])


def pick_kernel(index_ref, blocks_ref, out_ref):
    def body(i, carry):
        out_ref[i] = blocks_ref[index_ref[i]]
        return carry

    lax.fori_loop(0, out_ref.shape[0], body, 0, unroll=8)


def pick(index, blocks):
    count = index.shape[0]
    return pl.pallas_call(
        pick_kernel,
        in_specs=[
            pl.BlockSpec(memory_space=pltpu.SMEM),
            pl.BlockSpec(memory_space=pltpu.VMEM),
        ],
        out_specs=pl.BlockSpec(memory_space=pltpu.VMEM),
        out_shape=jax.ShapeDtypeStruct((count,) + blocks.shape[1:], blocks.dtype),
        compiler_params=pltpu.CompilerParams(vmem_limit_bytes=16 * MIB),
        cost_estimate=pl.CostEstimate(flops=0, bytes_accessed=3 * MIB, transcendentals=0),
        name="pick",
    )(index, blocks)


def tile_kernel(left_at, right_at, live_ref, left_ref, right_ref, out_ref):
    count = out_ref.shape[0]
    first = pl.program_id(0) * count
    live = live_ref[0]
    for i in range(count):
        slot = first + i

        @pl.when(slot < live)
        def _():
            gram = lax.dot_general(
                left_ref[left_at[slot]],
                right_ref[right_at[slot]],
                (((0,), (0,)), ((), ())),
                preferred_element_type=jnp.float32,
            )
            out_ref[i] = gram * (1.0 / TOKENS)

        @pl.when(slot >= live)
        def _():
            out_ref[i] = jnp.zeros(out_ref.shape[1:], jnp.float32)


def tiles(left_at, right_at, live, left, right):
    slots = left_at.shape[0]
    step = slots // RANKS
    return pl.pallas_call(
        tile_kernel,
        grid_spec=pltpu.PrefetchScalarGridSpec(
            num_scalar_prefetch=3,
            grid=(slots // step,),
            in_specs=[
                pl.BlockSpec(left.shape, lambda i, *s: (0, 0, 0)),
                pl.BlockSpec(right.shape, lambda i, *s: (0, 0, 0)),
            ],
            out_specs=pl.BlockSpec((step, BLOCK, BLOCK), lambda i, *s: (i, 0, 0)),
        ),
        out_shape=jax.ShapeDtypeStruct((slots, BLOCK, BLOCK), jnp.float32),
        compiler_params=pltpu.CompilerParams(vmem_limit_bytes=24 * MIB),
        cost_estimate=pl.CostEstimate(
            flops=2 * slots * 64 * BLOCK * BLOCK, bytes_accessed=12 * MIB, transcendentals=0
        ),
        name="tiles",
    )(left_at, right_at, live, left, right)


def positions(pair_blocks, group_blocks):
    source = pair_blocks // group_blocks
    within = pair_blocks % group_blocks
    slots = pair_blocks.shape[0]
    order = jnp.arange(slots)
    same = source[:, None, :] == source[None, :, :]
    before = (order[None, :] < order[:, None])[:, :, None]
    rank = jnp.sum(same & before, axis=1, dtype=jnp.int32)
    position = source * FROM_GROUP + rank
    hit = position[None, :, :] == order[:, None, None]
    table = jnp.sum(jnp.where(hit, within[None, :, :], 0), axis=1, dtype=jnp.int32)
    return position, table


def gather_z(acts):
    spread = jnp.broadcast_to(acts[None], (RANKS,) + acts.shape)
    return lax.all_to_all(spread, "z", 0, 0, tiled=True)


def shards(
    acts_early,
    acts_late,
    enc_early,
    enc_late,
    bias_early,
    bias_late,
    thresh_early,
    thresh_late,
    pair_blocks,
    live_pairs,
):
    core = lax.axis_index("c").astype(jnp.int32)[None]
    swap = [(0, 1), (1, 0)]
    depth = acts_early.shape[1]
    group_blocks = RANKS * enc_early.shape[1] // BLOCK

    near = gather_z(jnp.stack([acts_early, acts_late]))
    position, table = positions(pair_blocks, group_blocks)
    asked = lax.all_to_all(
        table.reshape(GROUPS, FROM_GROUP * 2), LAT, split_axis=0, concat_axis=0, tiled=True
    ).reshape(GROUPS * FROM_GROUP, 2)

    picked = []
    for layer, (weight, bias_vec, thresh) in enumerate(
        ((enc_early, bias_early, thresh_early), (enc_late, bias_late, thresh_late))
    ):
        own = lax.all_gather(
            near[:, layer].reshape(-1, depth), ("y", "x"), axis=0, tiled=True
        )
        other = lax.ppermute(own, "c", swap)
        codes = encode(core, own, other, weight, bias_vec, thresh)
        codes = lax.all_to_all(codes, "z", split_axis=0, concat_axis=0, tiled=True)
        blocks = codes.reshape((group_blocks,) + codes.shape[2:])
        sent = pick(asked[:, layer], blocks)
        got = lax.all_to_all(
            sent.reshape((GROUPS, FROM_GROUP) + sent.shape[1:]),
            LAT,
            split_axis=0,
            concat_axis=0,
            tiled=True,
        )
        picked.append(got.reshape(sent.shape))

    sums = tiles(position[:, 0], position[:, 1], live_pairs, picked[0], picked[1])
    return lax.psum_scatter(sums, "z", scatter_dimension=0, tiled=True)


def solution(mesh):
    fine = Mesh(mesh.devices.reshape(4, 4, 2, RANKS), ALL)
    in_specs = (
        P(ALL, None),
        P(ALL, None),
        P(None, ALL),
        P(None, ALL),
        P(ALL),
        P(ALL),
        P(ALL),
        P(ALL),
        P(LAT, None),
        P(LAT),
    )
    out_specs = P(ALL, None, None)
    return jax.shard_map(shards, mesh=fine, in_specs=in_specs, out_specs=out_specs, check_vma=False)
```

time: 459 us -> 384 us (0.84)
  waiting for transfers between devices: 331 us -> 274 us
  matrix products: 23.4 us -> 0 us
  Pallas kernels: 0 us -> 22.7 us
  blocking collectives: 37.1 us -> 18.6 us
  starting transfers between devices: 21.6 us -> 33.2 us
  local copies, waits for them, and re-layouts: 25.5 us -> 17.4 us
    all_gather x2, waiting for transfers between devices: 180 us -> 95.1 us  [shards(): lax.all_gather(near[:, layer].reshape(-1, depth), ('y', 'x'), axis=0, til...]
    all_gather x1 -> x0, blocking collectives: 25.8 us -> none  [shards(): lax.all_gather(pair_blocks, 'lat', axis=0, tiled=True)]
    dot_general x9 -> x0, matrix products: 23.4 us -> none  [the longest x2 12.2 us: encode(): jnp.dot(lax.all_gather(acts, ('lat', 'tok'), axis=0, tiled=True), weight,...]
    pallas_call x0 -> x5, Pallas kernels: none -> 22.7 us  [the longest x1 13.2 us: tiles(): pl.pallas_call(tile_kernel, grid_spec=pltpu.PrefetchScalarGridSpec(num_sc...]
    all_to_all x0 -> x1, blocking collectives: none -> 18.6 us  [gather_z(): return lax.all_to_all(spread, 'z', 0, 0, tiled=True)]
    all_to_all x4 -> x5, waiting for transfers between devices: 61 us -> 78.5 us  [the longest x2 53 us: shards(): lax.all_to_all(sent.reshape((GROUPS, FROM_GROUP) + sent.shape[1:]), LAT,...]
    reduce_scatter x1, waiting for transfers between devices: 88.8 us -> 101 us  [shards(): return lax.psum_scatter(sums, 'z', scatter_dimension=0, tiled=True)]
    unnamed x1 -> x0, blocking collectives: 11.3 us -> none
  transfers between devices with their start and end apart: 7 -> 10, of which waited for: 6 -> 7; matrix products, arithmetic and copies ran while one was open for 10% -> 1% of each run, Pallas kernels for 0% -> 2%
where the time goes in v1:
time: 384 us; the launch traced here: 383 us
  waiting for transfers between devices  274 us (71%)
  starting transfers between devices  33.2 us (9%)
  Pallas kernels  22.7 us (6%)
  blocking collectives  18.6 us (5%)
  local copies, waits for them, and re-layouts  17.4 us (5%)
  between operations  14 us (4%)
    reduce_scatter x1, waiting for transfers between devices, shards(): return lax.psum_scatter(sums, 'z', scatter_dimension=0, tiled=True)  101 us
    all_gather x2, waiting for transfers between devices, shards(): lax.all_gather(near[:, layer].reshape(-1, depth), ('y', 'x'), axis=0, til...  95.1 us
    all_to_all x2, waiting for transfers between devices, shards(): lax.all_to_all(sent.reshape((GROUPS, FROM_GROUP) + sent.shape[1:]), LAT,...  53 us
    all_to_all x2, waiting for transfers between devices, shards(): codes = lax.all_to_all(codes, 'z', split_axis=0, concat_axis=0, tiled=True)  25.5 us
    all_to_all x1, blocking collectives, gather_z(): return lax.all_to_all(spread, 'z', 0, 0, tiled=True)  18.6 us
    all_to_all x2, starting transfers between devices, shards(): lax.all_to_all(sent.reshape((GROUPS, FROM_GROUP) + sent.shape[1:]), LAT,...  14.2 us
    unnamed x26, local copies, waits for them, and re-layouts  14.2 us
    pallas_call x1, Pallas kernels, tiles(): pl.pallas_call(tile_kernel, grid_spec=pltpu.PrefetchScalarGridSpec(num_sc...  13.2 us
  transfers between devices with their start and end apart: 10, of which 7 were waited for; matrix products, arithmetic and copies ran while one was open for 1% of the time, Pallas kernels for 2%

profile of v1, /device:TPU:1, one launch (start us, length us, event | category | flops | bytes accessed | tf_op | source)
XLA Modules:
  0.0 382.6 jit_solution(15541631595004645186)
XLA Ops:
  6.5 0.8 pad_maximum_fusion
  7.5 18.6 %all_to_all.34 = bf16[8,2,2,3584]{3,2,1,0:T(2,128)(2,1)S(1)} all-to-all(bf16[8,2,2,3584]{3,2,1,0:T(2,128)(2,1)S(1)} %broadcast_in_dim.44), channel_id=1, replica_groups=mesh['y'=4,'x'=4,'c'=2,'z'=8] {'z'}, dimensions={0} | all-to-all | bytes 458752 | tf_op jit(solution)/shard_map/all_to_all | solution.py:150
  26.2 0.7 reshape_squeeze.6
  27.7 45.7 %all-gather.3.cloned.1.call-done.own_ref = bf16[256,3584]{1,0:T(8,128)(2,1)} async-done(((bf16[16,3584]{1,0:T(8,128)(2,1)}), bf16[256,3584]{1,0:T(8,128)(2,1)}) %all-gather.3.cloned.1.call-update) | async-done | bytes 1835024 | tf_op jit(solution)/shard_map/all_gather | solution.py:180
  73.4 1.8 collective-permute-start
  75.2 49.4 %all-gather.5.cloned.1.call-done.own_ref = bf16[256,3584]{1,0:T(8,128)(2,1)} async-done(((bf16[16,3584]{1,0:T(8,128)(2,1)}), bf16[256,3584]{1,0:T(8,128)(2,1)}) %all-gather.5.cloned.1.call-update) | async-done | bytes 1835024 | tf_op jit(solution)/shard_map/all_gather | solution.py:180
  124.6 1.8 collective-permute-start.1
  126.4 0.7 and_select_fusion
  128.2 5.1 %all-to-all-start = ((s32[32,1,8]{2,1,0:T(1,128)}), s32[32,1,8]{2,1,0:T(1,128)S(1)}, u32[]{:S(2)}, u32[]{:S(2)}) async-start(s32[32,1,8]{2,1,0:T(1,128)} %bitcast.2), calls=%async_computation | async-start | bytes 32768 | tf_op jit(solution)/shard_map/all_to_all | solution.py:172
  133.4 1.2 copy-done.7
  134.6 2.0 copy-done.3
  136.7 1.5 copy-done.6
  138.2 1.5 copy-done.8
  139.7 3.3 encode.2
  143.0 6.7 %all-to-all-start.2 = ((bf16[8,4,64,128]{3,2,1,0:T(8,128)(2,1)}), bf16[8,4,64,128]{3,2,1,0:T(8,128)(2,1)S(1)}, u32[]{:S(2)}, u32[]{:S(2)}) async-start(bf16[8,4,64,128]{3,2,1,0:T(8,128)(2,1)} %encode.2), calls=%async_computation.2 | async-start | bytes 1048576 | tf_op jit(solution)/shard_map/all_to_all | solution.py:185
  149.8 2.0 copy-done.4
  151.8 4.7 %encode.3 = bf16[8,4,64,128]{3,2,1,0:T(8,128)(2,1)} custom-call(s32[1]{0:T(128)} %bitcast.3.core_ref, bf16[256,3584]{1,0:T(8,128)(2,1)S(1)} %copy-done.5, bf16[256,3584]{1,0:T(8,128)(2,1)} %collective-permute-done.1.other_ref, bf16[3584,512]{1,0:T(8,128)(2,1)S(1)} %copy-done.4, f32[1,512]{1,0:T(1,128)S(1)} %bitcast.25, f32[1,512]{1,0:T(1,128)S(1)} %bitcast.26), custom_call_target="tpu_custom_call" | custom-call | flops 1879048192 | bytes 8388608 | tf_op jit(solution)/shard_map/encode/pallas_call | solution.py:38
  156.5 11.2 %all-to-all-done.2 = bf16[8,4,64,128]{3,2,1,0:T(8,128)(2,1)S(1)} async-done(((bf16[8,4,64,128]{3,2,1,0:T(8,128)(2,1)}), bf16[8,4,64,128]{3,2,1,0:T(8,128)(2,1)S(1)}, u32[]{:S(2)}, u32[]{:S(2)}) %all-to-all-start.2) | async-done | bytes 524320 | tf_op jit(solution)/shard_map/all_to_all | solution.py:185
  167.7 3.5 all-to-all-start.4
  171.7 0.7 reduce.7
  172.6 0.8 pick.2
  173.4 1.3 copy-done.2
  174.8 14.3 %all-to-all-done.4 = bf16[8,4,64,128]{3,2,1,0:T(8,128)(2,1)S(1)} async-done(((bf16[8,4,64,128]{3,2,1,0:T(8,128)(2,1)}), bf16[8,4,64,128]{3,2,1,0:T(8,128)(2,1)S(1)}, u32[]{:S(2)}, u32[]{:S(2)}) %all-to-all-start.4) | async-done | bytes 524320 | tf_op jit(solution)/shard_map/all_to_all | solution.py:185
  189.1 7.5 %all-to-all-start.3 = ((bf16[32,4,64,128]{3,2,1,0:T(8,128)(2,1)}), bf16[32,4,64,128]{3,2,1,0:T(8,128)(2,1)S(1)}, u32[]{:S(2)}, u32[]{:S(2)}) async-start(bf16[32,4,64,128]{3,2,1,0:T(8,128)(2,1)} %bitcast.20), calls=%async_computation.3 | async-start | bytes 4194304 | tf_op jit(solution)/shard_map/all_to_all | solution.py:188
  196.6 0.8 pick.3
  197.3 1.3 copy-done.1
  198.6 25.8 %all-to-all-done.3 = bf16[32,4,64,128]{3,2,1,0:T(8,128)(2,1)S(1)} async-done(((bf16[32,4,64,128]{3,2,1,0:T(8,128)(2,1)}), bf16[32,4,64,128]{3,2,1,0:T(8,128)(2,1)S(1)}, u32[]{:S(2)}, u32[]{:S(2)}) %all-to-all-start.3) | async-done | bytes 2097184 | tf_op jit(solution)/shard_map/all_to_all | solution.py:188
  224.4 6.7 %all-to-all-start.5 = ((bf16[32,4,64,128]{3,2,1,0:T(8,128)(2,1)}), bf16[32,4,64,128]{3,2,1,0:T(8,128)(2,1)}, u32[]{:S(2)}, u32[]{:S(2)}) async-start(bf16[32,4,64,128]{3,2,1,0:T(8,128)(2,1)} %bitcast.19), calls=%async_computation.5 | async-start | bytes 4194304 | tf_op jit(solution)/shard_map/all_to_all | solution.py:188
  231.8 27.3 %all-to-all-done.5 = bf16[32,4,64,128]{3,2,1,0:T(8,128)(2,1)} async-done(((bf16[32,4,64,128]{3,2,1,0:T(8,128)(2,1)}), bf16[32,4,64,128]{3,2,1,0:T(8,128)(2,1)}, u32[]{:S(2)}, u32[]{:S(2)}) %all-to-all-start.5) | async-done | bytes 2097184 | tf_op jit(solution)/shard_map/all_to_all | solution.py:188
  259.1 13.2 %tiles.1 = f32[128,128,128]{2,1,0:T(8,128)S(1)} custom-call(s32[128]{0:T(128)S(1)} %get-tuple-element.12.left_at, s32[128]{0:T(128)S(1)} %get-tuple-element.11.right_at, s32[1]{0:T(128)S(6)} %copy.30.live_ref, bf16[128,64,128]{2,1,0:T(8,128)(2,1)S(1)} %bitcast.18, bf16[128,64,128]{2,1,0:T(8,128)(2,1)} %bitcast.15.right_ref), custom_call_target="tpu_custom_call" | custom-call | flops 268435456 | bytes 12582912 | tf_op jit(solution)/shard_map/tiles/pallas_call | solution.py:114
  272.3 3.2 copy-done
  275.6 100.5 %reduce-scatter.2.cloned.1.call-done = f32[16,128,128]{2,1,0:T(8,128)} async-done(((f32[128,128,128]{2,1,0:T(8,128)}), f32[16,128,128]{2,1,0:T(8,128)}) %reduce-scatter.2.cloned.1.call-update) | async-done | bytes 1048592 | tf_op jit(solution)/shard_map/reduce_scatter | solution.py:198
  (40 shorter events, 3.0 us)
Async XLA Ops:
  6.5 128.1 %copy-start.10 = (f32[512]{0:T(512)S(1)}, f32[512]{0:T(512)}, u32[]{:S(2)}) copy-start(f32[512]{0:T(512)} %param.16) | copy-start | bytes 6148
  6.5 128.1 %copy-start.9 = (f32[512]{0:T(512)S(1)}, f32[512]{0:T(512)}, u32[]{:S(2)}) copy-start(f32[512]{0:T(512)} %param.14) | copy-start | bytes 6148
  6.5 66.8 %all-gather.3.cloned.1.call-start = ((), (), s32[]{:S(2)}) async-start(), calls=%async_computation.7 | async-start | bytes 1949696 | tf_op jit(solution)/shard_map/all_gather | solution.py:180
  26.9 97.7 %all-gather.5.cloned.1.call-start = ((), (), s32[]{:S(2)}) async-start(), calls=%async_computation.8 | async-start | bytes 1949696 | tf_op jit(solution)/shard_map/all_gather | solution.py:180
  73.4 60.0 %collective-permute-start = (bf16[256,3584]{1,0:T(8,128)(2,1)}, bf16[256,3584]{1,0:T(8,128)(2,1)S(1)}, u32[]{:S(2)}, u32[]{:S(2)}) collective-permute-start(bf16[256,3584]{1,0:T(8,128)(2,1)} %all-gather.3.cloned.1.call-done.own_ref), channel_id=1, source_target_pairs={{0,8},{8,0},{1,9},{9,1},{2,10},{10,2},{3,11},{11,3},{4,12},{12,4},... | collective-permute-start | bytes 5505032 | tf_op jit(solution)/shard_map/ppermute | solution.py:183
  124.6 25.1 %collective-permute-start.1 = (bf16[256,3584]{1,0:T(8,128)(2,1)}, bf16[256,3584]{1,0:T(8,128)(2,1)}, u32[]{:S(2)}, u32[]{:S(2)}) collective-permute-start(bf16[256,3584]{1,0:T(8,128)(2,1)} %all-gather.5.cloned.1.call-done.own_ref), channel_id=1, source_target_pairs={{0,8},{8,0},{1,9},{9,1},{2,10},{10,2},{3,11},{11,3},{4,12},{12,4},... | collective-permute-start | bytes 5505032 | tf_op jit(solution)/shard_map/ppermute | solution.py:183
  128.2 14.7 %all-to-all-start = ((s32[32,1,8]{2,1,0:T(1,128)}), s32[32,1,8]{2,1,0:T(1,128)S(1)}, u32[]{:S(2)}, u32[]{:S(2)}) async-start(s32[32,1,8]{2,1,0:T(1,128)} %bitcast.2), calls=%async_computation | async-start | bytes 32768 | tf_op jit(solution)/shard_map/all_to_all | solution.py:172
  133.4 1.3 copy-start.7
  134.6 2.0 copy-start.3
  136.7 1.5 copy-start.6
  138.2 1.5 copy-start.8
  139.7 10.1 %copy-start.5 = (bf16[256,3584]{1,0:T(8,128)(2,1)S(1)}, bf16[256,3584]{1,0:T(8,128)(2,1)}, u32[]{:S(2)}) copy-start(bf16[256,3584]{1,0:T(8,128)(2,1)} %all-gather.5.cloned.1.call-done.own_ref) | copy-start | bytes 5505028
  139.7 10.1 %copy-start.11 = (f32[512]{0:T(512)S(1)}, f32[512]{0:T(512)}, u32[]{:S(2)}) copy-start(f32[512]{0:T(512)} %param.15) | copy-start | bytes 6148
  139.7 10.1 %copy-start.12 = (f32[512]{0:T(512)S(1)}, f32[512]{0:T(512)}, u32[]{:S(2)}) copy-start(f32[512]{0:T(512)} %param.17) | copy-start | bytes 6148
  143.0 24.7 %all-to-all-start.2 = ((bf16[8,4,64,128]{3,2,1,0:T(8,128)(2,1)}), bf16[8,4,64,128]{3,2,1,0:T(8,128)(2,1)S(1)}, u32[]{:S(2)}, u32[]{:S(2)}) async-start(bf16[8,4,64,128]{3,2,1,0:T(8,128)(2,1)} %encode.2), calls=%async_computation.2 | async-start | bytes 1048576 | tf_op jit(solution)/shard_map/all_to_all | solution.py:185
  149.8 2.0 copy-start.4
  167.7 21.4 %all-to-all-start.4 = ((bf16[8,4,64,128]{3,2,1,0:T(8,128)(2,1)}), bf16[8,4,64,128]{3,2,1,0:T(8,128)(2,1)S(1)}, u32[]{:S(2)}, u32[]{:S(2)}) async-start(bf16[8,4,64,128]{3,2,1,0:T(8,128)(2,1)} %encode.3), calls=%async_computation.4 | async-start | bytes 1048576 | tf_op jit(solution)/shard_map/all_to_all | solution.py:185
  173.4 1.3 copy-start.2
  189.1 35.4 %all-to-all-start.3 = ((bf16[32,4,64,128]{3,2,1,0:T(8,128)(2,1)}), bf16[32,4,64,128]{3,2,1,0:T(8,128)(2,1)S(1)}, u32[]{:S(2)}, u32[]{:S(2)}) async-start(bf16[32,4,64,128]{3,2,1,0:T(8,128)(2,1)} %bitcast.20), calls=%async_computation.3 | async-start | bytes 4194304 | tf_op jit(solution)/shard_map/all_to_all | solution.py:188
  197.3 1.3 copy-start.1
  224.4 34.7 %all-to-all-start.5 = ((bf16[32,4,64,128]{3,2,1,0:T(8,128)(2,1)}), bf16[32,4,64,128]{3,2,1,0:T(8,128)(2,1)}, u32[]{:S(2)}, u32[]{:S(2)}) async-start(bf16[32,4,64,128]{3,2,1,0:T(8,128)(2,1)} %bitcast.19), calls=%async_computation.5 | async-start | bytes 4194304 | tf_op jit(solution)/shard_map/all_to_all | solution.py:188
  231.1 145.0 %reduce-scatter.2.cloned.1.call-start = ((), (), s32[]{:S(2)}) async-start(), calls=%async_computation.9 | async-start | bytes 9437184 | tf_op jit(solution)/shard_map/reduce_scatter | solution.py:198
  272.3 3.2 copy-start
Sparse Core Ops, SparseCore 0:
  27.0 46.2 all-gather.2
  75.8 48.7 all-gather.4
  275.7 100.3 reduce-scatter.1

commit v2 on v1

v2 whole, which is shorter than its diff:
```python
import functools

import jax
import jax.numpy as jnp
from jax import lax
from jax.experimental import pallas as pl
from jax.experimental.pallas import tpu as pltpu
from jax.sharding import Mesh, PartitionSpec as P

BLOCK = 128
FROM_GROUP = 4
GROUPS = 32
RANKS = 8
TOKENS = 512
SIDE = 4
CHIPS = SIDE * SIDE
HALF = 8
REACH = 3
ALL = ("y", "x", "c", "z")
LAT = ("y", "x", "c")
MIB = 1 << 20


def activate(preact, bias, thresh):
    preact = preact + bias
    return (preact * jnp.clip(2.0 * preact / thresh - 1.0, 0.0, 1.0)).astype(jnp.bfloat16)


def encode_kernel(place_ref, own_ref, other_ref, w_ref, bias_ref, thresh_ref, out_ref):
    piece = own_ref.shape[0] // CHIPS
    for side, acts_ref in enumerate((own_ref, other_ref)):
        preact = jnp.dot(acts_ref[...], w_ref[...], preferred_element_type=jnp.float32)
        codes = activate(preact, bias_ref[...], thresh_ref[...])
        for u in range(CHIPS):
            rank = place_ref[2 * u]
            at = pl.multiple_of(place_ref[2 * u + 1] ^ (side * piece), piece)
            for j in range(out_ref.shape[1]):
                out_ref[rank, j, pl.ds(at, piece), :] = codes[
                    u * piece : (u + 1) * piece, j * BLOCK : (j + 1) * BLOCK
                ]


def encode_pieces(place, own, other, weight, bias_vec, thresh):
    half, depth = own.shape
    width = weight.shape[1]
    step = 256
    return pl.pallas_call(
        encode_kernel,
        grid_spec=pltpu.PrefetchScalarGridSpec(
            num_scalar_prefetch=1,
            grid=(width // step,),
            in_specs=[
                pl.BlockSpec((half, depth), lambda i, s: (0, 0)),
                pl.BlockSpec((half, depth), lambda i, s: (0, 0)),
                pl.BlockSpec((depth, step), lambda i, s: (0, i)),
                pl.BlockSpec((1, step), lambda i, s: (0, i)),
                pl.BlockSpec((1, step), lambda i, s: (0, i)),
            ],
            out_specs=pl.BlockSpec(
                (RANKS, step // BLOCK, 2 * half // RANKS, BLOCK), lambda i, s: (0, i, 0, 0)
            ),
        ),
        out_shape=jax.ShapeDtypeStruct(
            (RANKS, width // BLOCK, 2 * half // RANKS, BLOCK), jnp.bfloat16
        ),
        compiler_params=pltpu.CompilerParams(vmem_limit_bytes=24 * MIB),
        cost_estimate=pl.CostEstimate(
            flops=4 * half * depth * width, bytes_accessed=8 * MIB, transcendentals=0
        ),
        name="encode_pieces",
    )(place, own, other, weight, bias_vec[None], thresh[None])


def encode_rows_kernel(acts_ref, w_ref, bias_ref, thresh_ref, out_ref):
    rows = out_ref.shape[2]
    preact = jnp.dot(acts_ref[...], w_ref[...], preferred_element_type=jnp.float32)
    codes = activate(preact, bias_ref[...], thresh_ref[...])
    for t in range(RANKS):
        for j in range(out_ref.shape[1]):
            out_ref[t, j] = codes[t * rows : (t + 1) * rows, j * BLOCK : (j + 1) * BLOCK]


def encode_rows(acts, weight, bias_vec, thresh):
    tokens, depth = acts.shape
    width = weight.shape[1]
    step = 256
    return pl.pallas_call(
        encode_rows_kernel,
        grid=(width // step,),
        in_specs=[
            pl.BlockSpec((tokens, depth), lambda i: (0, 0)),
            pl.BlockSpec((depth, step), lambda i: (0, i)),
            pl.BlockSpec((1, step), lambda i: (0, i)),
            pl.BlockSpec((1, step), lambda i: (0, i)),
        ],
        out_specs=pl.BlockSpec((RANKS, step // BLOCK, tokens // RANKS, BLOCK), lambda i: (0, i, 0, 0)),
        out_shape=jax.ShapeDtypeStruct((RANKS, width // BLOCK, tokens // RANKS, BLOCK), jnp.bfloat16),
        compiler_params=pltpu.CompilerParams(vmem_limit_bytes=24 * MIB),
        cost_estimate=pl.CostEstimate(
            flops=2 * tokens * depth * width, bytes_accessed=8 * MIB, transcendentals=0
        ),
        name="encode_rows",
    )(acts, weight, bias_vec[None], thresh[None])


def pick_kernel(index_ref, blocks_ref, out_ref):
    def body(i, carry):
        out_ref[i] = blocks_ref[index_ref[i]]
        return carry

    lax.fori_loop(0, out_ref.shape[0], body, 0, unroll=8)


def pick(index, blocks):
    count = index.shape[0]
    return pl.pallas_call(
        pick_kernel,
        in_specs=[
            pl.BlockSpec(memory_space=pltpu.SMEM),
            pl.BlockSpec(memory_space=pltpu.VMEM),
        ],
        out_specs=pl.BlockSpec(memory_space=pltpu.VMEM),
        out_shape=jax.ShapeDtypeStruct((count,) + blocks.shape[1:], blocks.dtype),
        compiler_params=pltpu.CompilerParams(vmem_limit_bytes=16 * MIB),
        cost_estimate=pl.CostEstimate(flops=0, bytes_accessed=3 * MIB, transcendentals=0),
        name="pick",
    )(index, blocks)


def route_kernel(slot_ref, at_ref, blocks_ref, *outs):
    for side in range(2):
        for k in range(REACH + 1):
            out_ref = outs[side * (REACH + 1) + k]
            for part in range(2):
                first = slot_ref[(side * (REACH + 1) + k) * 2 + part]
                for i in range(HALF):
                    out_ref[part * HALF + i] = blocks_ref[at_ref[first + i]]


def route(slot, at, blocks):
    one = jax.ShapeDtypeStruct((2 * HALF,) + blocks.shape[1:], blocks.dtype)
    count = 2 * (REACH + 1)
    return pl.pallas_call(
        route_kernel,
        in_specs=[
            pl.BlockSpec(memory_space=pltpu.SMEM),
            pl.BlockSpec(memory_space=pltpu.SMEM),
            pl.BlockSpec(memory_space=pltpu.VMEM),
        ],
        out_specs=[pl.BlockSpec(memory_space=pltpu.VMEM)] * count,
        out_shape=[one] * count,
        compiler_params=pltpu.CompilerParams(vmem_limit_bytes=16 * MIB),
        cost_estimate=pl.CostEstimate(flops=0, bytes_accessed=4 * MIB, transcendentals=0),
        name="route",
    )(slot, at, blocks)


def gram_sum(lefts, rights, i):
    total = None
    for left_ref, right_ref in zip(lefts, rights):
        gram = lax.dot_general(
            left_ref[i], right_ref[i], (((0,), (0,)), ((), ())), preferred_element_type=jnp.float32
        )
        total = gram if total is None else total + gram
    return total


def half_tiles_kernel(first, *refs):
    out_refs = refs[-2:]
    refs = refs[:-2]
    count = REACH + 1
    for side in range(2):
        lefts = refs[side * count : (side + 1) * count]
        rights = refs[(2 + side) * count : (3 + side) * count]
        for i in range(HALF):
            out_refs[side][i] = gram_sum(lefts, rights, first + i)


def half_tiles(first, lefts, rights):
    one = jax.ShapeDtypeStruct((HALF, BLOCK, BLOCK), jnp.float32)
    count = 4 * (REACH + 1)
    return pl.pallas_call(
        functools.partial(half_tiles_kernel, first),
        in_specs=[pl.BlockSpec(memory_space=pltpu.VMEM)] * count,
        out_specs=[pl.BlockSpec(memory_space=pltpu.VMEM)] * 2,
        out_shape=[one] * 2,
        compiler_params=pltpu.CompilerParams(vmem_limit_bytes=16 * MIB),
        cost_estimate=pl.CostEstimate(
            flops=2 * 16 * 256 * BLOCK * BLOCK, bytes_accessed=3 * MIB, transcendentals=0
        ),
        name="half_tiles",
    )(*lefts, *rights)


def finish_kernel(first_ref, live_ref, low_ref, low_far_ref, high_ref, high_far_ref, out_ref):
    for i in range(2 * HALF):
        near_ref, far_ref = (low_ref, low_far_ref) if i < HALF else (high_ref, high_far_ref)
        total = (near_ref[i % HALF] + far_ref[i % HALF]) * (1.0 / TOKENS)
        out_ref[i] = jnp.where(first_ref[0] + i < live_ref[0], total, 0.0)


def finish(first, live, low, low_far, high, high_far):
    return pl.pallas_call(
        finish_kernel,
        in_specs=[pl.BlockSpec(memory_space=pltpu.SMEM)] * 2
        + [pl.BlockSpec(memory_space=pltpu.VMEM)] * 4,
        out_specs=pl.BlockSpec(memory_space=pltpu.VMEM),
        out_shape=jax.ShapeDtypeStruct((2 * HALF, BLOCK, BLOCK), jnp.float32),
        compiler_params=pltpu.CompilerParams(vmem_limit_bytes=16 * MIB),
        cost_estimate=pl.CostEstimate(flops=MIB, bytes_accessed=3 * MIB, transcendentals=0),
        name="finish",
    )(first, live, low, low_far, high, high_far)


def positions(pair_blocks, group_blocks):
    source = pair_blocks // group_blocks
    within = pair_blocks % group_blocks
    slots = pair_blocks.shape[0]
    order = jnp.arange(slots)
    same = source[:, None, :] == source[None, :, :]
    before = (order[None, :] < order[:, None])[:, :, None]
    rank = jnp.sum(same & before, axis=1, dtype=jnp.int32)
    position = source * FROM_GROUP + rank
    hit = position[None, :, :] == order[:, None, None]
    table = jnp.sum(jnp.where(hit, within[None, :, :], 0), axis=1, dtype=jnp.int32)
    return position, table


def shift(value, axis, size, by):
    return lax.ppermute(value, axis, [(i, (i + by) % size) for i in range(size)])


def gather_z(acts):
    spread = jnp.broadcast_to(acts[None], (RANKS,) + acts.shape)
    return lax.all_to_all(spread, "z", 0, 0, tiled=True)


def ring_of_four(value, axis):
    return [value] + [shift(value, axis, SIDE, k) for k in range(1, SIDE)]


def gather_chips(rows):
    width = rows.shape[1] // 2
    left, right = rows[:, :width], rows[:, width:]
    left_x = jnp.stack(ring_of_four(left, "x"))
    right_y = jnp.stack(ring_of_four(right, "y"))
    left_all = jnp.stack(ring_of_four(left_x, "y"))
    right_all = jnp.stack(ring_of_four(right_y, "x"), axis=1)
    return jnp.concatenate([left_all, right_all], axis=3).reshape(-1, rows.shape[1])


def shards(
    acts_early,
    acts_late,
    enc_early,
    enc_late,
    bias_early,
    bias_late,
    thresh_early,
    thresh_late,
    pair_blocks,
    live_pairs,
):
    y, x, c, z = (lax.axis_index(name).astype(jnp.int32) for name in ALL)
    depth = acts_early.shape[1]
    group_blocks = RANKS * enc_early.shape[1] // BLOCK

    near = gather_z(jnp.stack([acts_early, acts_late]))
    rows_early = near[:, 0].reshape(-1, depth)
    rows_late = near[:, 1].reshape(-1, depth)
    all_late = lax.all_gather(rows_late, LAT, axis=0, tiled=True)

    position, table = positions(pair_blocks, group_blocks)
    asked = lax.all_to_all(
        table.reshape(GROUPS, FROM_GROUP * 2), LAT, split_axis=0, concat_axis=0, tiled=True
    ).reshape(GROUPS * FROM_GROUP, 2)

    own = gather_chips(rows_early)
    other = shift(own, "c", 2, 1)
    step = jnp.arange(SIDE, dtype=jnp.int32)
    chip = ((y - step) % SIDE)[:, None] * SIDE + ((x - step) % SIDE)[None, :]
    chip = chip.reshape(-1)
    place = jnp.stack([chip // 2, (chip % 2) * 32 + c * 16], axis=1).reshape(-1)

    def spread(codes, layer):
        codes = lax.all_to_all(codes, "z", split_axis=0, concat_axis=0, tiled=True)
        sent = pick(asked[:, layer], codes.reshape((group_blocks,) + codes.shape[2:]))
        got = lax.all_to_all(
            sent.reshape((GROUPS, FROM_GROUP) + sent.shape[1:]),
            LAT,
            split_axis=0,
            concat_axis=0,
            tiled=True,
        )
        return got.reshape(sent.shape)

    slots = []
    for side in range(2):
        for k in range(REACH + 1):
            by = k if side == 0 else -k
            past = by + (1 if side == 0 else -1)
            for part, (plane, half) in enumerate(((past, side), (by, 1 - side))):
                slots.append(((z + plane) % RANKS) * (2 * HALF) + half * HALF)
    slots = jnp.stack(slots)

    def trade(blocks, layer):
        parts = route(slots, position[:, layer], blocks)
        out = list(parts)
        for k in range(REACH, 0, -1):
            for side in range(2):
                at = side * (REACH + 1) + k
                out[at] = shift(parts[at], "z", RANKS, k if side == 0 else -k)
        return out

    codes_early = encode_pieces(place, own, other, enc_early, bias_early, thresh_early)
    lefts = trade(spread(codes_early, 0), 0)
    codes_late = encode_rows(all_late, enc_late, bias_late, thresh_late)
    rights = trade(spread(codes_late, 1), 1)

    up, down = half_tiles(0, lefts, rights)
    low_far = shift(up, "z", RANKS, 1)
    high_far = shift(down, "z", RANKS, -1)
    high, low = half_tiles(HALF, lefts, rights)
    return finish((z * (2 * HALF))[None], live_pairs, low, low_far, high, high_far)


def solution(mesh):
    fine = Mesh(mesh.devices.reshape(SIDE, SIDE, 2, RANKS), ALL)
    in_specs = (
        P(ALL, None),
        P(ALL, None),
        P(None, ALL),
        P(None, ALL),
        P(ALL),
        P(ALL),
        P(ALL),
        P(ALL),
        P(LAT, None),
        P(LAT),
    )
    out_specs = P(ALL, None, None)
    return jax.shard_map(shards, mesh=fine, in_specs=in_specs, out_specs=out_specs, check_vma=False)
```

time: 384 us -> 268 us (0.70)
  waiting for transfers between devices: 274 us -> 122 us
  starting transfers between devices: 33.2 us -> 70.7 us
    reduce_scatter x1 -> x0, waiting for transfers between devices: 101 us -> none  [shards(): return lax.psum_scatter(sums, 'z', scatter_dimension=0, tiled=True)]
    all_gather x2 -> x1, waiting for transfers between devices: 95.1 us -> 2.45 us  [shards(): all_late = lax.all_gather(rows_late, LAT, axis=0, tiled=True)]
    ppermute x2 -> x27, waiting for transfers between devices: 0.01 us -> 54.4 us  [shift(): lax.ppermute(value, axis, [(i, (i + by) % size) for i in range(size)])]
    ppermute x2 -> x27, starting transfers between devices: 3.61 us -> 46.2 us  [shift(): lax.ppermute(value, axis, [(i, (i + by) % size) for i in range(size)])]
    all_to_all x4, waiting for transfers between devices: 78.5 us -> 65.6 us  [the longest x2 44.7 us: spread(): lax.all_to_all(sent.reshape((GROUPS, FROM_GROUP) + sent.shape[1:]), LAT,...]
    pallas_call x3 -> x7, Pallas kernels: 21.2 us -> 17.7 us  [the longest x1 5.35 us: encode_pieces(): pl.pallas_call(encode_kernel, grid_spec=pltpu.PrefetchScalarGridSpec(num_...]
    unnamed x26 -> x34, local copies, waits for them, and re-layouts: 14.2 us -> 15.1 us
  transfers between devices with their start and end apart: 10 -> 33, of which waited for: 7 -> 15; matrix products, arithmetic and copies ran while one was open for 1% -> 1% of each run, Pallas kernels for 2% -> 5%
where the time goes in v2:
time: 268 us; the launch traced here: 266 us
  waiting for transfers between devices  122 us (46%)
  starting transfers between devices  70.7 us (26%)
  Pallas kernels  19.2 us (7%)
  blocking collectives  18.6 us (7%)
  local copies, waits for them, and re-layouts  18 us (7%)
  between operations  14.5 us (5%)
    ppermute x27, waiting for transfers between devices, shift(): lax.ppermute(value, axis, [(i, (i + by) % size) for i in range(size)])  54.4 us
    ppermute x27, starting transfers between devices, shift(): lax.ppermute(value, axis, [(i, (i + by) % size) for i in range(size)])  46.2 us
    all_to_all x2, waiting for transfers between devices, spread(): lax.all_to_all(sent.reshape((GROUPS, FROM_GROUP) + sent.shape[1:]), LAT,...  44.7 us
    all_to_all x2, waiting for transfers between devices, spread(): codes = lax.all_to_all(codes, 'z', split_axis=0, concat_axis=0, tiled=True)  20.9 us
    all_to_all x1, blocking collectives, gather_z(): return lax.all_to_all(spread, 'z', 0, 0, tiled=True)  18.6 us
    unnamed x34, local copies, waits for them, and re-layouts  15.1 us
    all_to_all x2, starting transfers between devices, spread(): lax.all_to_all(sent.reshape((GROUPS, FROM_GROUP) + sent.shape[1:]), LAT,...  13.7 us
    all_to_all x2, starting transfers between devices, spread(): codes = lax.all_to_all(codes, 'z', split_axis=0, concat_axis=0, tiled=True)  7.17 us
  transfers between devices with their start and end apart: 33, of which 15 were waited for; matrix products, arithmetic and copies ran while one was open for 1% of the time, Pallas kernels for 5%

profile of v2, /device:TPU:1, one launch (start us, length us, event | category | flops | bytes accessed | tf_op | source)
XLA Modules:
  0.0 265.6 jit_solution(6772984002298917012)
XLA Ops:
  7.5 18.6 %all_to_all.34 = bf16[8,2,2,3584]{3,2,1,0:T(2,128)(2,1)S(1)} all-to-all(bf16[8,2,2,3584]{3,2,1,0:T(2,128)(2,1)S(1)} %broadcast_in_dim.46), channel_id=1, replica_groups=mesh['y'=4,'x'=4,'c'=2,'z'=8] {'z'}, dimensions={0} | all-to-all | bytes 458752 | tf_op jit(solution)/shard_map/all_to_all | solution.py:235
  28.3 2.5 collective-permute-start.1
  33.2 2.6 collective-permute-start.7
  40.4 2.2 collective-permute-start.10
  42.6 2.7 %collective-permute-done.3 = bf16[4,16,1792]{2,1,0:T(8,128)(2,1)S(1)} collective-permute-done((bf16[4,16,1792]{2,1,0:T(8,128)(2,1)S(1)}, bf16[4,16,1792]{2,1,0:T(8,128)(2,1)S(1)}, u32[]{:S(2)}, u32[]{:S(2)}) %collective-permute-start.3) | collective-permute-done | bytes 229408 | tf_op jit(solution)/shard_map/ppermute | solution.py:230
  45.3 3.8 %collective-permute-done.4 = bf16[4,16,1792]{2,1,0:T(8,128)(2,1)S(1)} collective-permute-done((bf16[4,16,1792]{2,1,0:T(8,128)(2,1)S(1)}, bf16[4,16,1792]{2,1,0:T(8,128)(2,1)S(1)}, u32[]{:S(2)}, u32[]{:S(2)}) %collective-permute-start.4) | collective-permute-done | bytes 229408 | tf_op jit(solution)/shard_map/ppermute | solution.py:230
  51.8 8.1 %collective-permute-start.12 = (bf16[256,3584]{1,0:T(8,128)(2,1)S(1)}, bf16[256,3584]{1,0:T(8,128)(2,1)}, u32[]{:S(2)}, u32[]{:S(2)}) collective-permute-start(bf16[256,3584]{1,0:T(8,128)(2,1)S(1)} %bitcast.65), channel_id=1, source_target_pairs={{0,8},{8,0},{1,9},{9,1},{2,10},{10,2},{3,11},{11,3},{4,12},{12,4},... | collective-permute-start | bytes 5505032 | tf_op jit(solution)/shard_map/ppermute | solution.py:230
  61.1 3.7 %all-to-all-start = ((s32[32,1,8]{2,1,0:T(1,128)}), s32[32,1,8]{2,1,0:T(1,128)S(1)}, u32[]{:S(2)}, u32[]{:S(2)}) async-start(s32[32,1,8]{2,1,0:T(1,128)} %bitcast.18), calls=%async_computation | async-start | bytes 32768 | tf_op jit(solution)/shard_map/all_to_all | solution.py:274
  67.2 5.3 %encode_pieces.1 = bf16[8,4,64,128]{3,2,1,0:T(8,128)(2,1)} custom-call(s32[32]{0:T(128)S(1)} %reshape.181.place_ref, bf16[256,3584]{1,0:T(8,128)(2,1)S(1)} %bitcast.66, bf16[256,3584]{1,0:T(8,128)(2,1)} %collective-permute-done.12.other_ref, bf16[3584,512]{1,0:T(8,128)(2,1)S(1)} %copy-done.4, f32[1,512]{1,0:T(1,128)S(1)} %bitcast.69, f32[1,512]{1,0:T(1,128)S(1)} %bitcast.70), custom_call_target="tpu_custom_call" | custom-call | flops 1879048192 | bytes 8388608 | tf_op jit(solution)/shard_map/encode_pieces/pallas_call | solution.py:47
  72.6 3.7 %all-to-all-start.2 = ((bf16[8,4,64,128]{3,2,1,0:T(8,128)(2,1)}), bf16[8,4,64,128]{3,2,1,0:T(8,128)(2,1)S(1)}, u32[]{:S(2)}, u32[]{:S(2)}) async-start(bf16[8,4,64,128]{3,2,1,0:T(8,128)(2,1)} %encode_pieces.1), calls=%async_computation.2 | async-start | bytes 1048576 | tf_op jit(solution)/shard_map/all_to_all | solution.py:286
  76.3 2.4 all-gather.2.cloned.1.call-done.acts_ref
  78.7 2.0 copy-done.5
  82.8 3.2 %encode_rows.1 = bf16[8,4,64,128]{3,2,1,0:T(8,128)(2,1)} custom-call(bf16[512,3584]{1,0:T(8,128)(2,1)S(1)} %copy-done.6, bf16[3584,512]{1,0:T(8,128)(2,1)S(1)} %copy-done.5, f32[1,512]{1,0:T(1,128)S(1)} %bitcast.71, f32[1,512]{1,0:T(1,128)S(1)} %bitcast.72), custom_call_target="tpu_custom_call" | custom-call | flops 1879048192 | bytes 8388608 | tf_op jit(solution)/shard_map/encode_rows/pallas_call | solution.py:87
  86.1 6.6 %all-to-all-done.2 = bf16[8,4,64,128]{3,2,1,0:T(8,128)(2,1)S(1)} async-done(((bf16[8,4,64,128]{3,2,1,0:T(8,128)(2,1)}), bf16[8,4,64,128]{3,2,1,0:T(8,128)(2,1)S(1)}, u32[]{:S(2)}, u32[]{:S(2)}) %all-to-all-start.2) | async-done | bytes 524320 | tf_op jit(solution)/shard_map/all_to_all | solution.py:286
  92.7 3.5 %all-to-all-start.4 = ((bf16[8,4,64,128]{3,2,1,0:T(8,128)(2,1)}), bf16[8,4,64,128]{3,2,1,0:T(8,128)(2,1)S(1)}, u32[]{:S(2)}, u32[]{:S(2)}) async-start(bf16[8,4,64,128]{3,2,1,0:T(8,128)(2,1)} %encode_rows.1), calls=%async_computation.4 | async-start | bytes 1048576 | tf_op jit(solution)/shard_map/all_to_all | solution.py:286
  99.8 14.3 %all-to-all-done.4 = bf16[8,4,64,128]{3,2,1,0:T(8,128)(2,1)S(1)} async-done(((bf16[8,4,64,128]{3,2,1,0:T(8,128)(2,1)}), bf16[8,4,64,128]{3,2,1,0:T(8,128)(2,1)S(1)}, u32[]{:S(2)}, u32[]{:S(2)}) %all-to-all-start.4) | async-done | bytes 524320 | tf_op jit(solution)/shard_map/all_to_all | solution.py:286
  114.1 7.7 %all-to-all-start.3 = ((bf16[32,4,64,128]{3,2,1,0:T(8,128)(2,1)}), bf16[32,4,64,128]{3,2,1,0:T(8,128)(2,1)S(1)}, u32[]{:S(2)}, u32[]{:S(2)}) async-start(bf16[32,4,64,128]{3,2,1,0:T(8,128)(2,1)} %bitcast.64), calls=%async_computation.3 | async-start | bytes 4194304 | tf_op jit(solution)/shard_map/all_to_all | solution.py:288
  123.8 25.7 %all-to-all-done.3 = bf16[32,4,64,128]{3,2,1,0:T(8,128)(2,1)S(1)} async-done(((bf16[32,4,64,128]{3,2,1,0:T(8,128)(2,1)}), bf16[32,4,64,128]{3,2,1,0:T(8,128)(2,1)S(1)}, u32[]{:S(2)}, u32[]{:S(2)}) %all-to-all-start.3) | async-done | bytes 2097184 | tf_op jit(solution)/shard_map/all_to_all | solution.py:288
  150.9 6.0 %all-to-all-start.5 = ((bf16[32,4,64,128]{3,2,1,0:T(8,128)(2,1)}), bf16[32,4,64,128]{3,2,1,0:T(8,128)(2,1)S(1)}, u32[]{:S(2)}, u32[]{:S(2)}) async-start(bf16[32,4,64,128]{3,2,1,0:T(8,128)(2,1)} %bitcast.62), calls=%async_computation.5 | async-start | bytes 4194304 | tf_op jit(solution)/shard_map/all_to_all | solution.py:288
  161.5 2.2 collective-permute-start.15
  166.3 19.0 %all-to-all-done.5 = bf16[32,4,64,128]{3,2,1,0:T(8,128)(2,1)S(1)} async-done(((bf16[32,4,64,128]{3,2,1,0:T(8,128)(2,1)}), bf16[32,4,64,128]{3,2,1,0:T(8,128)(2,1)S(1)}, u32[]{:S(2)}, u32[]{:S(2)}) %all-to-all-start.5) | async-done | bytes 2097184 | tf_op jit(solution)/shard_map/all_to_all | solution.py:288
  187.5 7.6 %collective-permute-done.15.refs_3_ = bf16[16,64,128]{2,1,0:T(8,128)(2,1)S(1)} collective-permute-done((bf16[16,64,128]{2,1,0:T(8,128)(2,1)}, bf16[16,64,128]{2,1,0:T(8,128)(2,1)S(1)}, u32[]{:S(2)}, u32[]{:S(2)}) %collective-permute-start.15) | collective-permute-done | bytes 262176 | tf_op jit(solution)/shard_map/ppermute | solution.py:230
  195.1 5.3 %collective-permute-start.20 = (bf16[16,64,128]{2,1,0:T(8,128)(2,1)S(1)}, bf16[16,64,128]{2,1,0:T(8,128)(2,1)S(1)}, u32[]{:S(2)}, u32[]{:S(2)}) collective-permute-start(bf16[16,64,128]{2,1,0:T(8,128)(2,1)S(1)} %get-tuple-element.35), channel_id=1, source_target_pairs={{0,2},{1,3},{2,4},{3,5},{4,6},{5,7},{6,0},{7,1},{8,10},{9,11},{10,... | collective-permute-start | bytes 786440 | tf_op jit(solution)/shard_map/ppermute | solution.py:230
  200.3 2.4 collective-permute-start.22
  202.7 4.2 %collective-permute-start.23 = (bf16[16,64,128]{2,1,0:T(8,128)(2,1)S(1)}, bf16[16,64,128]{2,1,0:T(8,128)(2,1)S(1)}, u32[]{:S(2)}, u32[]{:S(2)}) collective-permute-start(bf16[16,64,128]{2,1,0:T(8,128)(2,1)S(1)} %get-tuple-element.39), channel_id=1, source_target_pairs={{0,6},{1,7},{2,0},{3,1},{4,2},{5,3},{6,4},{7,5},{8,14},{9,15},{10,... | collective-permute-start | bytes 786440 | tf_op jit(solution)/shard_map/ppermute | solution.py:230
  207.0 2.7 collective-permute-done.19.refs_9_
  209.9 18.8 %collective-permute-done.21.refs_11_ = bf16[16,64,128]{2,1,0:T(8,128)(2,1)S(1)} collective-permute-done((bf16[16,64,128]{2,1,0:T(8,128)(2,1)S(1)}, bf16[16,64,128]{2,1,0:T(8,128)(2,1)S(1)}, u32[]{:S(2)}, u32[]{:S(2)}) %collective-permute-start.21) | collective-permute-done | bytes 262176 | tf_op jit(solution)/shard_map/ppermute | solution.py:230
  228.8 8.7 %collective-permute-done.24.refs_15_ = bf16[16,64,128]{2,1,0:T(8,128)(2,1)S(1)} collective-permute-done((bf16[16,64,128]{2,1,0:T(8,128)(2,1)S(1)}, bf16[16,64,128]{2,1,0:T(8,128)(2,1)S(1)}, u32[]{:S(2)}, u32[]{:S(2)}) %collective-permute-start.24) | collective-permute-done | bytes 262176 | tf_op jit(solution)/shard_map/ppermute | solution.py:230
  237.5 2.6 half_tiles.3
  240.8 3.8 %collective-permute-start.25 = (f32[8,128,128]{2,1,0:T(8,128)}, f32[8,128,128]{2,1,0:T(8,128)}, u32[]{:S(2)}, u32[]{:S(2)}) collective-permute-start(f32[8,128,128]{2,1,0:T(8,128)} %get-tuple-element.42), channel_id=1, source_target_pairs={{0,1},{1,2},{2,3},{3,4},{4,5},{5,6},{6,7},{7,0},{8,9},{9,10},{10,1... | collective-permute-start | bytes 1572872 | tf_op jit(solution)/shard_map/ppermute | solution.py:230
  249.0 5.7 %collective-permute-done.25.low_far_ref = f32[8,128,128]{2,1,0:T(8,128)} collective-permute-done((f32[8,128,128]{2,1,0:T(8,128)}, f32[8,128,128]{2,1,0:T(8,128)}, u32[]{:S(2)}, u32[]{:S(2)}) %collective-permute-start.25) | collective-permute-done | bytes 524320 | tf_op jit(solution)/shard_map/ppermute | solution.py:230
  256.5 2.3 finish.1
  (108 shorter events, 41.1 us)
Async XLA Ops:
  6.5 72.2 %all-gather.2.cloned.1.call-start = ((), (), s32[]{:S(2)}) async-start(), calls=%async_computation.6 | async-start | bytes 3784704 | tf_op jit(solution)/shard_map/all_gather | solution.py:271
  27.0 8.8 %collective-permute-start = (bf16[16,1792]{1,0:T(8,128)(2,1)S(1)}, bf16[16,1792]{1,0:T(8,128)(2,1)S(1)}, u32[]{:S(2)}, u32[]{:S(2)}) collective-permute-start(bf16[16,1792]{1,0:T(8,128)(2,1)S(1)} %get-tuple-element.56), channel_id=1, source_target_pairs={{0,16},{16,32},{32,48},{48,0},{1,17},{17,33},{33,49},{49,1},{2,18}... | collective-permute-start | bytes 172040 | tf_op jit(solution)/shard_map/ppermute | solution.py:230
  28.3 8.6 %collective-permute-start.1 = (bf16[16,1792]{1,0:T(8,128)(2,1)S(1)}, bf16[16,1792]{1,0:T(8,128)(2,1)S(1)}, u32[]{:S(2)}, u32[]{:S(2)}) collective-permute-start(bf16[16,1792]{1,0:T(8,128)(2,1)S(1)} %get-tuple-element.56), channel_id=1, source_target_pairs={{0,32},{16,48},{32,0},{48,16},{1,33},{17,49},{33,1},{49,17},{2,34}... | collective-permute-start | bytes 172040 | tf_op jit(solution)/shard_map/ppermute | solution.py:230
  30.7 6.2 %collective-permute-start.2 = (bf16[16,1792]{1,0:T(8,128)(2,1)S(1)}, bf16[16,1792]{1,0:T(8,128)(2,1)S(1)}, u32[]{:S(2)}, u32[]{:S(2)}) collective-permute-start(bf16[16,1792]{1,0:T(8,128)(2,1)S(1)} %get-tuple-element.56), channel_id=1, source_target_pairs={{0,48},{16,0},{32,16},{48,32},{1,49},{17,1},{33,17},{49,33},{2,50}... | collective-permute-start | bytes 172040 | tf_op jit(solution)/shard_map/ppermute | solution.py:230
  31.9 6.3 %collective-permute-start.6 = (bf16[16,1792]{1,0:T(8,128)(2,1)S(1)}, bf16[16,1792]{1,0:T(8,128)(2,1)S(1)}, u32[]{:S(2)}, u32[]{:S(2)}) collective-permute-start(bf16[16,1792]{1,0:T(8,128)(2,1)S(1)} %get-tuple-element.55), channel_id=1, source_target_pairs={{0,64},{64,128},{128,192},{192,0},{1,65},{65,129},{129,193},{193,1... | collective-permute-start | bytes 172040 | tf_op jit(solution)/shard_map/ppermute | solution.py:230
  33.2 6.7 %collective-permute-start.7 = (bf16[16,1792]{1,0:T(8,128)(2,1)S(1)}, bf16[16,1792]{1,0:T(8,128)(2,1)S(1)}, u32[]{:S(2)}, u32[]{:S(2)}) collective-permute-start(bf16[16,1792]{1,0:T(8,128)(2,1)S(1)} %get-tuple-element.55), channel_id=1, source_target_pairs={{0,128},{64,192},{128,0},{192,64},{1,129},{65,193},{129,1},{193,65... | collective-permute-start | bytes 172040 | tf_op jit(solution)/shard_map/ppermute | solution.py:230
  36.9 8.3 %collective-permute-start.3 = (bf16[4,16,1792]{2,1,0:T(8,128)(2,1)S(1)}, bf16[4,16,1792]{2,1,0:T(8,128)(2,1)S(1)}, u32[]{:S(2)}, u32[]{:S(2)}) collective-permute-start(bf16[4,16,1792]{2,1,0:T(8,128)(2,1)S(1)} %get-tuple-element.50), channel_id=1, source_target_pairs={{0,64},{64,128},{128,192},{192,0},{1,65},{65,129},{129,193},{193,1... | collective-permute-start | bytes 688136 | tf_op jit(solution)/shard_map/ppermute | solution.py:230
  37.4 11.6 %collective-permute-start.4 = (bf16[4,16,1792]{2,1,0:T(8,128)(2,1)S(1)}, bf16[4,16,1792]{2,1,0:T(8,128)(2,1)S(1)}, u32[]{:S(2)}, u32[]{:S(2)}) collective-permute-start(bf16[4,16,1792]{2,1,0:T(8,128)(2,1)S(1)} %get-tuple-element.50), channel_id=1, source_target_pairs={{0,128},{64,192},{128,0},{192,64},{1,129},{65,193},{129,1},{193,65... | collective-permute-start | bytes 688136 | tf_op jit(solution)/shard_map/ppermute | solution.py:230
  38.2 12.8 %collective-permute-start.5 = (bf16[4,16,1792]{2,1,0:T(8,128)(2,1)S(1)}, bf16[4,16,1792]{2,1,0:T(8,128)(2,1)S(1)}, u32[]{:S(2)}, u32[]{:S(2)}) collective-permute-start(bf16[4,16,1792]{2,1,0:T(8,128)(2,1)S(1)} %get-tuple-element.50), channel_id=1, source_target_pairs={{0,192},{64,0},{128,64},{192,128},{1,193},{65,1},{129,65},{193,129... | collective-permute-start | bytes 688136 | tf_op jit(solution)/shard_map/ppermute | solution.py:230
  40.0 11.1 %collective-permute-start.9 = (bf16[4,16,1792]{2,1,0:T(8,128)(2,1)S(1)}, bf16[4,16,1792]{2,1,0:T(8,128)(2,1)S(1)}, u32[]{:S(2)}, u32[]{:S(2)}) collective-permute-start(bf16[4,16,1792]{2,1,0:T(8,128)(2,1)S(1)} %get-tuple-element.52), channel_id=1, source_target_pairs={{0,16},{16,32},{32,48},{48,0},{1,17},{17,33},{33,49},{49,1},{2,18}... | collective-permute-start | bytes 688136 | tf_op jit(solution)/shard_map/ppermute | solution.py:230
  40.4 10.7 %collective-permute-start.10 = (bf16[4,16,1792]{2,1,0:T(8,128)(2,1)S(1)}, bf16[4,16,1792]{2,1,0:T(8,128)(2,1)S(1)}, u32[]{:S(2)}, u32[]{:S(2)}) collective-permute-start(bf16[4,16,1792]{2,1,0:T(8,128)(2,1)S(1)} %get-tuple-element.52), channel_id=1, source_target_pairs={{0,32},{16,48},{32,0},{48,16},{1,33},{17,49},{33,1},{49,17},{2,34}... | collective-permute-start | bytes 688136 | tf_op jit(solution)/shard_map/ppermute | solution.py:230
  45.3 6.3 %collective-permute-start.11 = (bf16[4,16,1792]{2,1,0:T(8,128)(2,1)S(1)}, bf16[4,16,1792]{2,1,0:T(8,128)(2,1)S(1)}, u32[]{:S(2)}, u32[]{:S(2)}) collective-permute-start(bf16[4,16,1792]{2,1,0:T(8,128)(2,1)S(1)} %get-tuple-element.52), channel_id=1, source_target_pairs={{0,48},{16,0},{32,16},{48,32},{1,49},{17,1},{33,17},{49,33},{2,50}... | collective-permute-start | bytes 688136 | tf_op jit(solution)/shard_map/ppermute | solution.py:230
  51.8 13.4 %collective-permute-start.12 = (bf16[256,3584]{1,0:T(8,128)(2,1)S(1)}, bf16[256,3584]{1,0:T(8,128)(2,1)}, u32[]{:S(2)}, u32[]{:S(2)}) collective-permute-start(bf16[256,3584]{1,0:T(8,128)(2,1)S(1)} %bitcast.65), channel_id=1, source_target_pairs={{0,8},{8,0},{1,9},{9,1},{2,10},{10,2},{3,11},{11,3},{4,12},{12,4},... | collective-permute-start | bytes 5505032 | tf_op jit(solution)/shard_map/ppermute | solution.py:230
  61.1 11.5 %all-to-all-start = ((s32[32,1,8]{2,1,0:T(1,128)}), s32[32,1,8]{2,1,0:T(1,128)S(1)}, u32[]{:S(2)}, u32[]{:S(2)}) async-start(s32[32,1,8]{2,1,0:T(1,128)} %bitcast.18), calls=%async_computation | async-start | bytes 32768 | tf_op jit(solution)/shard_map/all_to_all | solution.py:274
  72.6 20.1 %all-to-all-start.2 = ((bf16[8,4,64,128]{3,2,1,0:T(8,128)(2,1)}), bf16[8,4,64,128]{3,2,1,0:T(8,128)(2,1)S(1)}, u32[]{:S(2)}, u32[]{:S(2)}) async-start(bf16[8,4,64,128]{3,2,1,0:T(8,128)(2,1)} %encode_pieces.1), calls=%async_computation.2 | async-start | bytes 1048576 | tf_op jit(solution)/shard_map/all_to_all | solution.py:286
  92.7 21.4 %all-to-all-start.4 = ((bf16[8,4,64,128]{3,2,1,0:T(8,128)(2,1)}), bf16[8,4,64,128]{3,2,1,0:T(8,128)(2,1)S(1)}, u32[]{:S(2)}, u32[]{:S(2)}) async-start(bf16[8,4,64,128]{3,2,1,0:T(8,128)(2,1)} %encode_rows.1), calls=%async_computation.4 | async-start | bytes 1048576 | tf_op jit(solution)/shard_map/all_to_all | solution.py:286
  114.1 35.5 %all-to-all-start.3 = ((bf16[32,4,64,128]{3,2,1,0:T(8,128)(2,1)}), bf16[32,4,64,128]{3,2,1,0:T(8,128)(2,1)S(1)}, u32[]{:S(2)}, u32[]{:S(2)}) async-start(bf16[32,4,64,128]{3,2,1,0:T(8,128)(2,1)} %bitcast.64), calls=%async_computation.3 | async-start | bytes 4194304 | tf_op jit(solution)/shard_map/all_to_all | solution.py:288
  150.9 34.3 %all-to-all-start.5 = ((bf16[32,4,64,128]{3,2,1,0:T(8,128)(2,1)}), bf16[32,4,64,128]{3,2,1,0:T(8,128)(2,1)S(1)}, u32[]{:S(2)}, u32[]{:S(2)}) async-start(bf16[32,4,64,128]{3,2,1,0:T(8,128)(2,1)} %bitcast.62), calls=%async_computation.5 | async-start | bytes 4194304 | tf_op jit(solution)/shard_map/all_to_all | solution.py:288
  161.2 24.7 %collective-permute-start.13 = (bf16[16,64,128]{2,1,0:T(8,128)(2,1)}, bf16[16,64,128]{2,1,0:T(8,128)(2,1)S(1)}, u32[]{:S(2)}, u32[]{:S(2)}) collective-permute-start(bf16[16,64,128]{2,1,0:T(8,128)(2,1)} %get-tuple-element.26), channel_id=1, source_target_pairs={{0,1},{1,2},{2,3},{3,4},{4,5},{5,6},{6,7},{7,0},{8,9},{9,10},{10,1... | collective-permute-start | bytes 786440 | tf_op jit(solution)/shard_map/ppermute | solution.py:230
  161.5 24.8 %collective-permute-start.14 = (bf16[16,64,128]{2,1,0:T(8,128)(2,1)}, bf16[16,64,128]{2,1,0:T(8,128)(2,1)S(1)}, u32[]{:S(2)}, u32[]{:S(2)}) collective-permute-start(bf16[16,64,128]{2,1,0:T(8,128)(2,1)} %get-tuple-element.27), channel_id=1, source_target_pairs={{0,2},{1,3},{2,4},{3,5},{4,6},{5,7},{6,0},{7,1},{8,10},{9,11},{10,... | collective-permute-start | bytes 786440 | tf_op jit(solution)/shard_map/ppermute | solution.py:230
  161.5 33.6 %collective-permute-start.15 = (bf16[16,64,128]{2,1,0:T(8,128)(2,1)}, bf16[16,64,128]{2,1,0:T(8,128)(2,1)S(1)}, u32[]{:S(2)}, u32[]{:S(2)}) collective-permute-start(bf16[16,64,128]{2,1,0:T(8,128)(2,1)} %get-tuple-element.28), channel_id=1, source_target_pairs={{0,3},{1,4},{2,5},{3,6},{4,7},{5,0},{6,1},{7,2},{8,11},{9,12},{10,... | collective-permute-start | bytes 786440 | tf_op jit(solution)/shard_map/ppermute | solution.py:230
  163.7 36.6 %collective-permute-start.16 = (bf16[16,64,128]{2,1,0:T(8,128)(2,1)}, bf16[16,64,128]{2,1,0:T(8,128)(2,1)}, u32[]{:S(2)}, u32[]{:S(2)}) collective-permute-start(bf16[16,64,128]{2,1,0:T(8,128)(2,1)} %get-tuple-element.30), channel_id=1, source_target_pairs={{0,7},{1,0},{2,1},{3,2},{4,3},{5,4},{6,5},{7,6},{8,15},{9,8},{10,9... | collective-permute-start | bytes 786440 | tf_op jit(solution)/shard_map/ppermute | solution.py:230
  165.3 35.0 %collective-permute-start.17 = (bf16[16,64,128]{2,1,0:T(8,128)(2,1)}, bf16[16,64,128]{2,1,0:T(8,128)(2,1)}, u32[]{:S(2)}, u32[]{:S(2)}) collective-permute-start(bf16[16,64,128]{2,1,0:T(8,128)(2,1)} %get-tuple-element.31), channel_id=1, source_target_pairs={{0,6},{1,7},{2,0},{3,1},{4,2},{5,3},{6,4},{7,5},{8,14},{9,15},{10,... | collective-permute-start | bytes 786440 | tf_op jit(solution)/shard_map/ppermute | solution.py:230
  186.0 16.8 %collective-permute-start.18 = (bf16[16,64,128]{2,1,0:T(8,128)(2,1)}, bf16[16,64,128]{2,1,0:T(8,128)(2,1)S(1)}, u32[]{:S(2)}, u32[]{:S(2)}) collective-permute-start(bf16[16,64,128]{2,1,0:T(8,128)(2,1)} %copy-done.15), channel_id=1, source_target_pairs={{0,5},{1,6},{2,7},{3,0},{4,1},{5,2},{6,3},{7,4},{8,13},{9,14},{10,... | collective-permute-start | bytes 786440 | tf_op jit(solution)/shard_map/ppermute | solution.py:230
  186.3 23.3 %collective-permute-start.19 = (bf16[16,64,128]{2,1,0:T(8,128)(2,1)S(1)}, bf16[16,64,128]{2,1,0:T(8,128)(2,1)S(1)}, u32[]{:S(2)}, u32[]{:S(2)}) collective-permute-start(bf16[16,64,128]{2,1,0:T(8,128)(2,1)S(1)} %get-tuple-element.34), channel_id=1, source_target_pairs={{0,1},{1,2},{2,3},{3,4},{4,5},{5,6},{6,7},{7,0},{8,9},{9,10},{10,1... | collective-permute-start | bytes 786440 | tf_op jit(solution)/shard_map/ppermute | solution.py:230
  195.1 14.9 %collective-permute-start.20 = (bf16[16,64,128]{2,1,0:T(8,128)(2,1)S(1)}, bf16[16,64,128]{2,1,0:T(8,128)(2,1)S(1)}, u32[]{:S(2)}, u32[]{:S(2)}) collective-permute-start(bf16[16,64,128]{2,1,0:T(8,128)(2,1)S(1)} %get-tuple-element.35), channel_id=1, source_target_pairs={{0,2},{1,3},{2,4},{3,5},{4,6},{5,7},{6,0},{7,1},{8,10},{9,11},{10,... | collective-permute-start | bytes 786440 | tf_op jit(solution)/shard_map/ppermute | solution.py:230
  200.3 28.4 %collective-permute-start.21 = (bf16[16,64,128]{2,1,0:T(8,128)(2,1)S(1)}, bf16[16,64,128]{2,1,0:T(8,128)(2,1)S(1)}, u32[]{:S(2)}, u32[]{:S(2)}) collective-permute-start(bf16[16,64,128]{2,1,0:T(8,128)(2,1)S(1)} %get-tuple-element.36), channel_id=1, source_target_pairs={{0,3},{1,4},{2,5},{3,6},{4,7},{5,0},{6,1},{7,2},{8,11},{9,12},{10,... | collective-permute-start | bytes 786440 | tf_op jit(solution)/shard_map/ppermute | solution.py:230
  200.3 28.4 %collective-permute-start.22 = (bf16[16,64,128]{2,1,0:T(8,128)(2,1)S(1)}, bf16[16,64,128]{2,1,0:T(8,128)(2,1)S(1)}, u32[]{:S(2)}, u32[]{:S(2)}) collective-permute-start(bf16[16,64,128]{2,1,0:T(8,128)(2,1)S(1)} %get-tuple-element.38), channel_id=1, source_target_pairs={{0,7},{1,0},{2,1},{3,2},{4,3},{5,4},{6,5},{7,6},{8,15},{9,8},{10,9... | collective-permute-start | bytes 786440 | tf_op jit(solution)/shard_map/ppermute | solution.py:230
  202.7 26.0 %collective-permute-start.23 = (bf16[16,64,128]{2,1,0:T(8,128)(2,1)S(1)}, bf16[16,64,128]{2,1,0:T(8,128)(2,1)S(1)}, u32[]{:S(2)}, u32[]{:S(2)}) collective-permute-start(bf16[16,64,128]{2,1,0:T(8,128)(2,1)S(1)} %get-tuple-element.39), channel_id=1, source_target_pairs={{0,6},{1,7},{2,0},{3,1},{4,2},{5,3},{6,4},{7,5},{8,14},{9,15},{10,... | collective-permute-start | bytes 786440 | tf_op jit(solution)/shard_map/ppermute | solution.py:230
  209.6 27.9 %collective-permute-start.24 = (bf16[16,64,128]{2,1,0:T(8,128)(2,1)S(1)}, bf16[16,64,128]{2,1,0:T(8,128)(2,1)S(1)}, u32[]{:S(2)}, u32[]{:S(2)}) collective-permute-start(bf16[16,64,128]{2,1,0:T(8,128)(2,1)S(1)} %get-tuple-element.40), channel_id=1, source_target_pairs={{0,5},{1,6},{2,7},{3,0},{4,1},{5,2},{6,3},{7,4},{8,13},{9,14},{10,... | collective-permute-start | bytes 786440 | tf_op jit(solution)/shard_map/ppermute | solution.py:230
  240.8 13.9 %collective-permute-start.25 = (f32[8,128,128]{2,1,0:T(8,128)}, f32[8,128,128]{2,1,0:T(8,128)}, u32[]{:S(2)}, u32[]{:S(2)}) collective-permute-start(f32[8,128,128]{2,1,0:T(8,128)} %get-tuple-element.42), channel_id=1, source_target_pairs={{0,1},{1,2},{2,3},{3,4},{4,5},{5,6},{6,7},{7,0},{8,9},{9,10},{10,1... | collective-permute-start | bytes 1572872 | tf_op jit(solution)/shard_map/ppermute | solution.py:230
  244.7 11.8 %collective-permute-start.26 = (f32[8,128,128]{2,1,0:T(8,128)}, f32[8,128,128]{2,1,0:T(8,128)}, u32[]{:S(2)}, u32[]{:S(2)}) collective-permute-start(f32[8,128,128]{2,1,0:T(8,128)} %get-tuple-element.44), channel_id=1, source_target_pairs={{0,7},{1,0},{2,1},{3,2},{4,3},{5,4},{6,5},{7,6},{8,15},{9,8},{10,9... | collective-permute-start | bytes 1572872 | tf_op jit(solution)/shard_map/ppermute | solution.py:230
  (18 other events, 265.2 us)
Sparse Core Ops, SparseCore 0:
  27.0 51.6 all-gather.1

commit v3 on v2

v3 whole, which is shorter than its diff:
```python
import functools

import jax
import jax.numpy as jnp
from jax import lax
from jax.experimental import pallas as pl
from jax.experimental.pallas import tpu as pltpu
from jax.sharding import Mesh, PartitionSpec as P

BLOCK = 128
FROM_GROUP = 4
GROUPS = 32
RANKS = 8
TOKENS = 512
SIDE = 4
CHIPS = SIDE * SIDE
HALF = 8
REACH = 3
STEP = 256
PICKS = 4
NEXT = (1, 2 + REACH)
ORDER = (3, 7, 2, 6, 1, 5, 0, 4)
ALL = ("y", "x", "c", "z")
LAT = ("y", "x", "c")
MIB = 1 << 20


def activate(preact, bias, thresh):
    preact = preact + bias
    return (preact * jnp.clip(2.0 * preact / thresh - 1.0, 0.0, 1.0)).astype(jnp.bfloat16)


def early_kernel(place_ref, own_ref, other_ref, w_ref, bias_ref, thresh_ref, out_ref):
    piece = own_ref.shape[0] // CHIPS
    for side, acts_ref in enumerate((own_ref, other_ref)):
        preact = jnp.dot(acts_ref[...], w_ref[...], preferred_element_type=jnp.float32)
        codes = activate(preact, bias_ref[...], thresh_ref[...])
        for u in range(CHIPS):
            rank = place_ref[2 * u]
            at = pl.multiple_of(place_ref[2 * u + 1] ^ (side * piece), piece)
            for j in range(out_ref.shape[1]):
                out_ref[rank, j, pl.ds(at, piece), :] = codes[
                    u * piece : (u + 1) * piece, j * BLOCK : (j + 1) * BLOCK
                ]


def late_kernel(plane_ref, acts_ref, w_ref, bias_ref, thresh_ref, *refs):
    codes_ref = refs[-1]
    piece = acts_ref.shape[0] // RANKS
    preact = jnp.dot(acts_ref[...], w_ref[...], preferred_element_type=jnp.float32)
    codes_ref[...] = activate(preact, bias_ref[...], thresh_ref[...])
    for k in range(RANKS):
        at = pl.multiple_of(((plane_ref[0] + k) % RANKS) * piece, piece)
        codes = codes_ref[pl.ds(at, piece), :]
        for j in range(refs[k].shape[0]):
            refs[k][j] = codes[:, j * BLOCK : (j + 1) * BLOCK]


def encode(kernel, name, scalar, acts, weight, bias_vec, thresh, out_shape, scratch=()):
    depth, width = weight.shape
    outs = jax.tree.leaves(out_shape)
    specs = [
        pl.BlockSpec((STEP // BLOCK,) + out.shape[1:], lambda i, s: (i, 0, 0))
        if out.ndim == 3
        else pl.BlockSpec(out.shape[:1] + (STEP // BLOCK,) + out.shape[2:], lambda i, s: (0, i, 0, 0))
        for out in outs
    ]
    return pl.pallas_call(
        kernel,
        grid_spec=pltpu.PrefetchScalarGridSpec(
            num_scalar_prefetch=1,
            grid=(width // STEP,),
            in_specs=[pl.BlockSpec(one.shape, lambda i, s: (0, 0)) for one in acts]
            + [pl.BlockSpec((depth, STEP), lambda i, s: (0, i))]
            + [pl.BlockSpec((1, STEP), lambda i, s: (0, i))] * 2,
            out_specs=specs if isinstance(out_shape, list) else specs[0],
            scratch_shapes=scratch,
        ),
        out_shape=out_shape,
        compiler_params=pltpu.CompilerParams(vmem_limit_bytes=24 * MIB),
        cost_estimate=pl.CostEstimate(
            flops=2 * TOKENS * depth * width, bytes_accessed=8 * MIB, transcendentals=0
        ),
        name=name,
    )(scalar, *acts, weight, bias_vec[None], thresh[None])


def pick_kernel(index_ref, blocks_ref, out_ref, buf_ref, sems):
    chunk = out_ref.shape[0] // PICKS
    copies = []
    for part in range(PICKS):
        for i in range(part * chunk, (part + 1) * chunk):
            buf_ref[i] = blocks_ref[index_ref[i]]
        at = pl.ds(part * chunk, chunk)
        copies.append(pltpu.make_async_copy(buf_ref.at[at], out_ref.at[at], sems.at[part]))
        copies[-1].start()
    for copy in copies:
        copy.wait()


def pick(index, blocks):
    shape = (index.shape[0],) + blocks.shape[1:]
    return pl.pallas_call(
        pick_kernel,
        in_specs=[
            pl.BlockSpec(memory_space=pltpu.SMEM),
            pl.BlockSpec(memory_space=pltpu.VMEM),
        ],
        out_specs=pl.BlockSpec(memory_space=pltpu.HBM),
        out_shape=pltpu.HBM(shape, blocks.dtype),
        scratch_shapes=[pltpu.VMEM(shape, blocks.dtype), pltpu.SemaphoreType.DMA((PICKS,))],
        compiler_params=pltpu.CompilerParams(vmem_limit_bytes=16 * MIB),
        cost_estimate=pl.CostEstimate(flops=0, bytes_accessed=3 * MIB, transcendentals=0),
        name="pick",
    )(index, blocks)


def route_kernel(extras, slot_ref, at_ref, blocks_ref, *refs):
    extra_refs, refs = refs[:extras], refs[extras:]
    outs, (buf_ref, sems) = refs[:-2], refs[-2:]
    copies = []
    for n, out_ref in enumerate(outs):
        extra = 2 * HALF if extras and n in NEXT else 0
        if extra:
            copies.append(
                pltpu.make_async_copy(
                    extra_refs[NEXT.index(n)], out_ref.at[pl.ds(0, extra)], sems.at[len(outs) + NEXT.index(n)]
                )
            )
            copies[-1].start()
    for n in ORDER:
        extra = 2 * HALF if extras and n in NEXT else 0
        for part in range(2):
            first = slot_ref[2 * n + part]
            for i in range(HALF):
                buf_ref[n, part * HALF + i] = blocks_ref[at_ref[first + i]]
        copies.append(
            pltpu.make_async_copy(buf_ref.at[n], outs[n].at[pl.ds(extra, 2 * HALF)], sems.at[n])
        )
        copies[-1].start()
    for copy in copies:
        copy.wait()


def route(slot, at, blocks, extras=()):
    count = 2 * (REACH + 1)
    tail = blocks.shape[1:]
    return pl.pallas_call(
        functools.partial(route_kernel, len(extras)),
        in_specs=[
            pl.BlockSpec(memory_space=pltpu.SMEM),
            pl.BlockSpec(memory_space=pltpu.SMEM),
            pl.BlockSpec(memory_space=pltpu.VMEM),
        ]
        + [pl.BlockSpec(memory_space=pl.ANY)] * len(extras),
        out_specs=[pl.BlockSpec(memory_space=pltpu.HBM)] * count,
        out_shape=[
            pltpu.HBM((2 * HALF * (2 if extras and n in NEXT else 1),) + tail, blocks.dtype)
            for n in range(count)
        ],
        scratch_shapes=[
            pltpu.VMEM((count, 2 * HALF) + tail, blocks.dtype),
            pltpu.SemaphoreType.DMA((count + 2,)),
        ],
        compiler_params=pltpu.CompilerParams(vmem_limit_bytes=16 * MIB),
        cost_estimate=pl.CostEstimate(flops=0, bytes_accessed=4 * MIB, transcendentals=0),
        name="route",
    )(slot, at, blocks, *extras)


def gram_kernel(lows, *refs):
    out_ref = refs[-1]
    count = REACH + 1
    for i in range(HALF):
        left, right = (
            jnp.concatenate([refs[n][lows[n] + i] for n in range(base, base + count)], axis=0)
            for base in (0, count)
        )
        out_ref[i] = lax.dot_general(
            left, right, (((0,), (0,)), ((), ())), preferred_element_type=jnp.float32
        )


def gram(lows, parts):
    return pl.pallas_call(
        functools.partial(gram_kernel, lows),
        in_specs=[pl.BlockSpec(memory_space=pltpu.VMEM)] * len(parts),
        out_specs=pl.BlockSpec(memory_space=pltpu.VMEM),
        out_shape=jax.ShapeDtypeStruct((HALF, BLOCK, BLOCK), jnp.float32),
        compiler_params=pltpu.CompilerParams(vmem_limit_bytes=16 * MIB),
        cost_estimate=pl.CostEstimate(
            flops=2 * HALF * 256 * BLOCK * BLOCK, bytes_accessed=2 * MIB, transcendentals=0
        ),
        name="gram",
    )(*parts)


def finish_kernel(first_ref, live_ref, low_ref, low_far_ref, high_ref, high_far_ref, out_ref):
    for i in range(2 * HALF):
        near_ref, far_ref = (low_ref, low_far_ref) if i < HALF else (high_ref, high_far_ref)
        total = (near_ref[i % HALF] + far_ref[i % HALF]) * (1.0 / TOKENS)
        out_ref[i] = jnp.where(first_ref[0] + i < live_ref[0], total, 0.0)


def finish(first, live, low, low_far, high, high_far):
    return pl.pallas_call(
        finish_kernel,
        in_specs=[pl.BlockSpec(memory_space=pltpu.SMEM)] * 2
        + [pl.BlockSpec(memory_space=pltpu.VMEM)] * 4,
        out_specs=pl.BlockSpec(memory_space=pltpu.VMEM),
        out_shape=jax.ShapeDtypeStruct((2 * HALF, BLOCK, BLOCK), jnp.float32),
        compiler_params=pltpu.CompilerParams(vmem_limit_bytes=16 * MIB),
        cost_estimate=pl.CostEstimate(flops=MIB, bytes_accessed=3 * MIB, transcendentals=0),
        name="finish",
    )(first, live, low, low_far, high, high_far)


def positions(pair_blocks, group_blocks):
    source = pair_blocks // group_blocks
    within = pair_blocks % group_blocks
    slots = pair_blocks.shape[0]
    order = jnp.arange(slots)
    same = source[:, None, :] == source[None, :, :]
    before = (order[None, :] < order[:, None])[:, :, None]
    rank = jnp.sum(same & before, axis=1, dtype=jnp.int32)
    position = source * FROM_GROUP + rank
    hit = position[None, :, :] == order[:, None, None]
    table = jnp.sum(jnp.where(hit, within[None, :, :], 0), axis=1, dtype=jnp.int32)
    return position, table


def shift(value, axis, size, by):
    return lax.ppermute(value, axis, [(i, (i + by) % size) for i in range(size)])


def gather_z(acts):
    spread = jnp.broadcast_to(acts[None], (RANKS,) + acts.shape)
    return lax.all_to_all(spread, "z", 0, 0, tiled=True)


def ring_of_four(value, axis):
    return [value] + [shift(value, axis, SIDE, k) for k in range(1, SIDE)]


def gather_chips(rows):
    width = rows.shape[1] // 2
    left, right = rows[:, :width], rows[:, width:]
    left_x = jnp.stack(ring_of_four(left, "x"))
    right_y = jnp.stack(ring_of_four(right, "y"))
    left_all = jnp.stack(ring_of_four(left_x, "y"))
    right_all = jnp.stack(ring_of_four(right_y, "x"), axis=1)
    return jnp.concatenate([left_all, right_all], axis=3).reshape(-1, rows.shape[1])


def shards(
    acts_early,
    acts_late,
    enc_early,
    enc_late,
    bias_early,
    bias_late,
    thresh_early,
    thresh_late,
    pair_blocks,
    live_pairs,
):
    y, x, c, z = (lax.axis_index(name).astype(jnp.int32) for name in ALL)
    depth = acts_early.shape[1]
    width = enc_early.shape[1]
    rank_blocks = width // BLOCK
    group_blocks = RANKS * rank_blocks

    near = gather_z(jnp.stack([acts_early, acts_late]))
    rows_early = near[:, 0].reshape(-1, depth)
    rows_late = near[:, 1].reshape(-1, depth)
    all_late = lax.all_gather(rows_late, LAT, axis=0, tiled=True)

    position, table = positions(pair_blocks, group_blocks)
    asked = lax.all_to_all(
        table.reshape(GROUPS, FROM_GROUP * 2), LAT, split_axis=0, concat_axis=0, tiled=True
    ).reshape(GROUPS * FROM_GROUP, 2)
    asked_late = ((z - asked[:, 1] // rank_blocks) & (RANKS - 1)) * rank_blocks + (
        asked[:, 1] % rank_blocks
    )

    own = gather_chips(rows_early)
    step = jnp.arange(CHIPS, dtype=jnp.int32)
    chip = ((y - step // SIDE) & (SIDE - 1)) * SIDE + ((x - step) & (SIDE - 1))
    place = jnp.stack([chip // 2, (chip & 1) * 32 + c * 16], axis=1).reshape(-1)

    def spread(sent):
        got = lax.all_to_all(
            sent.reshape((GROUPS, FROM_GROUP) + sent.shape[1:]),
            LAT,
            split_axis=0,
            concat_axis=0,
            tiled=True,
        )
        return got.reshape(sent.shape)

    offsets = []
    for side in range(2):
        for k in range(REACH + 1):
            by = k if side == 0 else -k
            past = by + (1 if side == 0 else -1)
            offsets += [(past, side), (by, 1 - side)]
    plane = jnp.array([by for by, half in offsets], jnp.int32)
    half = jnp.array([half for by, half in offsets], jnp.int32)
    slots = ((z + plane) & (RANKS - 1)) * (2 * HALF) + half * HALF

    def trade(parts, k):
        return [shift(part, "z", RANKS, by) for part, by in zip(parts, (k, -k))]

    shape = (rank_blocks, TOKENS // RANKS, BLOCK)
    other = shift(own, "c", 2, 1)
    codes_early = encode(
        early_kernel, "encode_early", place, (own, other), enc_early, bias_early, thresh_early,
        jax.ShapeDtypeStruct((RANKS,) + shape, jnp.bfloat16),
    )
    codes_early = lax.all_to_all(codes_early, "z", split_axis=0, concat_axis=0, tiled=True)
    codes_late = encode(
        late_kernel, "encode_late", z[None], (all_late,), enc_late, bias_late, thresh_late,
        [jax.ShapeDtypeStruct(shape, jnp.bfloat16)] * RANKS,
        [pltpu.VMEM((TOKENS, STEP), jnp.bfloat16)],
    )
    codes_early, codes_late = lax.optimization_barrier((codes_early, codes_late))
    sent_early = pick(asked[:, 0], codes_early.reshape((group_blocks,) + shape[1:]))
    got_early = spread(sent_early)
    codes_late = [codes_late[0]] + [shift(codes_late[k], "z", RANKS, k) for k in range(1, RANKS)]
    sent_late = pick(asked_late, jnp.concatenate(codes_late))
    got_early, sent_late = lax.optimization_barrier((got_early, sent_late))

    def both(parts, k):
        return parts[k], parts[k + REACH + 1]

    parts = route(slots, position[:, 0], got_early)
    sent_late, parts = lax.optimization_barrier((sent_late, parts))
    left = {k: trade(both(parts, k), k) for k in (3, 2)}
    left, got_late = lax.optimization_barrier((left, spread(sent_late)))
    left[0] = both(parts, 0)

    parts = route(slots, position[:, 1], got_late, both(parts, 1))
    right = {k: trade(both(parts, k), k) for k in (3, 2, 1)}
    right[0] = both(parts, 0)
    left[1] = right[1]

    def tiles(side, near):
        low = HALF if near else 0
        parts = [left[k][side] for k in range(REACH + 1)] + [right[k][side] for k in range(REACH + 1)]
        lows = [low] * len(parts)
        lows[REACH + 2] += 2 * HALF
        return gram(tuple(lows), parts)

    low_far = shift(tiles(0, False), "z", RANKS, 1)
    high_far = shift(tiles(1, False), "z", RANKS, -1)
    high = tiles(0, True)
    low = tiles(1, True)
    return finish((z * (2 * HALF))[None], live_pairs, low, low_far, high, high_far)


def solution(mesh):
    fine = Mesh(mesh.devices.reshape(SIDE, SIDE, 2, RANKS), ALL)
    in_specs = (
        P(ALL, None),
        P(ALL, None),
        P(None, ALL),
        P(None, ALL),
        P(ALL),
        P(ALL),
        P(ALL),
        P(ALL),
        P(LAT, None),
        P(LAT),
    )
    out_specs = P(ALL, None, None)
    return jax.shard_map(shards, mesh=fine, in_specs=in_specs, out_specs=out_specs, check_vma=False)
```

time: 268 us -> 248 us (0.925)
  waiting for transfers between devices: 122 us -> 92.8 us
  starting transfers between devices: 70.7 us -> 79.3 us
    all_to_all x2, waiting for transfers between devices: 44.7 us -> 6.86 us  [spread(): lax.all_to_all(sent.reshape((GROUPS, FROM_GROUP) + sent.shape[1:]), LAT,...]
    ppermute x27 -> x32, waiting for transfers between devices: 54.4 us -> 77.8 us  [shift(): lax.ppermute(value, axis, [(i, (i + by) % size) for i in range(size)])]
    all_to_all x2 -> x1, waiting for transfers between devices: 20.9 us -> 6.5 us  [shards(): lax.all_to_all(codes_early, 'z', split_axis=0, concat_axis=0, tiled=True)]
    ppermute x27 -> x32, starting transfers between devices: 46.2 us -> 56.6 us  [shift(): lax.ppermute(value, axis, [(i, (i + by) % size) for i in range(size)])]
    all_to_all x2 -> x1, starting transfers between devices: 7.17 us -> 3.69 us  [shards(): lax.all_to_all(codes_early, 'z', split_axis=0, concat_axis=0, tiled=True)]
    unnamed x34 -> x59, local copies, waits for them, and re-layouts: 15.1 us -> 13.9 us
    pallas_call x6 -> x8, Pallas kernels: 15.4 us -> 15 us  [the longest x2 7.94 us: encode(): pl.pallas_call(kernel, grid_spec=pltpu.PrefetchScalarGridSpec(num_scalar_...]
  transfers between devices with their start and end apart: 33 -> 37, of which waited for: 15 -> 18; matrix products, arithmetic and copies ran while one was open for 1% -> 1% of each run, Pallas kernels for 5% -> 5%
where the time goes in v3:
time: 248 us; the launch traced here: 245 us
  waiting for transfers between devices  92.8 us (37%)
  starting transfers between devices  79.3 us (32%)
  Pallas kernels  21.3 us (9%)
  blocking collectives  18.6 us (8%)
  local copies, waits for them, and re-layouts  16.8 us (7%)
  between operations  14.6 us (6%)
    ppermute x32, waiting for transfers between devices, shift(): lax.ppermute(value, axis, [(i, (i + by) % size) for i in range(size)])  77.8 us
    ppermute x32, starting transfers between devices, shift(): lax.ppermute(value, axis, [(i, (i + by) % size) for i in range(size)])  56.6 us
    all_to_all x1, blocking collectives, gather_z(): return lax.all_to_all(spread, 'z', 0, 0, tiled=True)  18.6 us
    unnamed x59, local copies, waits for them, and re-layouts  13.9 us
    all_to_all x2, starting transfers between devices, spread(): lax.all_to_all(sent.reshape((GROUPS, FROM_GROUP) + sent.shape[1:]), LAT,...  13.7 us
    pallas_call x2, Pallas kernels, encode(): pl.pallas_call(kernel, grid_spec=pltpu.PrefetchScalarGridSpec(num_scalar_...  7.94 us
    all_to_all x2, waiting for transfers between devices, spread(): lax.all_to_all(sent.reshape((GROUPS, FROM_GROUP) + sent.shape[1:]), LAT,...  6.86 us
    all_to_all x1, waiting for transfers between devices, shards(): lax.all_to_all(codes_early, 'z', split_axis=0, concat_axis=0, tiled=True)  6.5 us
  transfers between devices with their start and end apart: 37, of which 18 were waited for; matrix products, arithmetic and copies ran while one was open for 1% of the time, Pallas kernels for 5%

profile of v3, /device:TPU:1, one launch (start us, length us, event | category | flops | bytes accessed | tf_op | source)
XLA Modules:
  0.0 245.4 jit_solution(13747239781463153510)
XLA Ops:
  7.5 18.6 %all_to_all.29 = bf16[8,2,2,3584]{3,2,1,0:T(2,128)(2,1)S(1)} all-to-all(bf16[8,2,2,3584]{3,2,1,0:T(2,128)(2,1)S(1)} %broadcast_in_dim.47), channel_id=1, replica_groups=mesh['y'=4,'x'=4,'c'=2,'z'=8] {'z'}, dimensions={0} | all-to-all | bytes 458752 | tf_op jit(solution)/shard_map/all_to_all | solution.py:238
  28.3 2.5 collective-permute-start.1
  33.2 2.6 %collective-permute-start.7 = (bf16[16,1792]{1,0:T(8,128)(2,1)S(1)}, bf16[16,1792]{1,0:T(8,128)(2,1)S(1)}, u32[]{:S(2)}, u32[]{:S(2)}) collective-permute-start(bf16[16,1792]{1,0:T(8,128)(2,1)S(1)} %get-tuple-element.113), channel_id=1, source_target_pairs={{0,128},{64,192},{128,0},{192,64},{1,129},{65,193},{129,1},{193,65... | collective-permute-start | bytes 172040 | tf_op jit(solution)/shard_map/ppermute | solution.py:233
  37.1 2.7 %collective-permute-start.5 = (bf16[4,16,1792]{2,1,0:T(8,128)(2,1)S(1)}, bf16[4,16,1792]{2,1,0:T(8,128)(2,1)S(1)}, u32[]{:S(2)}, u32[]{:S(2)}) collective-permute-start(bf16[4,16,1792]{2,1,0:T(8,128)(2,1)S(1)} %get-tuple-element.108), channel_id=1, source_target_pairs={{0,192},{64,0},{128,64},{192,128},{1,193},{65,1},{129,65},{193,129... | collective-permute-start | bytes 688136 | tf_op jit(solution)/shard_map/ppermute | solution.py:233
  42.0 2.8 %collective-permute-done.4 = bf16[4,16,1792]{2,1,0:T(8,128)(2,1)S(1)} collective-permute-done((bf16[4,16,1792]{2,1,0:T(8,128)(2,1)S(1)}, bf16[4,16,1792]{2,1,0:T(8,128)(2,1)S(1)}, u32[]{:S(2)}, u32[]{:S(2)}) %collective-permute-start.4) | collective-permute-done | bytes 229408 | tf_op jit(solution)/shard_map/ppermute | solution.py:233
  44.8 4.9 %collective-permute-done.5 = bf16[4,16,1792]{2,1,0:T(8,128)(2,1)S(1)} collective-permute-done((bf16[4,16,1792]{2,1,0:T(8,128)(2,1)S(1)}, bf16[4,16,1792]{2,1,0:T(8,128)(2,1)S(1)}, u32[]{:S(2)}, u32[]{:S(2)}) %collective-permute-start.5) | collective-permute-done | bytes 229408 | tf_op jit(solution)/shard_map/ppermute | solution.py:233
  51.8 5.7 %collective-permute-start.12 = (bf16[256,3584]{1,0:T(8,128)(2,1)S(1)}, bf16[256,3584]{1,0:T(8,128)(2,1)}, u32[]{:S(2)}, u32[]{:S(2)}) collective-permute-start(bf16[256,3584]{1,0:T(8,128)(2,1)S(1)} %bitcast.47), channel_id=1, source_target_pairs={{0,8},{8,0},{1,9},{9,1},{2,10},{10,2},{3,11},{11,3},{4,12},{12,4},... | collective-permute-start | bytes 5505032 | tf_op jit(solution)/shard_map/ppermute | solution.py:233
  58.6 5.2 %all-to-all-start = ((s32[32,1,8]{2,1,0:T(1,128)}), s32[32,1,8]{2,1,0:T(1,128)S(1)}, u32[]{:S(2)}, u32[]{:S(2)}) async-start(s32[32,1,8]{2,1,0:T(1,128)} %bitcast.1), calls=%async_computation | async-start | bytes 32768 | tf_op jit(solution)/shard_map/all_to_all | solution.py:279
  66.1 5.3 %encode_early.1 = bf16[8,4,64,128]{3,2,1,0:T(8,128)(2,1)} custom-call(s32[32]{0:T(128)S(1)} %reshape.157.place_ref, bf16[256,3584]{1,0:T(8,128)(2,1)S(1)} %bitcast.48, bf16[256,3584]{1,0:T(8,128)(2,1)} %collective-permute-done.12.other_ref, bf16[3584,512]{1,0:T(8,128)(2,1)S(1)} %copy-done, f32[1,512]{1,0:T(1,128)S(1)} %bitcast.50, f32[1,512]{1,0:T(1,128)S(1)} %bitcast.51), custom_call_target="tpu_custom_call" | custom-call | flops 1879048192 | bytes 8388608 | tf_op jit(solution)/shard_map/encode_early/pallas_call | solution.py:68
  71.5 3.7 %all-to-all-start.2 = ((bf16[8,4,64,128]{3,2,1,0:T(8,128)(2,1)}), bf16[8,4,64,128]{3,2,1,0:T(8,128)(2,1)S(1)}, u32[]{:S(2)}, u32[]{:S(2)}) async-start(bf16[8,4,64,128]{3,2,1,0:T(8,128)(2,1)} %encode_early.1), calls=%async_computation.2 | async-start | bytes 1048576 | tf_op jit(solution)/shard_map/all_to_all | solution.py:320
  82.5 2.6 %encode_late.1 = (bf16[4,64,128]{2,1,0:T(8,128)(2,1)S(1)}, bf16[4,64,128]{2,1,0:T(8,128)(2,1)S(1)}, bf16[4,64,128]{2,1,0:T(8,128)(2,1)S(1)}, bf16[4,64,128]{2,1,...) custom-call(s32[1]{0:T(128)} %bitcast.26.plane_ref, ...), custom_call_target="tpu_custom_call" | custom-call | flops 1879048192 | bytes 8388608 | tf_op jit(solution)/shard_map/encode_late/pallas_call | solution.py:68
  85.1 6.5 %all-to-all-done.2 = bf16[8,4,64,128]{3,2,1,0:T(8,128)(2,1)S(1)} async-done(((bf16[8,4,64,128]{3,2,1,0:T(8,128)(2,1)}), bf16[8,4,64,128]{3,2,1,0:T(8,128)(2,1)S(1)}, u32[]{:S(2)}, u32[]{:S(2)}) %all-to-all-start.2) | async-done | bytes 524320 | tf_op jit(solution)/shard_map/all_to_all | solution.py:320
  93.6 7.6 %all-to-all-start.3 = ((bf16[32,4,64,128]{3,2,1,0:T(8,128)(2,1)}), bf16[32,4,64,128]{3,2,1,0:T(8,128)(2,1)S(1)}, u32[]{:S(2)}, u32[]{:S(2)}) async-start(bf16[32,4,64,128]{3,2,1,0:T(8,128)(2,1)} %bitcast.54), calls=%async_computation.3 | async-start | bytes 4194304 | tf_op jit(solution)/shard_map/all_to_all | solution.py:292
  102.9 2.4 collective-permute-start.15
  105.3 3.1 %collective-permute-start.16 = (bf16[4,64,128]{2,1,0:T(8,128)(2,1)S(1)}, bf16[4,64,128]{2,1,0:T(8,128)(2,1)S(1)}, u32[]{:S(2)}, u32[]{:S(2)}) collective-permute-start(bf16[4,64,128]{2,1,0:T(8,128)(2,1)S(1)} %get-tuple-element.67), channel_id=1, source_target_pairs={{0,4},{1,5},{2,6},{3,7},{4,0},{5,1},{6,2},{7,3},{8,12},{9,13},{10,... | collective-permute-start | bytes 196616 | tf_op jit(solution)/shard_map/ppermute | solution.py:233
  109.6 2.6 %collective-permute-start.18 = (bf16[4,64,128]{2,1,0:T(8,128)(2,1)S(1)}, bf16[4,64,128]{2,1,0:T(8,128)(2,1)S(1)}, u32[]{:S(2)}, u32[]{:S(2)}) collective-permute-start(bf16[4,64,128]{2,1,0:T(8,128)(2,1)S(1)} %get-tuple-element.69), channel_id=1, source_target_pairs={{0,6},{1,7},{2,0},{3,1},{4,2},{5,3},{6,4},{7,5},{8,14},{9,15},{10,... | collective-permute-start | bytes 196616 | tf_op jit(solution)/shard_map/ppermute | solution.py:233
  113.3 3.1 %collective-permute-done.16 = bf16[4,64,128]{2,1,0:T(8,128)(2,1)S(1)} collective-permute-done((bf16[4,64,128]{2,1,0:T(8,128)(2,1)S(1)}, bf16[4,64,128]{2,1,0:T(8,128)(2,1)S(1)}, u32[]{:S(2)}, u32[]{:S(2)}) %collective-permute-start.16) | collective-permute-done | bytes 65568 | tf_op jit(solution)/shard_map/ppermute | solution.py:233
  116.9 2.8 %collective-permute-done.18 = bf16[4,64,128]{2,1,0:T(8,128)(2,1)S(1)} collective-permute-done((bf16[4,64,128]{2,1,0:T(8,128)(2,1)S(1)}, bf16[4,64,128]{2,1,0:T(8,128)(2,1)S(1)}, u32[]{:S(2)}, u32[]{:S(2)}) %collective-permute-start.18) | collective-permute-done | bytes 65568 | tf_op jit(solution)/shard_map/ppermute | solution.py:233
  122.1 6.9 %all-to-all-done.3 = bf16[32,4,64,128]{3,2,1,0:T(8,128)(2,1)S(1)} async-done(((bf16[32,4,64,128]{3,2,1,0:T(8,128)(2,1)}), bf16[32,4,64,128]{3,2,1,0:T(8,128)(2,1)S(1)}, u32[]{:S(2)}, u32[]{:S(2)}) %all-to-all-start.3) | async-done | bytes 2097184 | tf_op jit(solution)/shard_map/all_to_all | solution.py:292
  131.0 6.2 %all-to-all-start.4 = ((bf16[32,4,64,128]{3,2,1,0:T(8,128)(2,1)}), bf16[32,4,64,128]{3,2,1,0:T(8,128)(2,1)S(1)}, u32[]{:S(2)}, u32[]{:S(2)}) async-start(bf16[32,4,64,128]{3,2,1,0:T(8,128)(2,1)} %bitcast.55), calls=%async_computation.4 | async-start | bytes 4194304 | tf_op jit(solution)/shard_map/all_to_all | solution.py:292
  138.1 2.7 %collective-permute-start.21 = (bf16[16,64,128]{2,1,0:T(8,128)(2,1)}, bf16[16,64,128]{2,1,0:T(8,128)(2,1)S(1)}, u32[]{:S(2)}, u32[]{:S(2)}) collective-permute-start(bf16[16,64,128]{2,1,0:T(8,128)(2,1)} %get-tuple-element.83), channel_id=1, source_target_pairs={{0,6},{1,7},{2,0},{3,1},{4,2},{5,3},{6,4},{7,5},{8,14},{9,15},{10,... | collective-permute-start | bytes 786440 | tf_op jit(solution)/shard_map/ppermute | solution.py:233
  141.0 4.3 %collective-permute-start.23 = (bf16[16,64,128]{2,1,0:T(8,128)(2,1)}, bf16[16,64,128]{2,1,0:T(8,128)(2,1)S(1)}, u32[]{:S(2)}, u32[]{:S(2)}) collective-permute-start(bf16[16,64,128]{2,1,0:T(8,128)(2,1)} %get-tuple-element.85), channel_id=1, source_target_pairs={{0,5},{1,6},{2,7},{3,0},{4,1},{5,2},{6,3},{7,4},{8,13},{9,14},{10,... | collective-permute-start | bytes 786440 | tf_op jit(solution)/shard_map/ppermute | solution.py:233
  145.3 3.1 %collective-permute-done.20.refs_2_ = bf16[16,64,128]{2,1,0:T(8,128)(2,1)S(1)} collective-permute-done((bf16[16,64,128]{2,1,0:T(8,128)(2,1)}, bf16[16,64,128]{2,1,0:T(8,128)(2,1)S(1)}, u32[]{:S(2)}, u32[]{:S(2)}) %collective-permute-start.20) | collective-permute-done | bytes 262176 | tf_op jit(solution)/shard_map/ppermute | solution.py:233
  150.5 17.4 %collective-permute-done.22.refs_3_ = bf16[16,64,128]{2,1,0:T(8,128)(2,1)S(1)} collective-permute-done((bf16[16,64,128]{2,1,0:T(8,128)(2,1)}, bf16[16,64,128]{2,1,0:T(8,128)(2,1)S(1)}, u32[]{:S(2)}, u32[]{:S(2)}) %collective-permute-start.22) | collective-permute-done | bytes 262176 | tf_op jit(solution)/shard_map/ppermute | solution.py:233
  172.7 3.4 %collective-permute-start.24 = (bf16[32,64,128]{2,1,0:T(8,128)(2,1)}, bf16[32,64,128]{2,1,0:T(8,128)(2,1)S(1)}, u32[]{:S(2)}, u32[]{:S(2)}) collective-permute-start(bf16[32,64,128]{2,1,0:T(8,128)(2,1)} %get-tuple-element.90), channel_id=1, source_target_pairs={{0,7},{1,0},{2,1},{3,2},{4,3},{5,4},{6,5},{7,6},{8,15},{9,8},{10,9... | collective-permute-start | bytes 1572872 | tf_op jit(solution)/shard_map/ppermute | solution.py:233
  176.0 2.8 %collective-permute-start.25 = (bf16[16,64,128]{2,1,0:T(8,128)(2,1)}, bf16[16,64,128]{2,1,0:T(8,128)(2,1)S(1)}, u32[]{:S(2)}, u32[]{:S(2)}) collective-permute-start(bf16[16,64,128]{2,1,0:T(8,128)(2,1)} %get-tuple-element.94), channel_id=1, source_target_pairs={{0,6},{1,7},{2,0},{3,1},{4,2},{5,3},{6,4},{7,5},{8,14},{9,15},{10,... | collective-permute-start | bytes 786440 | tf_op jit(solution)/shard_map/ppermute | solution.py:233
  181.0 2.6 %collective-permute-start.28 = (bf16[16,64,128]{2,1,0:T(8,128)(2,1)}, bf16[16,64,128]{2,1,0:T(8,128)(2,1)S(1)}, u32[]{:S(2)}, u32[]{:S(2)}) collective-permute-start(bf16[16,64,128]{2,1,0:T(8,128)(2,1)} %get-tuple-element.101), channel_id=1, source_target_pairs={{0,2},{1,3},{2,4},{3,5},{4,6},{5,7},{6,0},{7,1},{8,10},{9,11},{10,... | collective-permute-start | bytes 786440 | tf_op jit(solution)/shard_map/ppermute | solution.py:233
  183.6 15.9 %collective-permute-done.25.refs_6_ = bf16[16,64,128]{2,1,0:T(8,128)(2,1)S(1)} collective-permute-done((bf16[16,64,128]{2,1,0:T(8,128)(2,1)}, bf16[16,64,128]{2,1,0:T(8,128)(2,1)S(1)}, u32[]{:S(2)}, u32[]{:S(2)}) %collective-permute-start.25) | collective-permute-done | bytes 262176 | tf_op jit(solution)/shard_map/ppermute | solution.py:233
  199.6 4.6 %collective-permute-start.29 = (bf16[16,64,128]{2,1,0:T(8,128)(2,1)}, bf16[16,64,128]{2,1,0:T(8,128)(2,1)S(1)}, u32[]{:S(2)}, u32[]{:S(2)}) collective-permute-start(bf16[16,64,128]{2,1,0:T(8,128)(2,1)} %get-tuple-element.102), channel_id=1, source_target_pairs={{0,3},{1,4},{2,5},{3,6},{4,7},{5,0},{6,1},{7,2},{8,11},{9,12},{10,... | collective-permute-start | bytes 786440 | tf_op jit(solution)/shard_map/ppermute | solution.py:233
  204.2 14.3 %collective-permute-done.26.refs_7_ = bf16[16,64,128]{2,1,0:T(8,128)(2,1)S(1)} collective-permute-done((bf16[16,64,128]{2,1,0:T(8,128)(2,1)}, bf16[16,64,128]{2,1,0:T(8,128)(2,1)S(1)}, u32[]{:S(2)}, u32[]{:S(2)}) %collective-permute-start.26) | collective-permute-done | bytes 262176 | tf_op jit(solution)/shard_map/ppermute | solution.py:233
  228.8 4.3 %collective-permute-done.31.high_far_ref = f32[8,128,128]{2,1,0:T(8,128)} collective-permute-done((f32[8,128,128]{2,1,0:T(8,128)}, f32[8,128,128]{2,1,0:T(8,128)}, u32[]{:S(2)}, u32[]{:S(2)}) %collective-permute-start.31) | collective-permute-done | bytes 524320 | tf_op jit(solution)/shard_map/ppermute | solution.py:233
  233.1 3.1 %collective-permute-done.30.low_far_ref = f32[8,128,128]{2,1,0:T(8,128)} collective-permute-done((f32[8,128,128]{2,1,0:T(8,128)}, f32[8,128,128]{2,1,0:T(8,128)}, u32[]{:S(2)}, u32[]{:S(2)}) %collective-permute-start.30) | collective-permute-done | bytes 524320 | tf_op jit(solution)/shard_map/ppermute | solution.py:233
  (142 shorter events, 54.6 us)
Async XLA Ops:
  6.5 71.8 %all-gather.2.cloned.1.call-start = ((), (), s32[]{:S(2)}) async-start(), calls=%async_computation.5 | async-start | bytes 3784704 | tf_op jit(solution)/shard_map/all_gather | solution.py:276
  27.0 8.8 %collective-permute-start = (bf16[16,1792]{1,0:T(8,128)(2,1)S(1)}, bf16[16,1792]{1,0:T(8,128)(2,1)S(1)}, u32[]{:S(2)}, u32[]{:S(2)}) collective-permute-start(bf16[16,1792]{1,0:T(8,128)(2,1)S(1)} %get-tuple-element.114), channel_id=1, source_target_pairs={{0,16},{16,32},{32,48},{48,0},{1,17},{17,33},{33,49},{49,1},{2,18}... | collective-permute-start | bytes 172040 | tf_op jit(solution)/shard_map/ppermute | solution.py:233
  28.3 8.6 %collective-permute-start.1 = (bf16[16,1792]{1,0:T(8,128)(2,1)S(1)}, bf16[16,1792]{1,0:T(8,128)(2,1)S(1)}, u32[]{:S(2)}, u32[]{:S(2)}) collective-permute-start(bf16[16,1792]{1,0:T(8,128)(2,1)S(1)} %get-tuple-element.114), channel_id=1, source_target_pairs={{0,32},{16,48},{32,0},{48,16},{1,33},{17,49},{33,1},{49,17},{2,34}... | collective-permute-start | bytes 172040 | tf_op jit(solution)/shard_map/ppermute | solution.py:233
  31.9 7.9 %collective-permute-start.6 = (bf16[16,1792]{1,0:T(8,128)(2,1)S(1)}, bf16[16,1792]{1,0:T(8,128)(2,1)S(1)}, u32[]{:S(2)}, u32[]{:S(2)}) collective-permute-start(bf16[16,1792]{1,0:T(8,128)(2,1)S(1)} %get-tuple-element.113), channel_id=1, source_target_pairs={{0,64},{64,128},{128,192},{192,0},{1,65},{65,129},{129,193},{193,1... | collective-permute-start | bytes 172040 | tf_op jit(solution)/shard_map/ppermute | solution.py:233
  36.9 7.9 %collective-permute-start.4 = (bf16[4,16,1792]{2,1,0:T(8,128)(2,1)S(1)}, bf16[4,16,1792]{2,1,0:T(8,128)(2,1)S(1)}, u32[]{:S(2)}, u32[]{:S(2)}) collective-permute-start(bf16[4,16,1792]{2,1,0:T(8,128)(2,1)S(1)} %get-tuple-element.108), channel_id=1, source_target_pairs={{0,128},{64,192},{128,0},{192,64},{1,129},{65,193},{129,1},{193,65... | collective-permute-start | bytes 688136 | tf_op jit(solution)/shard_map/ppermute | solution.py:233
  37.1 12.6 %collective-permute-start.5 = (bf16[4,16,1792]{2,1,0:T(8,128)(2,1)S(1)}, bf16[4,16,1792]{2,1,0:T(8,128)(2,1)S(1)}, u32[]{:S(2)}, u32[]{:S(2)}) collective-permute-start(bf16[4,16,1792]{2,1,0:T(8,128)(2,1)S(1)} %get-tuple-element.108), channel_id=1, source_target_pairs={{0,192},{64,0},{128,64},{192,128},{1,193},{65,1},{129,65},{193,129... | collective-permute-start | bytes 688136 | tf_op jit(solution)/shard_map/ppermute | solution.py:233
  39.8 11.7 %collective-permute-start.3 = (bf16[4,16,1792]{2,1,0:T(8,128)(2,1)S(1)}, bf16[4,16,1792]{2,1,0:T(8,128)(2,1)S(1)}, u32[]{:S(2)}, u32[]{:S(2)}) collective-permute-start(bf16[4,16,1792]{2,1,0:T(8,128)(2,1)S(1)} %get-tuple-element.108), channel_id=1, source_target_pairs={{0,64},{64,128},{128,192},{192,0},{1,65},{65,129},{129,193},{193,1... | collective-permute-start | bytes 688136 | tf_op jit(solution)/shard_map/ppermute | solution.py:233
  39.9 11.7 %collective-permute-start.9 = (bf16[4,16,1792]{2,1,0:T(8,128)(2,1)S(1)}, bf16[4,16,1792]{2,1,0:T(8,128)(2,1)S(1)}, u32[]{:S(2)}, u32[]{:S(2)}) collective-permute-start(bf16[4,16,1792]{2,1,0:T(8,128)(2,1)S(1)} %get-tuple-element.110), channel_id=1, source_target_pairs={{0,16},{16,32},{32,48},{48,0},{1,17},{17,33},{33,49},{49,1},{2,18}... | collective-permute-start | bytes 688136 | tf_op jit(solution)/shard_map/ppermute | solution.py:233
  40.3 11.3 %collective-permute-start.10 = (bf16[4,16,1792]{2,1,0:T(8,128)(2,1)S(1)}, bf16[4,16,1792]{2,1,0:T(8,128)(2,1)S(1)}, u32[]{:S(2)}, u32[]{:S(2)}) collective-permute-start(bf16[4,16,1792]{2,1,0:T(8,128)(2,1)S(1)} %get-tuple-element.110), channel_id=1, source_target_pairs={{0,32},{16,48},{32,0},{48,16},{1,33},{17,49},{33,1},{49,17},{2,34}... | collective-permute-start | bytes 688136 | tf_op jit(solution)/shard_map/ppermute | solution.py:233
  51.8 12.3 %collective-permute-start.12 = (bf16[256,3584]{1,0:T(8,128)(2,1)S(1)}, bf16[256,3584]{1,0:T(8,128)(2,1)}, u32[]{:S(2)}, u32[]{:S(2)}) collective-permute-start(bf16[256,3584]{1,0:T(8,128)(2,1)S(1)} %bitcast.47), channel_id=1, source_target_pairs={{0,8},{8,0},{1,9},{9,1},{2,10},{10,2},{3,11},{11,3},{4,12},{12,4},... | collective-permute-start | bytes 5505032 | tf_op jit(solution)/shard_map/ppermute | solution.py:233
  58.6 12.9 %all-to-all-start = ((s32[32,1,8]{2,1,0:T(1,128)}), s32[32,1,8]{2,1,0:T(1,128)S(1)}, u32[]{:S(2)}, u32[]{:S(2)}) async-start(s32[32,1,8]{2,1,0:T(1,128)} %bitcast.1), calls=%async_computation | async-start | bytes 32768 | tf_op jit(solution)/shard_map/all_to_all | solution.py:279
  71.5 20.1 %all-to-all-start.2 = ((bf16[8,4,64,128]{3,2,1,0:T(8,128)(2,1)}), bf16[8,4,64,128]{3,2,1,0:T(8,128)(2,1)S(1)}, u32[]{:S(2)}, u32[]{:S(2)}) async-start(bf16[8,4,64,128]{3,2,1,0:T(8,128)(2,1)} %encode_early.1), calls=%async_computation.2 | async-start | bytes 1048576 | tf_op jit(solution)/shard_map/all_to_all | solution.py:320
  93.6 35.4 %all-to-all-start.3 = ((bf16[32,4,64,128]{3,2,1,0:T(8,128)(2,1)}), bf16[32,4,64,128]{3,2,1,0:T(8,128)(2,1)S(1)}, u32[]{:S(2)}, u32[]{:S(2)}) async-start(bf16[32,4,64,128]{3,2,1,0:T(8,128)(2,1)} %bitcast.54), calls=%async_computation.3 | async-start | bytes 4194304 | tf_op jit(solution)/shard_map/all_to_all | solution.py:292
  101.2 8.3 %collective-permute-start.13 = (bf16[4,64,128]{2,1,0:T(8,128)(2,1)S(1)}, bf16[4,64,128]{2,1,0:T(8,128)(2,1)S(1)}, u32[]{:S(2)}, u32[]{:S(2)}) collective-permute-start(bf16[4,64,128]{2,1,0:T(8,128)(2,1)S(1)} %get-tuple-element.64), channel_id=1, source_target_pairs={{0,1},{1,2},{2,3},{3,4},{4,5},{5,6},{6,7},{7,0},{8,9},{9,10},{10,1... | collective-permute-start | bytes 196616 | tf_op jit(solution)/shard_map/ppermute | solution.py:233
  102.9 10.4 %collective-permute-start.14 = (bf16[4,64,128]{2,1,0:T(8,128)(2,1)S(1)}, bf16[4,64,128]{2,1,0:T(8,128)(2,1)S(1)}, u32[]{:S(2)}, u32[]{:S(2)}) collective-permute-start(bf16[4,64,128]{2,1,0:T(8,128)(2,1)S(1)} %get-tuple-element.65), channel_id=1, source_target_pairs={{0,2},{1,3},{2,4},{3,5},{4,6},{5,7},{6,0},{7,1},{8,10},{9,11},{10,... | collective-permute-start | bytes 196616 | tf_op jit(solution)/shard_map/ppermute | solution.py:233
  102.9 10.4 %collective-permute-start.15 = (bf16[4,64,128]{2,1,0:T(8,128)(2,1)S(1)}, bf16[4,64,128]{2,1,0:T(8,128)(2,1)S(1)}, u32[]{:S(2)}, u32[]{:S(2)}) collective-permute-start(bf16[4,64,128]{2,1,0:T(8,128)(2,1)S(1)} %get-tuple-element.66), channel_id=1, source_target_pairs={{0,3},{1,4},{2,5},{3,6},{4,7},{5,0},{6,1},{7,2},{8,11},{9,12},{10,... | collective-permute-start | bytes 196616 | tf_op jit(solution)/shard_map/ppermute | solution.py:233
  105.3 11.1 %collective-permute-start.16 = (bf16[4,64,128]{2,1,0:T(8,128)(2,1)S(1)}, bf16[4,64,128]{2,1,0:T(8,128)(2,1)S(1)}, u32[]{:S(2)}, u32[]{:S(2)}) collective-permute-start(bf16[4,64,128]{2,1,0:T(8,128)(2,1)S(1)} %get-tuple-element.67), channel_id=1, source_target_pairs={{0,4},{1,5},{2,6},{3,7},{4,0},{5,1},{6,2},{7,3},{8,12},{9,13},{10,... | collective-permute-start | bytes 196616 | tf_op jit(solution)/shard_map/ppermute | solution.py:233
  108.3 8.5 %collective-permute-start.17 = (bf16[4,64,128]{2,1,0:T(8,128)(2,1)S(1)}, bf16[4,64,128]{2,1,0:T(8,128)(2,1)S(1)}, u32[]{:S(2)}, u32[]{:S(2)}) collective-permute-start(bf16[4,64,128]{2,1,0:T(8,128)(2,1)S(1)} %get-tuple-element.68), channel_id=1, source_target_pairs={{0,5},{1,6},{2,7},{3,0},{4,1},{5,2},{6,3},{7,4},{8,13},{9,14},{10,... | collective-permute-start | bytes 196616 | tf_op jit(solution)/shard_map/ppermute | solution.py:233
  109.6 10.1 %collective-permute-start.18 = (bf16[4,64,128]{2,1,0:T(8,128)(2,1)S(1)}, bf16[4,64,128]{2,1,0:T(8,128)(2,1)S(1)}, u32[]{:S(2)}, u32[]{:S(2)}) collective-permute-start(bf16[4,64,128]{2,1,0:T(8,128)(2,1)S(1)} %get-tuple-element.69), channel_id=1, source_target_pairs={{0,6},{1,7},{2,0},{3,1},{4,2},{5,3},{6,4},{7,5},{8,14},{9,15},{10,... | collective-permute-start | bytes 196616 | tf_op jit(solution)/shard_map/ppermute | solution.py:233
  131.0 37.7 %all-to-all-start.4 = ((bf16[32,4,64,128]{3,2,1,0:T(8,128)(2,1)}), bf16[32,4,64,128]{3,2,1,0:T(8,128)(2,1)S(1)}, u32[]{:S(2)}, u32[]{:S(2)}) async-start(bf16[32,4,64,128]{3,2,1,0:T(8,128)(2,1)} %bitcast.55), calls=%async_computation.4 | async-start | bytes 4194304 | tf_op jit(solution)/shard_map/all_to_all | solution.py:292
  137.2 11.2 %collective-permute-start.20 = (bf16[16,64,128]{2,1,0:T(8,128)(2,1)}, bf16[16,64,128]{2,1,0:T(8,128)(2,1)S(1)}, u32[]{:S(2)}, u32[]{:S(2)}) collective-permute-start(bf16[16,64,128]{2,1,0:T(8,128)(2,1)} %get-tuple-element.82), channel_id=1, source_target_pairs={{0,2},{1,3},{2,4},{3,5},{4,6},{5,7},{6,0},{7,1},{8,10},{9,11},{10,... | collective-permute-start | bytes 786440 | tf_op jit(solution)/shard_map/ppermute | solution.py:233
  138.1 12.4 %collective-permute-start.21 = (bf16[16,64,128]{2,1,0:T(8,128)(2,1)}, bf16[16,64,128]{2,1,0:T(8,128)(2,1)S(1)}, u32[]{:S(2)}, u32[]{:S(2)}) collective-permute-start(bf16[16,64,128]{2,1,0:T(8,128)(2,1)} %get-tuple-element.83), channel_id=1, source_target_pairs={{0,6},{1,7},{2,0},{3,1},{4,2},{5,3},{6,4},{7,5},{8,14},{9,15},{10,... | collective-permute-start | bytes 786440 | tf_op jit(solution)/shard_map/ppermute | solution.py:233
  140.8 27.1 %collective-permute-start.22 = (bf16[16,64,128]{2,1,0:T(8,128)(2,1)}, bf16[16,64,128]{2,1,0:T(8,128)(2,1)S(1)}, u32[]{:S(2)}, u32[]{:S(2)}) collective-permute-start(bf16[16,64,128]{2,1,0:T(8,128)(2,1)} %get-tuple-element.84), channel_id=1, source_target_pairs={{0,3},{1,4},{2,5},{3,6},{4,7},{5,0},{6,1},{7,2},{8,11},{9,12},{10,... | collective-permute-start | bytes 786440 | tf_op jit(solution)/shard_map/ppermute | solution.py:233
  141.0 27.6 %collective-permute-start.23 = (bf16[16,64,128]{2,1,0:T(8,128)(2,1)}, bf16[16,64,128]{2,1,0:T(8,128)(2,1)S(1)}, u32[]{:S(2)}, u32[]{:S(2)}) collective-permute-start(bf16[16,64,128]{2,1,0:T(8,128)(2,1)} %get-tuple-element.85), channel_id=1, source_target_pairs={{0,5},{1,6},{2,7},{3,0},{4,1},{5,2},{6,3},{7,4},{8,13},{9,14},{10,... | collective-permute-start | bytes 786440 | tf_op jit(solution)/shard_map/ppermute | solution.py:233
  172.7 45.8 %collective-permute-start.24 = (bf16[32,64,128]{2,1,0:T(8,128)(2,1)}, bf16[32,64,128]{2,1,0:T(8,128)(2,1)S(1)}, u32[]{:S(2)}, u32[]{:S(2)}) collective-permute-start(bf16[32,64,128]{2,1,0:T(8,128)(2,1)} %get-tuple-element.90), channel_id=1, source_target_pairs={{0,7},{1,0},{2,1},{3,2},{4,3},{5,4},{6,5},{7,6},{8,15},{9,8},{10,9... | collective-permute-start | bytes 1572872 | tf_op jit(solution)/shard_map/ppermute | solution.py:233
  176.0 23.5 %collective-permute-start.25 = (bf16[16,64,128]{2,1,0:T(8,128)(2,1)}, bf16[16,64,128]{2,1,0:T(8,128)(2,1)S(1)}, u32[]{:S(2)}, u32[]{:S(2)}) collective-permute-start(bf16[16,64,128]{2,1,0:T(8,128)(2,1)} %get-tuple-element.94), channel_id=1, source_target_pairs={{0,6},{1,7},{2,0},{3,1},{4,2},{5,3},{6,4},{7,5},{8,14},{9,15},{10,... | collective-permute-start | bytes 786440 | tf_op jit(solution)/shard_map/ppermute | solution.py:233
  178.9 41.9 %collective-permute-start.27 = (bf16[32,64,128]{2,1,0:T(8,128)(2,1)}, bf16[32,64,128]{2,1,0:T(8,128)(2,1)S(1)}, u32[]{:S(2)}, u32[]{:S(2)}) collective-permute-start(bf16[32,64,128]{2,1,0:T(8,128)(2,1)} %get-tuple-element.97), channel_id=1, source_target_pairs={{0,1},{1,2},{2,3},{3,4},{4,5},{5,6},{6,7},{7,0},{8,9},{9,10},{10,1... | collective-permute-start | bytes 1572872 | tf_op jit(solution)/shard_map/ppermute | solution.py:233
  180.0 38.5 %collective-permute-start.26 = (bf16[16,64,128]{2,1,0:T(8,128)(2,1)}, bf16[16,64,128]{2,1,0:T(8,128)(2,1)S(1)}, u32[]{:S(2)}, u32[]{:S(2)}) collective-permute-start(bf16[16,64,128]{2,1,0:T(8,128)(2,1)} %get-tuple-element.95), channel_id=1, source_target_pairs={{0,5},{1,6},{2,7},{3,0},{4,1},{5,2},{6,3},{7,4},{8,13},{9,14},{10,... | collective-permute-start | bytes 786440 | tf_op jit(solution)/shard_map/ppermute | solution.py:233
  181.0 39.7 %collective-permute-start.28 = (bf16[16,64,128]{2,1,0:T(8,128)(2,1)}, bf16[16,64,128]{2,1,0:T(8,128)(2,1)S(1)}, u32[]{:S(2)}, u32[]{:S(2)}) collective-permute-start(bf16[16,64,128]{2,1,0:T(8,128)(2,1)} %get-tuple-element.101), channel_id=1, source_target_pairs={{0,2},{1,3},{2,4},{3,5},{4,6},{5,7},{6,0},{7,1},{8,10},{9,11},{10,... | collective-permute-start | bytes 786440 | tf_op jit(solution)/shard_map/ppermute | solution.py:233
  199.6 21.2 %collective-permute-start.29 = (bf16[16,64,128]{2,1,0:T(8,128)(2,1)}, bf16[16,64,128]{2,1,0:T(8,128)(2,1)S(1)}, u32[]{:S(2)}, u32[]{:S(2)}) collective-permute-start(bf16[16,64,128]{2,1,0:T(8,128)(2,1)} %get-tuple-element.102), channel_id=1, source_target_pairs={{0,3},{1,4},{2,5},{3,6},{4,7},{5,0},{6,1},{7,2},{8,11},{9,12},{10,... | collective-permute-start | bytes 786440 | tf_op jit(solution)/shard_map/ppermute | solution.py:233
  220.7 12.4 %collective-permute-start.31 = (f32[8,128,128]{2,1,0:T(8,128)}, f32[8,128,128]{2,1,0:T(8,128)}, u32[]{:S(2)}, u32[]{:S(2)}) collective-permute-start(f32[8,128,128]{2,1,0:T(8,128)} %gram.7), channel_id=1, source_target_pairs={{0,7},{1,0},{2,1},{3,2},{4,3},{5,4},{6,5},{7,6},{8,15},{9,8},{10,9... | collective-permute-start | bytes 1572872 | tf_op jit(solution)/shard_map/ppermute | solution.py:233
  223.1 13.1 %collective-permute-start.30 = (f32[8,128,128]{2,1,0:T(8,128)}, f32[8,128,128]{2,1,0:T(8,128)}, u32[]{:S(2)}, u32[]{:S(2)}) collective-permute-start(f32[8,128,128]{2,1,0:T(8,128)} %gram.5), channel_id=1, source_target_pairs={{0,1},{1,2},{2,3},{3,4},{4,5},{5,6},{6,7},{7,0},{8,9},{9,10},{10,1... | collective-permute-start | bytes 1572872 | tf_op jit(solution)/shard_map/ppermute | solution.py:233
  (31 other events, 557.1 us)
Sparse Core Ops, SparseCore 0:
  27.0 51.2 all-gather.1

commit v4 on v3

--- a/solution.py
+++ b/solution.py
@@ -18,11 +18,17 @@
 REACH = 3
 STEP = 256
 PICKS = 4
+EARLY_PIECES = 1
+LATE_PIECES = 1
 NEXT = (1, 2 + REACH)
 ORDER = (3, 7, 2, 6, 1, 5, 0, 4)
 ALL = ("y", "x", "c", "z")
 LAT = ("y", "x", "c")
 MIB = 1 << 20
+
+
+def in_hbm(array):
+    return pltpu.with_memory_space_constraint(array, pltpu.HBM)
 
 
 def activate(preact, bias, thresh):
@@ -70,7 +76,7 @@
         grid_spec=pltpu.PrefetchScalarGridSpec(
             num_scalar_prefetch=1,
             grid=(width // STEP,),
-            in_specs=[pl.BlockSpec(one.shape, lambda i, s: (0, 0)) for one in acts]
+            in_specs=[pl.BlockSpec((one.shape[0], depth), lambda i, s: (0, 0)) for one in acts]
             + [pl.BlockSpec((depth, STEP), lambda i, s: (0, i))]
             + [pl.BlockSpec((1, STEP), lambda i, s: (0, i))] * 2,
             out_specs=specs if isinstance(out_shape, list) else specs[0],
@@ -82,33 +88,42 @@
             flops=2 * TOKENS * depth * width, bytes_accessed=8 * MIB, transcendentals=0
         ),
         name=name,
-    )(scalar, *acts, weight, bias_vec[None], thresh[None])
-
-
-def pick_kernel(index_ref, blocks_ref, out_ref, buf_ref, sems):
-    chunk = out_ref.shape[0] // PICKS
+    )(scalar, *acts, in_hbm(weight), bias_vec[None], thresh[None])
+
+
+def pick_kernel(index_ref, blocks_ref, *refs):
+    outs, (buf_ref, sems) = refs[:-2], refs[-2:]
+    chunk = index_ref.shape[0] // PICKS
+    tokens = outs[0].shape[1]
     copies = []
-    for part in range(PICKS):
-        for i in range(part * chunk, (part + 1) * chunk):
-            buf_ref[i] = blocks_ref[index_ref[i]]
-        at = pl.ds(part * chunk, chunk)
-        copies.append(pltpu.make_async_copy(buf_ref.at[at], out_ref.at[at], sems.at[part]))
-        copies[-1].start()
+    for n, out_ref in enumerate(outs):
+        for part in range(PICKS):
+            for i in range(part * chunk, (part + 1) * chunk):
+                buf_ref[n, i] = blocks_ref[index_ref[i], n * tokens : (n + 1) * tokens, :]
+            at = pl.ds(part * chunk, chunk)
+            copies.append(
+                pltpu.make_async_copy(buf_ref.at[n, at], out_ref.at[at], sems.at[n * PICKS + part])
+            )
+            copies[-1].start()
     for copy in copies:
         copy.wait()
 
 
-def pick(index, blocks):
-    shape = (index.shape[0],) + blocks.shape[1:]
+def pick(index, blocks, pieces):
+    count, (tokens, width) = index.shape[0], blocks.shape[1:]
+    shape = (count, tokens // pieces, width)
     return pl.pallas_call(
         pick_kernel,
         in_specs=[
             pl.BlockSpec(memory_space=pltpu.SMEM),
             pl.BlockSpec(memory_space=pltpu.VMEM),
         ],
-        out_specs=pl.BlockSpec(memory_space=pltpu.HBM),
-        out_shape=pltpu.HBM(shape, blocks.dtype),
-        scratch_shapes=[pltpu.VMEM(shape, blocks.dtype), pltpu.SemaphoreType.DMA((PICKS,))],
+        out_specs=[pl.BlockSpec(memory_space=pltpu.HBM)] * pieces,
+        out_shape=[pltpu.HBM(shape, blocks.dtype)] * pieces,
+        scratch_shapes=[
+            pltpu.VMEM((pieces,) + shape, blocks.dtype),
+            pltpu.SemaphoreType.DMA((pieces * PICKS,)),
+        ],
         compiler_params=pltpu.CompilerParams(vmem_limit_bytes=16 * MIB),
         cost_estimate=pl.CostEstimate(flops=0, bytes_accessed=3 * MIB, transcendentals=0),
         name="pick",
@@ -117,25 +132,30 @@
 
 def route_kernel(extras, slot_ref, at_ref, blocks_ref, *refs):
     extra_refs, refs = refs[:extras], refs[extras:]
-    outs, (buf_ref, sems) = refs[:-2], refs[-2:]
+    count = 2 * (REACH + 1)
+    outs, buf_ref, holds, sems = refs[:count], refs[count], refs[count + 1 : -1], refs[-1]
+    arriving = [
+        pltpu.make_async_copy(extra_ref, holds[m], sems.at[count + m])
+        for m, extra_ref in enumerate(extra_refs)
+    ]
+    for copy in arriving:
+        copy.start()
     copies = []
-    for n, out_ref in enumerate(outs):
-        extra = 2 * HALF if extras and n in NEXT else 0
-        if extra:
-            copies.append(
-                pltpu.make_async_copy(
-                    extra_refs[NEXT.index(n)], out_ref.at[pl.ds(0, extra)], sems.at[len(outs) + NEXT.index(n)]
-                )
-            )
-            copies[-1].start()
     for n in ORDER:
-        extra = 2 * HALF if extras and n in NEXT else 0
         for part in range(2):
             first = slot_ref[2 * n + part]
             for i in range(HALF):
                 buf_ref[n, part * HALF + i] = blocks_ref[at_ref[first + i]]
+        kept = outs[n].shape[0] - 2 * HALF
         copies.append(
-            pltpu.make_async_copy(buf_ref.at[n], outs[n].at[pl.ds(extra, 2 * HALF)], sems.at[n])
+            pltpu.make_async_copy(buf_ref.at[n], outs[n].at[pl.ds(kept, 2 * HALF)], sems.at[n])
+        )
+        copies[-1].start()
+    for m, copy in enumerate(arriving):
+        copy.wait()
+        rows = pl.ds(0, holds[m].shape[0])
+        copies.append(
+            pltpu.make_async_copy(holds[m], outs[NEXT[m]].at[rows], sems.at[count + extras + m])
         )
         copies[-1].start()
     for copy in copies:
@@ -145,6 +165,9 @@
 def route(slot, at, blocks, extras=()):
     count = 2 * (REACH + 1)
     tail = blocks.shape[1:]
+    rows = [2 * HALF] * count
+    for m, extra in enumerate(extras):
+        rows[NEXT[m]] += extra.shape[0]
     return pl.pallas_call(
         functools.partial(route_kernel, len(extras)),
         in_specs=[
@@ -154,45 +177,59 @@
         ]
         + [pl.BlockSpec(memory_space=pl.ANY)] * len(extras),
         out_specs=[pl.BlockSpec(memory_space=pltpu.HBM)] * count,
-        out_shape=[
-            pltpu.HBM((2 * HALF * (2 if extras and n in NEXT else 1),) + tail, blocks.dtype)
-            for n in range(count)
-        ],
+        out_shape=[pltpu.HBM((row,) + tail, blocks.dtype) for row in rows],
         scratch_shapes=[
             pltpu.VMEM((count, 2 * HALF) + tail, blocks.dtype),
-            pltpu.SemaphoreType.DMA((count + 2,)),
+            *(pltpu.VMEM(extra.shape, extra.dtype) for extra in extras),
+            pltpu.SemaphoreType.DMA((count + 2 * len(extras),)),
         ],
         compiler_params=pltpu.CompilerParams(vmem_limit_bytes=16 * MIB),
         cost_estimate=pl.CostEstimate(flops=0, bytes_accessed=4 * MIB, transcendentals=0),
         name="route",
-    )(slot, at, blocks, *extras)
-
-
-def gram_kernel(lows, *refs):
-    out_ref = refs[-1]
-    count = REACH + 1
+    )(slot, at, blocks, *map(in_hbm, extras))
+
+
+def gram_kernel(layout, lefts, *refs):
+    count = len(layout)
+    sources, out_ref, bufs, sems = refs[:count], refs[count], refs[count + 1 : -1], refs[-1]
+    copies = []
+    for n, (low, stride) in enumerate(layout):
+        copies.append(
+            pltpu.make_async_copy(sources[n].at[pl.ds(low, HALF * stride)], bufs[n], sems.at[n])
+        )
+        copies[-1].start()
+    for copy in copies:
+        copy.wait()
     for i in range(HALF):
         left, right = (
-            jnp.concatenate([refs[n][lows[n] + i] for n in range(base, base + count)], axis=0)
-            for base in (0, count)
+            jnp.concatenate(
+                [bufs[n][i * layout[n][1] + j] for n in some for j in range(layout[n][1])], axis=0
+            )
+            for some in (range(lefts), range(lefts, count))
         )
         out_ref[i] = lax.dot_general(
             left, right, (((0,), (0,)), ((), ())), preferred_element_type=jnp.float32
         )
 
 
-def gram(lows, parts):
+def gram(lefts, rights, near):
+    parts = lefts + rights
+    layout = tuple((low + (HALF * stride if near else 0), stride) for _, low, stride in parts)
     return pl.pallas_call(
-        functools.partial(gram_kernel, lows),
-        in_specs=[pl.BlockSpec(memory_space=pltpu.VMEM)] * len(parts),
+        functools.partial(gram_kernel, layout, len(lefts)),
+        in_specs=[pl.BlockSpec(memory_space=pl.ANY)] * len(parts),
         out_specs=pl.BlockSpec(memory_space=pltpu.VMEM),
         out_shape=jax.ShapeDtypeStruct((HALF, BLOCK, BLOCK), jnp.float32),
+        scratch_shapes=[
+            pltpu.VMEM((HALF * stride,) + array.shape[1:], array.dtype) for array, _, stride in parts
+        ]
+        + [pltpu.SemaphoreType.DMA((len(parts),))],
         compiler_params=pltpu.CompilerParams(vmem_limit_bytes=16 * MIB),
         cost_estimate=pl.CostEstimate(
             flops=2 * HALF * 256 * BLOCK * BLOCK, bytes_accessed=2 * MIB, transcendentals=0
         ),
         name="gram",
-    )(*parts)
+    )(*(in_hbm(array) for array, _, _ in parts))
 
 
 def finish_kernel(first_ref, live_ref, low_ref, low_far_ref, high_ref, high_far_ref, out_ref):
@@ -273,12 +310,15 @@
     near = gather_z(jnp.stack([acts_early, acts_late]))
     rows_early = near[:, 0].reshape(-1, depth)
     rows_late = near[:, 1].reshape(-1, depth)
-    all_late = lax.all_gather(rows_late, LAT, axis=0, tiled=True)
-
     position, table = positions(pair_blocks, group_blocks)
-    asked = lax.all_to_all(
-        table.reshape(GROUPS, FROM_GROUP * 2), LAT, split_axis=0, concat_axis=0, tiled=True
-    ).reshape(GROUPS * FROM_GROUP, 2)
+    lists = jnp.zeros((rows_late.shape[0], BLOCK), jnp.bfloat16).at[:2].set(table.T.astype(jnp.bfloat16))
+    all_late = lax.all_gather(
+        jnp.concatenate([rows_late, lists], axis=1), LAT, axis=0, tiled=True
+    )
+    group = (y * SIDE + x) * 2 + c
+    asked = all_late.reshape(GROUPS, -1, depth + BLOCK)[:, :2, depth:]
+    asked = lax.dynamic_slice_in_dim(asked, group * FROM_GROUP, FROM_GROUP, axis=2)
+    asked = jnp.swapaxes(asked, 1, 2).reshape(GROUPS * FROM_GROUP, 2).astype(jnp.int32)
     asked_late = ((z - asked[:, 1] // rank_blocks) & (RANKS - 1)) * rank_blocks + (
         asked[:, 1] % rank_blocks
     )
@@ -324,32 +364,54 @@
         [pltpu.VMEM((TOKENS, STEP), jnp.bfloat16)],
     )
     codes_early, codes_late = lax.optimization_barrier((codes_early, codes_late))
-    sent_early = pick(asked[:, 0], codes_early.reshape((group_blocks,) + shape[1:]))
-    got_early = spread(sent_early)
+    sent_early = pick(asked[:, 0], codes_early.reshape((group_blocks,) + shape[1:]), EARLY_PIECES)
+    sent_early, codes_late = lax.optimization_barrier((sent_early, codes_late))
     codes_late = [codes_late[0]] + [shift(codes_late[k], "z", RANKS, k) for k in range(1, RANKS)]
-    sent_late = pick(asked_late, jnp.concatenate(codes_late))
-    got_early, sent_late = lax.optimization_barrier((got_early, sent_late))
+    sent_late = pick(asked_late, jnp.concatenate(codes_late), LATE_PIECES)
 
     def both(parts, k):
         return parts[k], parts[k + REACH + 1]
 
-    parts = route(slots, position[:, 0], got_early)
-    sent_late, parts = lax.optimization_barrier((sent_late, parts))
-    left = {k: trade(both(parts, k), k) for k in (3, 2)}
-    left, got_late = lax.optimization_barrier((left, spread(sent_late)))
-    left[0] = both(parts, 0)
-
-    parts = route(slots, position[:, 1], got_late, both(parts, 1))
-    right = {k: trade(both(parts, k), k) for k in (3, 2, 1)}
-    right[0] = both(parts, 0)
-    left[1] = right[1]
+    sent = list(sent_early) + list(sent_late)
+    fine = (-1, TOKENS // RANKS // LATE_PIECES, BLOCK)
+    held, extras, traded = [], [], None
+    for n in range(len(sent)):
+        late = n >= EARLY_PIECES
+        got = spread(sent[n])
+        if n == EARLY_PIECES - 1:
+            got, sent[n + 1 :] = lax.optimization_barrier((got, sent[n + 1 :]))
+        if traded is not None:
+            traded, got = lax.optimization_barrier((traded, got))
+            held[-1].update(traded)
+        first_late = n == EARLY_PIECES
+        parts = route(slots, position[:, int(late)], got, extras if first_late else ())
+        if n + 1 < len(sent):
+            sent[n + 1], parts = lax.optimization_barrier((sent[n + 1], parts))
+        traded = {k: trade(both(parts, k), k) for k in (3, 2)}
+        held.append({0: both(parts, 0), **traded})
+        if late:
+            held[-1][1] = trade(both(parts, 1), 1)
+        else:
+            extras += [part.reshape(fine) for part in both(parts, 1)]
+
+    def layer(side, late):
+        out = []
+        for k in range(REACH + 1):
+            at = 0
+            rows = 2 * HALF * (LATE_PIECES if k == 1 and not late else EARLY_PIECES) // EARLY_PIECES
+            for n in range(EARLY_PIECES if not late else LATE_PIECES):
+                if late:
+                    low = 2 * HALF * LATE_PIECES if k == 1 and n == 0 else 0
+                    out.append((held[EARLY_PIECES + n][k][side], low, 1))
+                elif k == 1:
+                    out.append((held[EARLY_PIECES][1][side], at, rows // (2 * HALF)))
+                    at += rows
+                else:
+                    out.append((held[n][k][side], 0, 1))
+        return out
 
     def tiles(side, near):
-        low = HALF if near else 0
-        parts = [left[k][side] for k in range(REACH + 1)] + [right[k][side] for k in range(REACH + 1)]
-        lows = [low] * len(parts)
-        lows[REACH + 2] += 2 * HALF
-        return gram(tuple(lows), parts)
+        return gram(layer(side, False), layer(side, True), near)
 
     low_far = shift(tiles(0, False), "z", RANKS, 1)
     high_far = shift(tiles(1, False), "z", RANKS, -1)

time: 248 us -> 242 us (0.976)
  blocking collectives: 18.6 us -> 0 us
  waiting for transfers between devices: 92.8 us -> 108 us
  local copies, waits for them, and re-layouts: 16.8 us -> 6.34 us
  Pallas kernels: 21.3 us -> 26.2 us
    all_to_all x1 -> x0, blocking collectives: 18.6 us -> none  [gather_z(): return lax.all_to_all(spread, 'z', 0, 0, tiled=True)]
    unnamed x59 -> x43, local copies, waits for them, and re-layouts: 13.9 us -> 4.02 us
    all_to_all x1, waiting for transfers between devices: 0.01 us -> 8.67 us  [gather_z(): return lax.all_to_all(spread, 'z', 0, 0, tiled=True)]
    all_gather x1, waiting for transfers between devices: 1.63 us -> 6.55 us  [shards(): lax.all_gather(jnp.concatenate([rows_late, lists], axis=1), LAT, axis=0,...]
    ppermute x32, waiting for transfers between devices: 77.8 us -> 82.7 us  [shift(): lax.ppermute(value, axis, [(i, (i + by) % size) for i in range(size)])]
    all_to_all x1, starting transfers between devices: 5.22 us -> 9.15 us  [gather_z(): return lax.all_to_all(spread, 'z', 0, 0, tiled=True)]
    pallas_call x4, Pallas kernels: 3.01 us -> 6.8 us  [gram(): pl.pallas_call(functools.partial(gram_kernel, layout, len(lefts)), in_spe...]
    all_to_all x2, starting transfers between devices: 13.7 us -> 10.9 us  [spread(): lax.all_to_all(sent.reshape((GROUPS, FROM_GROUP) + sent.shape[1:]), LAT,...]
  transfers between devices with their start and end apart: 37 -> 37, of which waited for: 18 -> 19; matrix products, arithmetic and copies ran while one was open for 1% -> 1% of each run, Pallas kernels for 5% -> 8%
where the time goes in v4:
time: 242 us; the launch traced here: 238 us
  waiting for transfers between devices  108 us (45%)
  starting transfers between devices  79.9 us (33%)
  Pallas kernels  26.2 us (11%)
  between operations  14.5 us (6%)
  local copies, waits for them, and re-layouts  6.34 us (3%)
  other arithmetic  2.79 us (1%)
    ppermute x32, waiting for transfers between devices, shift(): lax.ppermute(value, axis, [(i, (i + by) % size) for i in range(size)])  82.7 us
    ppermute x32, starting transfers between devices, shift(): lax.ppermute(value, axis, [(i, (i + by) % size) for i in range(size)])  56.1 us
    all_to_all x2, starting transfers between devices, spread(): lax.all_to_all(sent.reshape((GROUPS, FROM_GROUP) + sent.shape[1:]), LAT,...  10.9 us
    pallas_call x2, Pallas kernels, encode(): pl.pallas_call(kernel, grid_spec=pltpu.PrefetchScalarGridSpec(num_scalar_...  9.72 us
    all_to_all x1, starting transfers between devices, gather_z(): return lax.all_to_all(spread, 'z', 0, 0, tiled=True)  9.15 us
    all_to_all x1, waiting for transfers between devices, gather_z(): return lax.all_to_all(spread, 'z', 0, 0, tiled=True)  8.67 us
    pallas_call x4, Pallas kernels, gram(): pl.pallas_call(functools.partial(gram_kernel, layout, len(lefts)), in_spe...  6.8 us
    all_gather x1, waiting for transfers between devices, shards(): lax.all_gather(jnp.concatenate([rows_late, lists], axis=1), LAT, axis=0,...  6.55 us
  transfers between devices with their start and end apart: 37, of which 19 were waited for; matrix products, arithmetic and copies ran while one was open for 1% of the time, Pallas kernels for 8%

profile of v4, /device:TPU:1, one launch (start us, length us, event | category | flops | bytes accessed | tf_op | source)
XLA Modules:
  0.0 237.9 jit_solution(17995036919905475998)
XLA Ops:
  8.1 9.1 %all-to-all-start = ((bf16[8,2,2,3584]{3,2,1,0:T(2,128)(2,1)}), bf16[8,2,2,3584]{3,2,1,0:T(2,128)(2,1)S(1)}, u32[]{:S(2)}, u32[]{:S(2)}) async-start(bf16[8,2,2,3584]{3,2,1,0:T(2,128)(2,1)} %broadcast_in_dim.46), calls=%async_computation | async-start | bytes 458752 | tf_op jit(solution)/shard_map/all_to_all | solution.py:275
  18.3 8.7 %all-to-all-done = bf16[8,2,2,3584]{3,2,1,0:T(2,128)(2,1)S(1)} async-done(((bf16[8,2,2,3584]{3,2,1,0:T(2,128)(2,1)}), bf16[8,2,2,3584]{3,2,1,0:T(2,128)(2,1)S(1)}, u32[]{:S(2)}, u32[]{:S(2)}) %all-to-all-start) | async-done | bytes 229408 | tf_op jit(solution)/shard_map/all_to_all | solution.py:275
  28.0 2.6 %collective-permute-start.2 = (bf16[16,1792]{1,0:T(8,128)(2,1)S(1)}, bf16[16,1792]{1,0:T(8,128)(2,1)S(1)}, u32[]{:S(2)}, u32[]{:S(2)}) collective-permute-start(bf16[16,1792]{1,0:T(8,128)(2,1)S(1)} %get-tuple-element.142), channel_id=1, source_target_pairs={{0,48},{16,0},{32,16},{48,32},{1,49},{17,1},{33,17},{49,33},{2,50}... | collective-permute-start | bytes 172040 | tf_op jit(solution)/shard_map/ppermute | solution.py:270
  33.6 2.6 %collective-permute-start.7 = (bf16[16,1792]{1,0:T(8,128)(2,1)S(1)}, bf16[16,1792]{1,0:T(8,128)(2,1)S(1)}, u32[]{:S(2)}, u32[]{:S(2)}) collective-permute-start(bf16[16,1792]{1,0:T(8,128)(2,1)S(1)} %get-tuple-element.141), channel_id=1, source_target_pairs={{0,128},{64,192},{128,0},{192,64},{1,129},{65,193},{129,1},{193,65... | collective-permute-start | bytes 172040 | tf_op jit(solution)/shard_map/ppermute | solution.py:270
  45.1 5.4 %collective-permute-done.4 = bf16[4,16,1792]{2,1,0:T(8,128)(2,1)S(1)} collective-permute-done((bf16[4,16,1792]{2,1,0:T(8,128)(2,1)S(1)}, bf16[4,16,1792]{2,1,0:T(8,128)(2,1)S(1)}, u32[]{:S(2)}, u32[]{:S(2)}) %collective-permute-start.4) | collective-permute-done | bytes 229408 | tf_op jit(solution)/shard_map/ppermute | solution.py:270
  52.0 2.5 %collective-permute-done.11 = bf16[4,16,1792]{2,1,0:T(8,128)(2,1)S(1)} collective-permute-done((bf16[4,16,1792]{2,1,0:T(8,128)(2,1)S(1)}, bf16[4,16,1792]{2,1,0:T(8,128)(2,1)S(1)}, u32[]{:S(2)}, u32[]{:S(2)}) %collective-permute-start.11) | collective-permute-done | bytes 229408 | tf_op jit(solution)/shard_map/ppermute | solution.py:270
  54.7 6.0 %collective-permute-start.12 = (bf16[256,3584]{1,0:T(8,128)(2,1)S(1)}, bf16[256,3584]{1,0:T(8,128)(2,1)}, u32[]{:S(2)}, u32[]{:S(2)}) collective-permute-start(bf16[256,3584]{1,0:T(8,128)(2,1)S(1)} %bitcast.68), channel_id=1, source_target_pairs={{0,8},{8,0},{1,9},{9,1},{2,10},{10,2},{3,11},{11,3},{4,12},{12,4},... | collective-permute-start | bytes 5505032 | tf_op jit(solution)/shard_map/ppermute | solution.py:270
  61.0 3.3 %collective-permute-done.12.other_ref = bf16[256,3584]{1,0:T(8,128)(2,1)} collective-permute-done((bf16[256,3584]{1,0:T(8,128)(2,1)S(1)}, bf16[256,3584]{1,0:T(8,128)(2,1)}, u32[]{:S(2)}, u32[]{:S(2)}) %collective-permute-start.12) | collective-permute-done | bytes 1835040 | tf_op jit(solution)/shard_map/ppermute | solution.py:270
  64.3 5.9 %encode_early.1 = bf16[8,4,64,128]{3,2,1,0:T(8,128)(2,1)} custom-call(s32[32]{0:T(128)S(1)} %reshape.181.place_ref, bf16[256,3584]{1,0:T(8,128)(2,1)S(1)} %bitcast.69, bf16[256,3584]{1,0:T(8,128)(2,1)} %collective-permute-done.12.other_ref, bf16[3584,512]{1,0:T(8,128)(2,1)} %w_ref.2, f32[1,512]{1,0:T(1,128)S(1)} %bitcast.72, f32[1,512]{1,0:T(1,128)S(1)} %bitcast.73), custom_call_target="tpu_custom_call" | custom-call | flops 1879048192 | bytes 8388608 | tf_op jit(solution)/shard_map/encode_early/pallas_call | solution.py:74
  70.2 3.7 %all-to-all-start.1 = ((bf16[8,4,64,128]{3,2,1,0:T(8,128)(2,1)}), bf16[8,4,64,128]{3,2,1,0:T(8,128)(2,1)S(1)}, u32[]{:S(2)}, u32[]{:S(2)}) async-start(bf16[8,4,64,128]{3,2,1,0:T(8,128)(2,1)} %encode_early.1), calls=%async_computation.1 | async-start | bytes 1048576 | tf_op jit(solution)/shard_map/all_to_all | solution.py:360
  73.9 6.5 %all-gather.2.cloned.1.call-done.acts_ref = bf16[512,3712]{1,0:T(8,128)(2,1)} async-done(((bf16[16,3712]{1,0:T(8,128)(2,1)}), bf16[512,3712]{1,0:T(8,128)(2,1)}) %all-gather.2.cloned.1.call-update) | async-done | bytes 3801104 | tf_op jit(solution)/shard_map/all_gather | solution.py:315
  82.5 3.9 %encode_late.1 = (bf16[4,64,128]{2,1,0:T(8,128)(2,1)S(1)}, bf16[4,64,128]{2,1,0:T(8,128)(2,1)S(1)}, bf16[4,64,128]{2,1,0:T(8,128)(2,1)S(1)}, bf16[4,64,128]{2,1,...) custom-call(s32[1]{0:T(128)} %bitcast.29.plane_ref, ...), custom_call_target="tpu_custom_call" | custom-call | flops 1879048192 | bytes 8388608 | tf_op jit(solution)/shard_map/encode_late/pallas_call | solution.py:74
  86.4 3.9 %all-to-all-done.1 = bf16[8,4,64,128]{3,2,1,0:T(8,128)(2,1)S(1)} async-done(((bf16[8,4,64,128]{3,2,1,0:T(8,128)(2,1)}), bf16[8,4,64,128]{3,2,1,0:T(8,128)(2,1)S(1)}, u32[]{:S(2)}, u32[]{:S(2)}) %all-to-all-start.1) | async-done | bytes 524320 | tf_op jit(solution)/shard_map/all_to_all | solution.py:360
  93.3 4.7 %all-to-all-start.2 = ((bf16[32,4,64,128]{3,2,1,0:T(8,128)(2,1)}), bf16[32,4,64,128]{3,2,1,0:T(8,128)(2,1)S(1)}, u32[]{:S(2)}, u32[]{:S(2)}) async-start(bf16[32,4,64,128]{3,2,1,0:T(8,128)(2,1)} %bitcast.76), calls=%async_computation.2 | async-start | bytes 4194304 | tf_op jit(solution)/shard_map/all_to_all | solution.py:332
  101.6 3.1 %collective-permute-start.16 = (bf16[4,64,128]{2,1,0:T(8,128)(2,1)S(1)}, bf16[4,64,128]{2,1,0:T(8,128)(2,1)S(1)}, u32[]{:S(2)}, u32[]{:S(2)}) collective-permute-start(bf16[4,64,128]{2,1,0:T(8,128)(2,1)S(1)} %get-tuple-element.97), channel_id=1, source_target_pairs={{0,4},{1,5},{2,6},{3,7},{4,0},{5,1},{6,2},{7,3},{8,12},{9,13},{10,... | collective-permute-start | bytes 196616 | tf_op jit(solution)/shard_map/ppermute | solution.py:270
  105.9 2.9 %collective-permute-start.18 = (bf16[4,64,128]{2,1,0:T(8,128)(2,1)S(1)}, bf16[4,64,128]{2,1,0:T(8,128)(2,1)S(1)}, u32[]{:S(2)}, u32[]{:S(2)}) collective-permute-start(bf16[4,64,128]{2,1,0:T(8,128)(2,1)S(1)} %get-tuple-element.99), channel_id=1, source_target_pairs={{0,6},{1,7},{2,0},{3,1},{4,2},{5,3},{6,4},{7,5},{8,14},{9,15},{10,... | collective-permute-start | bytes 196616 | tf_op jit(solution)/shard_map/ppermute | solution.py:270
  110.1 2.8 %collective-permute-done.16 = bf16[4,64,128]{2,1,0:T(8,128)(2,1)S(1)} collective-permute-done((bf16[4,64,128]{2,1,0:T(8,128)(2,1)S(1)}, bf16[4,64,128]{2,1,0:T(8,128)(2,1)S(1)}, u32[]{:S(2)}, u32[]{:S(2)}) %collective-permute-start.16) | collective-permute-done | bytes 65568 | tf_op jit(solution)/shard_map/ppermute | solution.py:270
  113.0 4.5 %collective-permute-done.18 = bf16[4,64,128]{2,1,0:T(8,128)(2,1)S(1)} collective-permute-done((bf16[4,64,128]{2,1,0:T(8,128)(2,1)S(1)}, bf16[4,64,128]{2,1,0:T(8,128)(2,1)S(1)}, u32[]{:S(2)}, u32[]{:S(2)}) %collective-permute-start.18) | collective-permute-done | bytes 65568 | tf_op jit(solution)/shard_map/ppermute | solution.py:270
  119.5 6.4 %all-to-all-done.2 = bf16[32,4,64,128]{3,2,1,0:T(8,128)(2,1)S(1)} async-done(((bf16[32,4,64,128]{3,2,1,0:T(8,128)(2,1)}), bf16[32,4,64,128]{3,2,1,0:T(8,128)(2,1)S(1)}, u32[]{:S(2)}, u32[]{:S(2)}) %all-to-all-start.2) | async-done | bytes 2097184 | tf_op jit(solution)/shard_map/all_to_all | solution.py:332
  127.9 6.2 %all-to-all-start.3 = ((bf16[32,4,64,128]{3,2,1,0:T(8,128)(2,1)}), bf16[32,4,64,128]{3,2,1,0:T(8,128)(2,1)S(1)}, u32[]{:S(2)}, u32[]{:S(2)}) async-start(bf16[32,4,64,128]{3,2,1,0:T(8,128)(2,1)} %bitcast.77), calls=%async_computation.3 | async-start | bytes 4194304 | tf_op jit(solution)/shard_map/all_to_all | solution.py:332
  134.6 3.2 %collective-permute-start.21 = (bf16[16,64,128]{2,1,0:T(8,128)(2,1)}, bf16[16,64,128]{2,1,0:T(8,128)(2,1)S(1)}, u32[]{:S(2)}, u32[]{:S(2)}) collective-permute-start(bf16[16,64,128]{2,1,0:T(8,128)(2,1)} %get-tuple-element.113), channel_id=1, source_target_pairs={{0,6},{1,7},{2,0},{3,1},{4,2},{5,3},{6,4},{7,5},{8,14},{9,15},{10,... | collective-permute-start | bytes 786440 | tf_op jit(solution)/shard_map/ppermute | solution.py:270
  137.7 4.5 %collective-permute-start.23 = (bf16[16,64,128]{2,1,0:T(8,128)(2,1)S(1)}, bf16[16,64,128]{2,1,0:T(8,128)(2,1)S(1)}, u32[]{:S(2)}, u32[]{:S(2)}) collective-permute-start(bf16[16,64,128]{2,1,0:T(8,128)(2,1)S(1)} %copy-done.17), channel_id=1, source_target_pairs={{0,5},{1,6},{2,7},{3,0},{4,1},{5,2},{6,3},{7,4},{8,13},{9,14},{10,... | collective-permute-start | bytes 786440 | tf_op jit(solution)/shard_map/ppermute | solution.py:270
  142.2 3.2 %collective-permute-done.20.refs_2_ = bf16[16,64,128]{2,1,0:T(8,128)(2,1)S(1)} collective-permute-done((bf16[16,64,128]{2,1,0:T(8,128)(2,1)}, bf16[16,64,128]{2,1,0:T(8,128)(2,1)S(1)}, u32[]{:S(2)}, u32[]{:S(2)}) %collective-permute-start.20) | collective-permute-done | bytes 262176 | tf_op jit(solution)/shard_map/ppermute | solution.py:270
  145.4 5.5 %collective-permute-done.21.refs_2_ = bf16[16,64,128]{2,1,0:T(8,128)(2,1)S(1)} collective-permute-done((bf16[16,64,128]{2,1,0:T(8,128)(2,1)}, bf16[16,64,128]{2,1,0:T(8,128)(2,1)S(1)}, u32[]{:S(2)}, u32[]{:S(2)}) %collective-permute-start.21) | collective-permute-done | bytes 262176 | tf_op jit(solution)/shard_map/ppermute | solution.py:270
  150.9 13.4 %collective-permute-done.22.refs_3_ = bf16[16,64,128]{2,1,0:T(8,128)(2,1)S(1)} collective-permute-done((bf16[16,64,128]{2,1,0:T(8,128)(2,1)}, bf16[16,64,128]{2,1,0:T(8,128)(2,1)S(1)}, u32[]{:S(2)}, u32[]{:S(2)}) %collective-permute-start.22) | collective-permute-done | bytes 262176 | tf_op jit(solution)/shard_map/ppermute | solution.py:270
  164.2 2.7 %route.3 = (bf16[16,64,128]{2,1,0:T(8,128)(2,1)}, bf16[32,64,128]{2,1,0:T(8,128)(2,1)}, bf16[16,64,128]{2,1,0:T(8,128)(2,1)}, bf16[16,64,128]{2,1,0:T(8,128)(2,1...) custom-call(s32[16]{0:T(128)S(1)} %multiply_add_fusion.1.slot_ref, ...), custom_call_target="tpu_custom_call" | custom-call | bytes 4194304 | tf_op jit(solution)/shard_map/route/pallas_call | solution.py:171
  167.0 3.8 %collective-permute-start.24 = (bf16[32,64,128]{2,1,0:T(8,128)(2,1)}, bf16[32,64,128]{2,1,0:T(8,128)(2,1)S(1)}, u32[]{:S(2)}, u32[]{:S(2)}) collective-permute-start(bf16[32,64,128]{2,1,0:T(8,128)(2,1)} %get-tuple-element.120), channel_id=1, source_target_pairs={{0,7},{1,0},{2,1},{3,2},{4,3},{5,4},{6,5},{7,6},{8,15},{9,8},{10,9... | collective-permute-start | bytes 1572872 | tf_op jit(solution)/shard_map/ppermute | solution.py:270
  177.9 20.4 %collective-permute-done.25.refs_6_ = bf16[16,64,128]{2,1,0:T(8,128)(2,1)S(1)} collective-permute-done((bf16[16,64,128]{2,1,0:T(8,128)(2,1)}, bf16[16,64,128]{2,1,0:T(8,128)(2,1)S(1)}, u32[]{:S(2)}, u32[]{:S(2)}) %collective-permute-start.25) | collective-permute-done | bytes 262176 | tf_op jit(solution)/shard_map/ppermute | solution.py:270
  198.3 14.5 %collective-permute-done.26.refs_7_ = bf16[16,64,128]{2,1,0:T(8,128)(2,1)S(1)} collective-permute-done((bf16[16,64,128]{2,1,0:T(8,128)(2,1)}, bf16[16,64,128]{2,1,0:T(8,128)(2,1)S(1)}, u32[]{:S(2)}, u32[]{:S(2)}) %collective-permute-start.26) | collective-permute-done | bytes 262176 | tf_op jit(solution)/shard_map/ppermute | solution.py:270
  218.1 2.5 %collective-permute-start.30 = (f32[8,128,128]{2,1,0:T(8,128)S(1)}, f32[8,128,128]{2,1,0:T(8,128)S(1)}, u32[]{:S(2)}, u32[]{:S(2)}) collective-permute-start(f32[8,128,128]{2,1,0:T(8,128)S(1)} %gram.5), channel_id=1, source_target_pairs={{0,1},{1,2},{2,3},{3,4},{4,5},{5,6},{6,7},{7,0},{8,9},{9,10},{10,1... | collective-permute-start | bytes 1572872 | tf_op jit(solution)/shard_map/ppermute | solution.py:270
  224.7 2.7 %collective-permute-done.31.high_far_ref = f32[8,128,128]{2,1,0:T(8,128)S(1)} collective-permute-done((f32[8,128,128]{2,1,0:T(8,128)S(1)}, f32[8,128,128]{2,1,0:T(8,128)S(1)}, u32[]{:S(2)}, u32[]{:S(2)}) %collective-permute-start.31) | collective-permute-done | bytes 524320 | tf_op jit(solution)/shard_map/ppermute | solution.py:270
  227.4 2.6 %collective-permute-done.30.low_far_ref = f32[8,128,128]{2,1,0:T(8,128)S(1)} collective-permute-done((f32[8,128,128]{2,1,0:T(8,128)S(1)}, f32[8,128,128]{2,1,0:T(8,128)S(1)}, u32[]{:S(2)}, u32[]{:S(2)}) %collective-permute-start.30) | collective-permute-done | bytes 524320 | tf_op jit(solution)/shard_map/ppermute | solution.py:270
  (126 shorter events, 49.9 us)
Async XLA Ops:
  8.1 18.9 %all-to-all-start = ((bf16[8,2,2,3584]{3,2,1,0:T(2,128)(2,1)}), bf16[8,2,2,3584]{3,2,1,0:T(2,128)(2,1)S(1)}, u32[]{:S(2)}, u32[]{:S(2)}) async-start(bf16[8,2,2,3584]{3,2,1,0:T(2,128)(2,1)} %broadcast_in_dim.46), calls=%async_computation | async-start | bytes 458752 | tf_op jit(solution)/shard_map/all_to_all | solution.py:275
  17.3 63.2 %all-gather.2.cloned.1.call-start = ((), (), s32[]{:S(2)}) async-start(), calls=%async_computation.4 | async-start | bytes 3919872 | tf_op jit(solution)/shard_map/all_gather | solution.py:315
  28.0 8.2 %collective-permute-start.2 = (bf16[16,1792]{1,0:T(8,128)(2,1)S(1)}, bf16[16,1792]{1,0:T(8,128)(2,1)S(1)}, u32[]{:S(2)}, u32[]{:S(2)}) collective-permute-start(bf16[16,1792]{1,0:T(8,128)(2,1)S(1)} %get-tuple-element.142), channel_id=1, source_target_pairs={{0,48},{16,0},{32,16},{48,32},{1,49},{17,1},{33,17},{49,33},{2,50}... | collective-permute-start | bytes 172040 | tf_op jit(solution)/shard_map/ppermute | solution.py:270
  37.3 7.4 %collective-permute-start.3 = (bf16[4,16,1792]{2,1,0:T(8,128)(2,1)S(1)}, bf16[4,16,1792]{2,1,0:T(8,128)(2,1)S(1)}, u32[]{:S(2)}, u32[]{:S(2)}) collective-permute-start(bf16[4,16,1792]{2,1,0:T(8,128)(2,1)S(1)} %get-tuple-element.134), channel_id=1, source_target_pairs={{0,64},{64,128},{128,192},{192,0},{1,65},{65,129},{129,193},{193,1... | collective-permute-start | bytes 688136 | tf_op jit(solution)/shard_map/ppermute | solution.py:270
  37.8 12.7 %collective-permute-start.4 = (bf16[4,16,1792]{2,1,0:T(8,128)(2,1)S(1)}, bf16[4,16,1792]{2,1,0:T(8,128)(2,1)S(1)}, u32[]{:S(2)}, u32[]{:S(2)}) collective-permute-start(bf16[4,16,1792]{2,1,0:T(8,128)(2,1)S(1)} %get-tuple-element.134), channel_id=1, source_target_pairs={{0,128},{64,192},{128,0},{192,64},{1,129},{65,193},{129,1},{193,65... | collective-permute-start | bytes 688136 | tf_op jit(solution)/shard_map/ppermute | solution.py:270
  39.5 11.7 %collective-permute-start.5 = (bf16[4,16,1792]{2,1,0:T(8,128)(2,1)S(1)}, bf16[4,16,1792]{2,1,0:T(8,128)(2,1)S(1)}, u32[]{:S(2)}, u32[]{:S(2)}) collective-permute-start(bf16[4,16,1792]{2,1,0:T(8,128)(2,1)S(1)} %get-tuple-element.134), channel_id=1, source_target_pairs={{0,192},{64,0},{128,64},{192,128},{1,193},{65,1},{129,65},{193,129... | collective-permute-start | bytes 688136 | tf_op jit(solution)/shard_map/ppermute | solution.py:270
  40.6 10.6 %collective-permute-start.9 = (bf16[4,16,1792]{2,1,0:T(8,128)(2,1)S(1)}, bf16[4,16,1792]{2,1,0:T(8,128)(2,1)S(1)}, u32[]{:S(2)}, u32[]{:S(2)}) collective-permute-start(bf16[4,16,1792]{2,1,0:T(8,128)(2,1)S(1)} %get-tuple-element.136), channel_id=1, source_target_pairs={{0,16},{16,32},{32,48},{48,0},{1,17},{17,33},{33,49},{49,1},{2,18}... | collective-permute-start | bytes 688136 | tf_op jit(solution)/shard_map/ppermute | solution.py:270
  42.0 10.1 %collective-permute-start.10 = (bf16[4,16,1792]{2,1,0:T(8,128)(2,1)S(1)}, bf16[4,16,1792]{2,1,0:T(8,128)(2,1)S(1)}, u32[]{:S(2)}, u32[]{:S(2)}) collective-permute-start(bf16[4,16,1792]{2,1,0:T(8,128)(2,1)S(1)} %get-tuple-element.136), channel_id=1, source_target_pairs={{0,32},{16,48},{32,0},{48,16},{1,33},{17,49},{33,1},{49,17},{2,34}... | collective-permute-start | bytes 688136 | tf_op jit(solution)/shard_map/ppermute | solution.py:270
  44.8 9.8 %collective-permute-start.11 = (bf16[4,16,1792]{2,1,0:T(8,128)(2,1)S(1)}, bf16[4,16,1792]{2,1,0:T(8,128)(2,1)S(1)}, u32[]{:S(2)}, u32[]{:S(2)}) collective-permute-start(bf16[4,16,1792]{2,1,0:T(8,128)(2,1)S(1)} %get-tuple-element.136), channel_id=1, source_target_pairs={{0,48},{16,0},{32,16},{48,32},{1,49},{17,1},{33,17},{49,33},{2,50}... | collective-permute-start | bytes 688136 | tf_op jit(solution)/shard_map/ppermute | solution.py:270
  54.7 9.6 %collective-permute-start.12 = (bf16[256,3584]{1,0:T(8,128)(2,1)S(1)}, bf16[256,3584]{1,0:T(8,128)(2,1)}, u32[]{:S(2)}, u32[]{:S(2)}) collective-permute-start(bf16[256,3584]{1,0:T(8,128)(2,1)S(1)} %bitcast.68), channel_id=1, source_target_pairs={{0,8},{8,0},{1,9},{9,1},{2,10},{10,2},{3,11},{11,3},{4,12},{12,4},... | collective-permute-start | bytes 5505032 | tf_op jit(solution)/shard_map/ppermute | solution.py:270
  70.2 20.1 %all-to-all-start.1 = ((bf16[8,4,64,128]{3,2,1,0:T(8,128)(2,1)}), bf16[8,4,64,128]{3,2,1,0:T(8,128)(2,1)S(1)}, u32[]{:S(2)}, u32[]{:S(2)}) async-start(bf16[8,4,64,128]{3,2,1,0:T(8,128)(2,1)} %encode_early.1), calls=%async_computation.1 | async-start | bytes 1048576 | tf_op jit(solution)/shard_map/all_to_all | solution.py:360
  93.3 32.6 %all-to-all-start.2 = ((bf16[32,4,64,128]{3,2,1,0:T(8,128)(2,1)}), bf16[32,4,64,128]{3,2,1,0:T(8,128)(2,1)S(1)}, u32[]{:S(2)}, u32[]{:S(2)}) async-start(bf16[32,4,64,128]{3,2,1,0:T(8,128)(2,1)} %bitcast.76), calls=%async_computation.2 | async-start | bytes 4194304 | tf_op jit(solution)/shard_map/all_to_all | solution.py:332
  98.1 7.8 %collective-permute-start.13 = (bf16[4,64,128]{2,1,0:T(8,128)(2,1)S(1)}, bf16[4,64,128]{2,1,0:T(8,128)(2,1)S(1)}, u32[]{:S(2)}, u32[]{:S(2)}) collective-permute-start(bf16[4,64,128]{2,1,0:T(8,128)(2,1)S(1)} %get-tuple-element.94), channel_id=1, source_target_pairs={{0,1},{1,2},{2,3},{3,4},{4,5},{5,6},{6,7},{7,0},{8,9},{9,10},{10,1... | collective-permute-start | bytes 196616 | tf_op jit(solution)/shard_map/ppermute | solution.py:270
  99.2 9.7 %collective-permute-start.14 = (bf16[4,64,128]{2,1,0:T(8,128)(2,1)S(1)}, bf16[4,64,128]{2,1,0:T(8,128)(2,1)S(1)}, u32[]{:S(2)}, u32[]{:S(2)}) collective-permute-start(bf16[4,64,128]{2,1,0:T(8,128)(2,1)S(1)} %get-tuple-element.95), channel_id=1, source_target_pairs={{0,2},{1,3},{2,4},{3,5},{4,6},{5,7},{6,0},{7,1},{8,10},{9,11},{10,... | collective-permute-start | bytes 196616 | tf_op jit(solution)/shard_map/ppermute | solution.py:270
  99.2 10.9 %collective-permute-start.15 = (bf16[4,64,128]{2,1,0:T(8,128)(2,1)S(1)}, bf16[4,64,128]{2,1,0:T(8,128)(2,1)S(1)}, u32[]{:S(2)}, u32[]{:S(2)}) collective-permute-start(bf16[4,64,128]{2,1,0:T(8,128)(2,1)S(1)} %get-tuple-element.96), channel_id=1, source_target_pairs={{0,3},{1,4},{2,5},{3,6},{4,7},{5,0},{6,1},{7,2},{8,11},{9,12},{10,... | collective-permute-start | bytes 196616 | tf_op jit(solution)/shard_map/ppermute | solution.py:270
  101.6 11.3 %collective-permute-start.16 = (bf16[4,64,128]{2,1,0:T(8,128)(2,1)S(1)}, bf16[4,64,128]{2,1,0:T(8,128)(2,1)S(1)}, u32[]{:S(2)}, u32[]{:S(2)}) collective-permute-start(bf16[4,64,128]{2,1,0:T(8,128)(2,1)S(1)} %get-tuple-element.97), channel_id=1, source_target_pairs={{0,4},{1,5},{2,6},{3,7},{4,0},{5,1},{6,2},{7,3},{8,12},{9,13},{10,... | collective-permute-start | bytes 196616 | tf_op jit(solution)/shard_map/ppermute | solution.py:270
  104.7 8.3 %collective-permute-start.17 = (bf16[4,64,128]{2,1,0:T(8,128)(2,1)S(1)}, bf16[4,64,128]{2,1,0:T(8,128)(2,1)S(1)}, u32[]{:S(2)}, u32[]{:S(2)}) collective-permute-start(bf16[4,64,128]{2,1,0:T(8,128)(2,1)S(1)} %get-tuple-element.98), channel_id=1, source_target_pairs={{0,5},{1,6},{2,7},{3,0},{4,1},{5,2},{6,3},{7,4},{8,13},{9,14},{10,... | collective-permute-start | bytes 196616 | tf_op jit(solution)/shard_map/ppermute | solution.py:270
  105.9 11.5 %collective-permute-start.18 = (bf16[4,64,128]{2,1,0:T(8,128)(2,1)S(1)}, bf16[4,64,128]{2,1,0:T(8,128)(2,1)S(1)}, u32[]{:S(2)}, u32[]{:S(2)}) collective-permute-start(bf16[4,64,128]{2,1,0:T(8,128)(2,1)S(1)} %get-tuple-element.99), channel_id=1, source_target_pairs={{0,6},{1,7},{2,0},{3,1},{4,2},{5,3},{6,4},{7,5},{8,14},{9,15},{10,... | collective-permute-start | bytes 196616 | tf_op jit(solution)/shard_map/ppermute | solution.py:270
  108.9 8.6 %collective-permute-start.19 = (bf16[4,64,128]{2,1,0:T(8,128)(2,1)S(1)}, bf16[4,64,128]{2,1,0:T(8,128)(2,1)S(1)}, u32[]{:S(2)}, u32[]{:S(2)}) collective-permute-start(bf16[4,64,128]{2,1,0:T(8,128)(2,1)S(1)} %get-tuple-element.100), channel_id=1, source_target_pairs={{0,7},{1,0},{2,1},{3,2},{4,3},{5,4},{6,5},{7,6},{8,15},{9,8},{10,9... | collective-permute-start | bytes 196616 | tf_op jit(solution)/shard_map/ppermute | solution.py:270
  127.9 36.4 %all-to-all-start.3 = ((bf16[32,4,64,128]{3,2,1,0:T(8,128)(2,1)}), bf16[32,4,64,128]{3,2,1,0:T(8,128)(2,1)S(1)}, u32[]{:S(2)}, u32[]{:S(2)}) async-start(bf16[32,4,64,128]{3,2,1,0:T(8,128)(2,1)} %bitcast.77), calls=%async_computation.3 | async-start | bytes 4194304 | tf_op jit(solution)/shard_map/all_to_all | solution.py:332
  134.1 11.3 %collective-permute-start.20 = (bf16[16,64,128]{2,1,0:T(8,128)(2,1)}, bf16[16,64,128]{2,1,0:T(8,128)(2,1)S(1)}, u32[]{:S(2)}, u32[]{:S(2)}) collective-permute-start(bf16[16,64,128]{2,1,0:T(8,128)(2,1)} %get-tuple-element.112), channel_id=1, source_target_pairs={{0,2},{1,3},{2,4},{3,5},{4,6},{5,7},{6,0},{7,1},{8,10},{9,11},{10,... | collective-permute-start | bytes 786440 | tf_op jit(solution)/shard_map/ppermute | solution.py:270
  134.6 16.3 %collective-permute-start.21 = (bf16[16,64,128]{2,1,0:T(8,128)(2,1)}, bf16[16,64,128]{2,1,0:T(8,128)(2,1)S(1)}, u32[]{:S(2)}, u32[]{:S(2)}) collective-permute-start(bf16[16,64,128]{2,1,0:T(8,128)(2,1)} %get-tuple-element.113), channel_id=1, source_target_pairs={{0,6},{1,7},{2,0},{3,1},{4,2},{5,3},{6,4},{7,5},{8,14},{9,15},{10,... | collective-permute-start | bytes 786440 | tf_op jit(solution)/shard_map/ppermute | solution.py:270
  137.7 26.5 %collective-permute-start.22 = (bf16[16,64,128]{2,1,0:T(8,128)(2,1)}, bf16[16,64,128]{2,1,0:T(8,128)(2,1)S(1)}, u32[]{:S(2)}, u32[]{:S(2)}) collective-permute-start(bf16[16,64,128]{2,1,0:T(8,128)(2,1)} %get-tuple-element.114), channel_id=1, source_target_pairs={{0,3},{1,4},{2,5},{3,6},{4,7},{5,0},{6,1},{7,2},{8,11},{9,12},{10,... | collective-permute-start | bytes 786440 | tf_op jit(solution)/shard_map/ppermute | solution.py:270
  137.7 26.5 %collective-permute-start.23 = (bf16[16,64,128]{2,1,0:T(8,128)(2,1)S(1)}, bf16[16,64,128]{2,1,0:T(8,128)(2,1)S(1)}, u32[]{:S(2)}, u32[]{:S(2)}) collective-permute-start(bf16[16,64,128]{2,1,0:T(8,128)(2,1)S(1)} %copy-done.17), channel_id=1, source_target_pairs={{0,5},{1,6},{2,7},{3,0},{4,1},{5,2},{6,3},{7,4},{8,13},{9,14},{10,... | collective-permute-start | bytes 786440 | tf_op jit(solution)/shard_map/ppermute | solution.py:270
  167.0 45.8 %collective-permute-start.24 = (bf16[32,64,128]{2,1,0:T(8,128)(2,1)}, bf16[32,64,128]{2,1,0:T(8,128)(2,1)S(1)}, u32[]{:S(2)}, u32[]{:S(2)}) collective-permute-start(bf16[32,64,128]{2,1,0:T(8,128)(2,1)} %get-tuple-element.120), channel_id=1, source_target_pairs={{0,7},{1,0},{2,1},{3,2},{4,3},{5,4},{6,5},{7,6},{8,15},{9,8},{10,9... | collective-permute-start | bytes 1572872 | tf_op jit(solution)/shard_map/ppermute | solution.py:270
  170.8 27.5 %collective-permute-start.25 = (bf16[16,64,128]{2,1,0:T(8,128)(2,1)}, bf16[16,64,128]{2,1,0:T(8,128)(2,1)S(1)}, u32[]{:S(2)}, u32[]{:S(2)}) collective-permute-start(bf16[16,64,128]{2,1,0:T(8,128)(2,1)} %get-tuple-element.124), channel_id=1, source_target_pairs={{0,6},{1,7},{2,0},{3,1},{4,2},{5,3},{6,4},{7,5},{8,14},{9,15},{10,... | collective-permute-start | bytes 786440 | tf_op jit(solution)/shard_map/ppermute | solution.py:270
  173.2 42.4 %collective-permute-start.27 = (bf16[32,64,128]{2,1,0:T(8,128)(2,1)}, bf16[32,64,128]{2,1,0:T(8,128)(2,1)S(1)}, u32[]{:S(2)}, u32[]{:S(2)}) collective-permute-start(bf16[32,64,128]{2,1,0:T(8,128)(2,1)} %get-tuple-element.127), channel_id=1, source_target_pairs={{0,1},{1,2},{2,3},{3,4},{4,5},{5,6},{6,7},{7,0},{8,9},{9,10},{10,1... | collective-permute-start | bytes 1572872 | tf_op jit(solution)/shard_map/ppermute | solution.py:270
  174.3 38.4 %collective-permute-start.26 = (bf16[16,64,128]{2,1,0:T(8,128)(2,1)}, bf16[16,64,128]{2,1,0:T(8,128)(2,1)S(1)}, u32[]{:S(2)}, u32[]{:S(2)}) collective-permute-start(bf16[16,64,128]{2,1,0:T(8,128)(2,1)} %get-tuple-element.125), channel_id=1, source_target_pairs={{0,5},{1,6},{2,7},{3,0},{4,1},{5,2},{6,3},{7,4},{8,13},{9,14},{10,... | collective-permute-start | bytes 786440 | tf_op jit(solution)/shard_map/ppermute | solution.py:270
  175.5 40.0 %collective-permute-start.28 = (bf16[16,64,128]{2,1,0:T(8,128)(2,1)}, bf16[16,64,128]{2,1,0:T(8,128)(2,1)S(1)}, u32[]{:S(2)}, u32[]{:S(2)}) collective-permute-start(bf16[16,64,128]{2,1,0:T(8,128)(2,1)} %get-tuple-element.131), channel_id=1, source_target_pairs={{0,2},{1,3},{2,4},{3,5},{4,6},{5,7},{6,0},{7,1},{8,10},{9,11},{10,... | collective-permute-start | bytes 786440 | tf_op jit(solution)/shard_map/ppermute | solution.py:270
  198.3 17.2 %collective-permute-start.29 = (bf16[16,64,128]{2,1,0:T(8,128)(2,1)}, bf16[16,64,128]{2,1,0:T(8,128)(2,1)S(1)}, u32[]{:S(2)}, u32[]{:S(2)}) collective-permute-start(bf16[16,64,128]{2,1,0:T(8,128)(2,1)} %get-tuple-element.132), channel_id=1, source_target_pairs={{0,3},{1,4},{2,5},{3,6},{4,7},{5,0},{6,1},{7,2},{8,11},{9,12},{10,... | collective-permute-start | bytes 786440 | tf_op jit(solution)/shard_map/ppermute | solution.py:270
  215.4 12.0 %collective-permute-start.31 = (f32[8,128,128]{2,1,0:T(8,128)S(1)}, f32[8,128,128]{2,1,0:T(8,128)S(1)}, u32[]{:S(2)}, u32[]{:S(2)}) collective-permute-start(f32[8,128,128]{2,1,0:T(8,128)S(1)} %gram.7), channel_id=1, source_target_pairs={{0,7},{1,0},{2,1},{3,2},{4,3},{5,4},{6,5},{7,6},{8,15},{9,8},{10,9... | collective-permute-start | bytes 1572872 | tf_op jit(solution)/shard_map/ppermute | solution.py:270
  218.1 11.8 %collective-permute-start.30 = (f32[8,128,128]{2,1,0:T(8,128)S(1)}, f32[8,128,128]{2,1,0:T(8,128)S(1)}, u32[]{:S(2)}, u32[]{:S(2)}) collective-permute-start(f32[8,128,128]{2,1,0:T(8,128)S(1)} %gram.5), channel_id=1, source_target_pairs={{0,1},{1,2},{2,3},{3,4},{4,5},{5,6},{6,7},{7,0},{8,9},{9,10},{10,1... | collective-permute-start | bytes 1572872 | tf_op jit(solution)/shard_map/ppermute | solution.py:270
  (23 other events, 325.5 us)
Sparse Core Ops, SparseCore 0:
  28.0 52.3 all-gather.1

commit v5 on v4

--- a/solution.py
+++ b/solution.py
@@ -20,7 +20,6 @@
 PICKS = 4
 EARLY_PIECES = 1
 LATE_PIECES = 1
-NEXT = (1, 2 + REACH)
 ORDER = (3, 7, 2, 6, 1, 5, 0, 4)
 ALL = ("y", "x", "c", "z")
 LAT = ("y", "x", "c")
@@ -130,63 +129,76 @@
     )(index, blocks)
 
 
-def route_kernel(extras, slot_ref, at_ref, blocks_ref, *refs):
-    extra_refs, refs = refs[:extras], refs[extras:]
-    count = 2 * (REACH + 1)
-    outs, buf_ref, holds, sems = refs[:count], refs[count], refs[count + 1 : -1], refs[-1]
-    arriving = [
-        pltpu.make_async_copy(extra_ref, holds[m], sems.at[count + m])
-        for m, extra_ref in enumerate(extra_refs)
-    ]
-    for copy in arriving:
-        copy.start()
+def route_kernel(slot_ref, at_ref, blocks_ref, *refs):
+    outs, buf_ref, sems = refs[:-2], refs[-2], refs[-1]
     copies = []
     for n in ORDER:
         for part in range(2):
             first = slot_ref[2 * n + part]
             for i in range(HALF):
                 buf_ref[n, part * HALF + i] = blocks_ref[at_ref[first + i]]
-        kept = outs[n].shape[0] - 2 * HALF
-        copies.append(
-            pltpu.make_async_copy(buf_ref.at[n], outs[n].at[pl.ds(kept, 2 * HALF)], sems.at[n])
-        )
-        copies[-1].start()
-    for m, copy in enumerate(arriving):
-        copy.wait()
-        rows = pl.ds(0, holds[m].shape[0])
-        copies.append(
-            pltpu.make_async_copy(holds[m], outs[NEXT[m]].at[rows], sems.at[count + extras + m])
-        )
+        copies.append(pltpu.make_async_copy(buf_ref.at[n], outs[n], sems.at[n]))
         copies[-1].start()
     for copy in copies:
         copy.wait()
 
 
-def route(slot, at, blocks, extras=()):
+def route(slot, at, blocks):
     count = 2 * (REACH + 1)
-    tail = blocks.shape[1:]
-    rows = [2 * HALF] * count
-    for m, extra in enumerate(extras):
-        rows[NEXT[m]] += extra.shape[0]
-    return pl.pallas_call(
-        functools.partial(route_kernel, len(extras)),
+    shape = (2 * HALF,) + blocks.shape[1:]
+    return pl.pallas_call(
+        route_kernel,
         in_specs=[
             pl.BlockSpec(memory_space=pltpu.SMEM),
             pl.BlockSpec(memory_space=pltpu.SMEM),
             pl.BlockSpec(memory_space=pltpu.VMEM),
-        ]
-        + [pl.BlockSpec(memory_space=pl.ANY)] * len(extras),
+        ],
         out_specs=[pl.BlockSpec(memory_space=pltpu.HBM)] * count,
-        out_shape=[pltpu.HBM((row,) + tail, blocks.dtype) for row in rows],
+        out_shape=[pltpu.HBM(shape, blocks.dtype)] * count,
         scratch_shapes=[
-            pltpu.VMEM((count, 2 * HALF) + tail, blocks.dtype),
-            *(pltpu.VMEM(extra.shape, extra.dtype) for extra in extras),
-            pltpu.SemaphoreType.DMA((count + 2 * len(extras),)),
+            pltpu.VMEM((count,) + shape, blocks.dtype),
+            pltpu.SemaphoreType.DMA((count,)),
         ],
         compiler_params=pltpu.CompilerParams(vmem_limit_bytes=16 * MIB),
         cost_estimate=pl.CostEstimate(flops=0, bytes_accessed=4 * MIB, transcendentals=0),
         name="route",
-    )(slot, at, blocks, *map(in_hbm, extras))
+    )(slot, at, blocks)
+
+
+def join_kernel(*refs):
+    ins, outs, (buf_ref, sems) = refs[:4], refs[4:6], refs[6:]
+    rows = ins[0].shape[0]
+    copies = [pltpu.make_async_copy(ins[n], buf_ref.at[n], sems.at[n]) for n in range(4)]
+    for copy in copies:
+        copy.start()
+    for n in range(4):
+        copies[n].wait()
+        copies.append(
+            pltpu.make_async_copy(
+                buf_ref.at[n], outs[n // 2].at[pl.ds(n % 2 * rows, rows)], sems.at[4 + n]
+            )
+        )
+        copies[-1].start()
+    for copy in copies[4:]:
+        copy.wait()
+
+
+def join(parts):
+    shape = parts[0].shape
+    out = pltpu.HBM((2 * shape[0],) + shape[1:], parts[0].dtype)
+    return pl.pallas_call(
+        join_kernel,
+        in_specs=[pl.BlockSpec(memory_space=pl.ANY)] * 4,
+        out_specs=[pl.BlockSpec(memory_space=pltpu.HBM)] * 2,
+        out_shape=[out] * 2,
+        scratch_shapes=[
+            pltpu.VMEM((4,) + shape, parts[0].dtype),
+            pltpu.SemaphoreType.DMA((8,)),
+        ],
+        compiler_params=pltpu.CompilerParams(vmem_limit_bytes=8 * MIB),
+        cost_estimate=pl.CostEstimate(flops=0, bytes_accessed=2 * MIB, transcendentals=0),
+        name="join",
+    )(*map(in_hbm, parts))
 
 
 def gram_kernel(layout, lefts, *refs):
@@ -373,8 +385,7 @@
         return parts[k], parts[k + REACH + 1]
 
     sent = list(sent_early) + list(sent_late)
-    fine = (-1, TOKENS // RANKS // LATE_PIECES, BLOCK)
-    held, extras, traded = [], [], None
+    held, extras, traded = [], None, None
     for n in range(len(sent)):
         late = n >= EARLY_PIECES
         got = spread(sent[n])
@@ -383,16 +394,16 @@
         if traded is not None:
             traded, got = lax.optimization_barrier((traded, got))
             held[-1].update(traded)
-        first_late = n == EARLY_PIECES
-        parts = route(slots, position[:, int(late)], got, extras if first_late else ())
+        parts = route(slots, position[:, int(late)], got)
         if n + 1 < len(sent):
             sent[n + 1], parts = lax.optimization_barrier((sent[n + 1], parts))
         traded = {k: trade(both(parts, k), k) for k in (3, 2)}
         held.append({0: both(parts, 0), **traded})
         if late:
-            held[-1][1] = trade(both(parts, 1), 1)
+            low, high = both(parts, 1)
+            held[-1][1] = trade(join((extras[0], low, extras[1], high)), 1)
         else:
-            extras += [part.reshape(fine) for part in both(parts, 1)]
+            extras = both(parts, 1)
 
     def layer(side, late):
         out = []

time: 242 us -> 242 us (level)
    pallas_call x2 -> x3, Pallas kernels: 4.62 us -> 5.92 us  [the longest x2 3.93 us: route(): pl.pallas_call(route_kernel, in_specs=[pl.BlockSpec(memory_space=pltpu.SM...]
where the time goes in v5:
time: 242 us; the launch traced here: 239 us
  waiting for transfers between devices  108 us (45%)
  starting transfers between devices  79.7 us (33%)
  Pallas kernels  27.5 us (11%)
  between operations  14.5 us (6%)
  local copies, waits for them, and re-layouts  6.34 us (3%)
  other arithmetic  2.78 us (1%)
    ppermute x32, waiting for transfers between devices, shift(): lax.ppermute(value, axis, [(i, (i + by) % size) for i in range(size)])  82.8 us
    ppermute x32, starting transfers between devices, shift(): lax.ppermute(value, axis, [(i, (i + by) % size) for i in range(size)])  55.9 us
    all_to_all x2, starting transfers between devices, spread(): lax.all_to_all(sent.reshape((GROUPS, FROM_GROUP) + sent.shape[1:]), LAT,...  10.9 us
    pallas_call x2, Pallas kernels, encode(): pl.pallas_call(kernel, grid_spec=pltpu.PrefetchScalarGridSpec(num_scalar_...  9.73 us
    all_to_all x1, starting transfers between devices, gather_z(): return lax.all_to_all(spread, 'z', 0, 0, tiled=True)  9.15 us
    all_to_all x1, waiting for transfers between devices, gather_z(): return lax.all_to_all(spread, 'z', 0, 0, tiled=True)  8.67 us
    pallas_call x4, Pallas kernels, gram(): pl.pallas_call(functools.partial(gram_kernel, layout, len(lefts)), in_spe...  6.8 us
    all_gather x1, waiting for transfers between devices, shards(): lax.all_gather(jnp.concatenate([rows_late, lists], axis=1), LAT, axis=0,...  6.54 us
  transfers between devices with their start and end apart: 37, of which 19 were waited for; matrix products, arithmetic and copies ran while one was open for 1% of the time, Pallas kernels for 8%

profile of v5, /device:TPU:1, one launch (start us, length us, event | category | flops | bytes accessed | tf_op | source)
XLA Modules:
  0.0 239.2 jit_solution(3498006734848233769)
XLA Ops:
  8.1 9.1 %all-to-all-start = ((bf16[8,2,2,3584]{3,2,1,0:T(2,128)(2,1)}), bf16[8,2,2,3584]{3,2,1,0:T(2,128)(2,1)S(1)}, u32[]{:S(2)}, u32[]{:S(2)}) async-start(bf16[8,2,2,3584]{3,2,1,0:T(2,128)(2,1)} %broadcast_in_dim.46), calls=%async_computation | async-start | bytes 458752 | tf_op jit(solution)/shard_map/all_to_all | solution.py:287
  18.3 8.7 %all-to-all-done = bf16[8,2,2,3584]{3,2,1,0:T(2,128)(2,1)S(1)} async-done(((bf16[8,2,2,3584]{3,2,1,0:T(2,128)(2,1)}), bf16[8,2,2,3584]{3,2,1,0:T(2,128)(2,1)S(1)}, u32[]{:S(2)}, u32[]{:S(2)}) %all-to-all-start) | async-done | bytes 229408 | tf_op jit(solution)/shard_map/all_to_all | solution.py:287
  28.0 2.6 %collective-permute-start.2 = (bf16[16,1792]{1,0:T(8,128)(2,1)S(1)}, bf16[16,1792]{1,0:T(8,128)(2,1)S(1)}, u32[]{:S(2)}, u32[]{:S(2)}) collective-permute-start(bf16[16,1792]{1,0:T(8,128)(2,1)S(1)} %get-tuple-element.146), channel_id=1, source_target_pairs={{0,48},{16,0},{32,16},{48,32},{1,49},{17,1},{33,17},{49,33},{2,50}... | collective-permute-start | bytes 172040 | tf_op jit(solution)/shard_map/ppermute | solution.py:282
  33.6 2.6 %collective-permute-start.7 = (bf16[16,1792]{1,0:T(8,128)(2,1)S(1)}, bf16[16,1792]{1,0:T(8,128)(2,1)S(1)}, u32[]{:S(2)}, u32[]{:S(2)}) collective-permute-start(bf16[16,1792]{1,0:T(8,128)(2,1)S(1)} %get-tuple-element.145), channel_id=1, source_target_pairs={{0,128},{64,192},{128,0},{192,64},{1,129},{65,193},{129,1},{193,65... | collective-permute-start | bytes 172040 | tf_op jit(solution)/shard_map/ppermute | solution.py:282
  45.1 5.4 %collective-permute-done.4 = bf16[4,16,1792]{2,1,0:T(8,128)(2,1)S(1)} collective-permute-done((bf16[4,16,1792]{2,1,0:T(8,128)(2,1)S(1)}, bf16[4,16,1792]{2,1,0:T(8,128)(2,1)S(1)}, u32[]{:S(2)}, u32[]{:S(2)}) %collective-permute-start.4) | collective-permute-done | bytes 229408 | tf_op jit(solution)/shard_map/ppermute | solution.py:282
  52.0 2.5 %collective-permute-done.11 = bf16[4,16,1792]{2,1,0:T(8,128)(2,1)S(1)} collective-permute-done((bf16[4,16,1792]{2,1,0:T(8,128)(2,1)S(1)}, bf16[4,16,1792]{2,1,0:T(8,128)(2,1)S(1)}, u32[]{:S(2)}, u32[]{:S(2)}) %collective-permute-start.11) | collective-permute-done | bytes 229408 | tf_op jit(solution)/shard_map/ppermute | solution.py:282
  54.7 6.0 %collective-permute-start.12 = (bf16[256,3584]{1,0:T(8,128)(2,1)S(1)}, bf16[256,3584]{1,0:T(8,128)(2,1)}, u32[]{:S(2)}, u32[]{:S(2)}) collective-permute-start(bf16[256,3584]{1,0:T(8,128)(2,1)S(1)} %bitcast.68), channel_id=1, source_target_pairs={{0,8},{8,0},{1,9},{9,1},{2,10},{10,2},{3,11},{11,3},{4,12},{12,4},... | collective-permute-start | bytes 5505032 | tf_op jit(solution)/shard_map/ppermute | solution.py:282
  61.0 3.3 %collective-permute-done.12.other_ref = bf16[256,3584]{1,0:T(8,128)(2,1)} collective-permute-done((bf16[256,3584]{1,0:T(8,128)(2,1)S(1)}, bf16[256,3584]{1,0:T(8,128)(2,1)}, u32[]{:S(2)}, u32[]{:S(2)}) %collective-permute-start.12) | collective-permute-done | bytes 1835040 | tf_op jit(solution)/shard_map/ppermute | solution.py:282
  64.3 5.9 %encode_early.1 = bf16[8,4,64,128]{3,2,1,0:T(8,128)(2,1)} custom-call(s32[32]{0:T(128)S(1)} %reshape.181.place_ref, bf16[256,3584]{1,0:T(8,128)(2,1)S(1)} %bitcast.69, bf16[256,3584]{1,0:T(8,128)(2,1)} %collective-permute-done.12.other_ref, bf16[3584,512]{1,0:T(8,128)(2,1)} %w_ref.2, f32[1,512]{1,0:T(1,128)S(1)} %bitcast.72, f32[1,512]{1,0:T(1,128)S(1)} %bitcast.73), custom_call_target="tpu_custom_call" | custom-call | flops 1879048192 | bytes 8388608 | tf_op jit(solution)/shard_map/encode_early/pallas_call | solution.py:73
  70.2 3.7 %all-to-all-start.1 = ((bf16[8,4,64,128]{3,2,1,0:T(8,128)(2,1)}), bf16[8,4,64,128]{3,2,1,0:T(8,128)(2,1)S(1)}, u32[]{:S(2)}, u32[]{:S(2)}) async-start(bf16[8,4,64,128]{3,2,1,0:T(8,128)(2,1)} %encode_early.1), calls=%async_computation.1 | async-start | bytes 1048576 | tf_op jit(solution)/shard_map/all_to_all | solution.py:372
  73.9 6.5 %all-gather.2.cloned.1.call-done.acts_ref = bf16[512,3712]{1,0:T(8,128)(2,1)} async-done(((bf16[16,3712]{1,0:T(8,128)(2,1)}), bf16[512,3712]{1,0:T(8,128)(2,1)}) %all-gather.2.cloned.1.call-update) | async-done | bytes 3801104 | tf_op jit(solution)/shard_map/all_gather | solution.py:327
  82.5 3.9 %encode_late.1 = (bf16[4,64,128]{2,1,0:T(8,128)(2,1)S(1)}, bf16[4,64,128]{2,1,0:T(8,128)(2,1)S(1)}, bf16[4,64,128]{2,1,0:T(8,128)(2,1)S(1)}, bf16[4,64,128]{2,1,...) custom-call(s32[1]{0:T(128)} %bitcast.29.plane_ref, ...), custom_call_target="tpu_custom_call" | custom-call | flops 1879048192 | bytes 8388608 | tf_op jit(solution)/shard_map/encode_late/pallas_call | solution.py:73
  86.4 3.9 %all-to-all-done.1 = bf16[8,4,64,128]{3,2,1,0:T(8,128)(2,1)S(1)} async-done(((bf16[8,4,64,128]{3,2,1,0:T(8,128)(2,1)}), bf16[8,4,64,128]{3,2,1,0:T(8,128)(2,1)S(1)}, u32[]{:S(2)}, u32[]{:S(2)}) %all-to-all-start.1) | async-done | bytes 524320 | tf_op jit(solution)/shard_map/all_to_all | solution.py:372
  93.3 4.7 %all-to-all-start.2 = ((bf16[32,4,64,128]{3,2,1,0:T(8,128)(2,1)}), bf16[32,4,64,128]{3,2,1,0:T(8,128)(2,1)S(1)}, u32[]{:S(2)}, u32[]{:S(2)}) async-start(bf16[32,4,64,128]{3,2,1,0:T(8,128)(2,1)} %bitcast.76), calls=%async_computation.2 | async-start | bytes 4194304 | tf_op jit(solution)/shard_map/all_to_all | solution.py:344
  99.2 2.4 %collective-permute-start.15 = (bf16[4,64,128]{2,1,0:T(8,128)(2,1)S(1)}, bf16[4,64,128]{2,1,0:T(8,128)(2,1)S(1)}, u32[]{:S(2)}, u32[]{:S(2)}) collective-permute-start(bf16[4,64,128]{2,1,0:T(8,128)(2,1)S(1)} %get-tuple-element.98), channel_id=1, source_target_pairs={{0,3},{1,4},{2,5},{3,6},{4,7},{5,0},{6,1},{7,2},{8,11},{9,12},{10,... | collective-permute-start | bytes 196616 | tf_op jit(solution)/shard_map/ppermute | solution.py:282
  101.6 3.1 %collective-permute-start.16 = (bf16[4,64,128]{2,1,0:T(8,128)(2,1)S(1)}, bf16[4,64,128]{2,1,0:T(8,128)(2,1)S(1)}, u32[]{:S(2)}, u32[]{:S(2)}) collective-permute-start(bf16[4,64,128]{2,1,0:T(8,128)(2,1)S(1)} %get-tuple-element.99), channel_id=1, source_target_pairs={{0,4},{1,5},{2,6},{3,7},{4,0},{5,1},{6,2},{7,3},{8,12},{9,13},{10,... | collective-permute-start | bytes 196616 | tf_op jit(solution)/shard_map/ppermute | solution.py:282
  105.9 2.9 %collective-permute-start.18 = (bf16[4,64,128]{2,1,0:T(8,128)(2,1)S(1)}, bf16[4,64,128]{2,1,0:T(8,128)(2,1)S(1)}, u32[]{:S(2)}, u32[]{:S(2)}) collective-permute-start(bf16[4,64,128]{2,1,0:T(8,128)(2,1)S(1)} %get-tuple-element.101), channel_id=1, source_target_pairs={{0,6},{1,7},{2,0},{3,1},{4,2},{5,3},{6,4},{7,5},{8,14},{9,15},{10,... | collective-permute-start | bytes 196616 | tf_op jit(solution)/shard_map/ppermute | solution.py:282
  110.1 2.8 %collective-permute-done.16 = bf16[4,64,128]{2,1,0:T(8,128)(2,1)S(1)} collective-permute-done((bf16[4,64,128]{2,1,0:T(8,128)(2,1)S(1)}, bf16[4,64,128]{2,1,0:T(8,128)(2,1)S(1)}, u32[]{:S(2)}, u32[]{:S(2)}) %collective-permute-start.16) | collective-permute-done | bytes 65568 | tf_op jit(solution)/shard_map/ppermute | solution.py:282
  113.0 4.5 %collective-permute-done.18 = bf16[4,64,128]{2,1,0:T(8,128)(2,1)S(1)} collective-permute-done((bf16[4,64,128]{2,1,0:T(8,128)(2,1)S(1)}, bf16[4,64,128]{2,1,0:T(8,128)(2,1)S(1)}, u32[]{:S(2)}, u32[]{:S(2)}) %collective-permute-start.18) | collective-permute-done | bytes 65568 | tf_op jit(solution)/shard_map/ppermute | solution.py:282
  119.5 6.5 %all-to-all-done.2 = bf16[32,4,64,128]{3,2,1,0:T(8,128)(2,1)S(1)} async-done(((bf16[32,4,64,128]{3,2,1,0:T(8,128)(2,1)}), bf16[32,4,64,128]{3,2,1,0:T(8,128)(2,1)S(1)}, u32[]{:S(2)}, u32[]{:S(2)}) %all-to-all-start.2) | async-done | bytes 2097184 | tf_op jit(solution)/shard_map/all_to_all | solution.py:344
  127.9 6.2 %all-to-all-start.3 = ((bf16[32,4,64,128]{3,2,1,0:T(8,128)(2,1)}), bf16[32,4,64,128]{3,2,1,0:T(8,128)(2,1)S(1)}, u32[]{:S(2)}, u32[]{:S(2)}) async-start(bf16[32,4,64,128]{3,2,1,0:T(8,128)(2,1)} %bitcast.77), calls=%async_computation.3 | async-start | bytes 4194304 | tf_op jit(solution)/shard_map/all_to_all | solution.py:344
  134.6 3.2 %collective-permute-start.21 = (bf16[16,64,128]{2,1,0:T(8,128)(2,1)}, bf16[16,64,128]{2,1,0:T(8,128)(2,1)S(1)}, u32[]{:S(2)}, u32[]{:S(2)}) collective-permute-start(bf16[16,64,128]{2,1,0:T(8,128)(2,1)} %get-tuple-element.116), channel_id=1, source_target_pairs={{0,6},{1,7},{2,0},{3,1},{4,2},{5,3},{6,4},{7,5},{8,14},{9,15},{10,... | collective-permute-start | bytes 786440 | tf_op jit(solution)/shard_map/ppermute | solution.py:282
  137.7 4.5 %collective-permute-start.23 = (bf16[16,64,128]{2,1,0:T(8,128)(2,1)S(1)}, bf16[16,64,128]{2,1,0:T(8,128)(2,1)S(1)}, u32[]{:S(2)}, u32[]{:S(2)}) collective-permute-start(bf16[16,64,128]{2,1,0:T(8,128)(2,1)S(1)} %copy-done.17), channel_id=1, source_target_pairs={{0,5},{1,6},{2,7},{3,0},{4,1},{5,2},{6,3},{7,4},{8,13},{9,14},{10,... | collective-permute-start | bytes 786440 | tf_op jit(solution)/shard_map/ppermute | solution.py:282
  142.2 3.2 %collective-permute-done.20.refs_2_ = bf16[16,64,128]{2,1,0:T(8,128)(2,1)S(1)} collective-permute-done((bf16[16,64,128]{2,1,0:T(8,128)(2,1)}, bf16[16,64,128]{2,1,0:T(8,128)(2,1)S(1)}, u32[]{:S(2)}, u32[]{:S(2)}) %collective-permute-start.20) | collective-permute-done | bytes 262176 | tf_op jit(solution)/shard_map/ppermute | solution.py:282
  145.4 5.4 %collective-permute-done.21.refs_2_ = bf16[16,64,128]{2,1,0:T(8,128)(2,1)S(1)} collective-permute-done((bf16[16,64,128]{2,1,0:T(8,128)(2,1)}, bf16[16,64,128]{2,1,0:T(8,128)(2,1)S(1)}, u32[]{:S(2)}, u32[]{:S(2)}) %collective-permute-start.21) | collective-permute-done | bytes 262176 | tf_op jit(solution)/shard_map/ppermute | solution.py:282
  150.8 13.4 %collective-permute-done.22.refs_3_ = bf16[16,64,128]{2,1,0:T(8,128)(2,1)S(1)} collective-permute-done((bf16[16,64,128]{2,1,0:T(8,128)(2,1)}, bf16[16,64,128]{2,1,0:T(8,128)(2,1)S(1)}, u32[]{:S(2)}, u32[]{:S(2)}) %collective-permute-start.22) | collective-permute-done | bytes 262176 | tf_op jit(solution)/shard_map/ppermute | solution.py:282
  168.3 3.8 %collective-permute-start.24 = (bf16[32,64,128]{2,1,0:T(8,128)(2,1)}, bf16[32,64,128]{2,1,0:T(8,128)(2,1)S(1)}, u32[]{:S(2)}, u32[]{:S(2)}) collective-permute-start(bf16[32,64,128]{2,1,0:T(8,128)(2,1)} %get-tuple-element.124), channel_id=1, source_target_pairs={{0,7},{1,0},{2,1},{3,2},{4,3},{5,4},{6,5},{7,6},{8,15},{9,8},{10,9... | collective-permute-start | bytes 1572872 | tf_op jit(solution)/shard_map/ppermute | solution.py:282
  176.8 2.4 %collective-permute-start.28 = (bf16[16,64,128]{2,1,0:T(8,128)(2,1)}, bf16[16,64,128]{2,1,0:T(8,128)(2,1)S(1)}, u32[]{:S(2)}, u32[]{:S(2)}) collective-permute-start(bf16[16,64,128]{2,1,0:T(8,128)(2,1)} %get-tuple-element.135), channel_id=1, source_target_pairs={{0,2},{1,3},{2,4},{3,5},{4,6},{5,7},{6,0},{7,1},{8,10},{9,11},{10,... | collective-permute-start | bytes 786440 | tf_op jit(solution)/shard_map/ppermute | solution.py:282
  179.2 20.3 %collective-permute-done.25.refs_6_ = bf16[16,64,128]{2,1,0:T(8,128)(2,1)S(1)} collective-permute-done((bf16[16,64,128]{2,1,0:T(8,128)(2,1)}, bf16[16,64,128]{2,1,0:T(8,128)(2,1)S(1)}, u32[]{:S(2)}, u32[]{:S(2)}) %collective-permute-start.25) | collective-permute-done | bytes 262176 | tf_op jit(solution)/shard_map/ppermute | solution.py:282
  199.5 14.6 %collective-permute-done.26.refs_7_ = bf16[16,64,128]{2,1,0:T(8,128)(2,1)S(1)} collective-permute-done((bf16[16,64,128]{2,1,0:T(8,128)(2,1)}, bf16[16,64,128]{2,1,0:T(8,128)(2,1)S(1)}, u32[]{:S(2)}, u32[]{:S(2)}) %collective-permute-start.26) | collective-permute-done | bytes 262176 | tf_op jit(solution)/shard_map/ppermute | solution.py:282
  225.9 2.8 %collective-permute-done.31.high_far_ref = f32[8,128,128]{2,1,0:T(8,128)S(1)} collective-permute-done((f32[8,128,128]{2,1,0:T(8,128)S(1)}, f32[8,128,128]{2,1,0:T(8,128)S(1)}, u32[]{:S(2)}, u32[]{:S(2)}) %collective-permute-start.31) | collective-permute-done | bytes 524320 | tf_op jit(solution)/shard_map/ppermute | solution.py:282
  228.7 2.6 %collective-permute-done.30.low_far_ref = f32[8,128,128]{2,1,0:T(8,128)S(1)} collective-permute-done((f32[8,128,128]{2,1,0:T(8,128)S(1)}, f32[8,128,128]{2,1,0:T(8,128)S(1)}, u32[]{:S(2)}, u32[]{:S(2)}) %collective-permute-start.30) | collective-permute-done | bytes 524320 | tf_op jit(solution)/shard_map/ppermute | solution.py:282
  (127 shorter events, 51.4 us)
Async XLA Ops:
  8.1 18.9 %all-to-all-start = ((bf16[8,2,2,3584]{3,2,1,0:T(2,128)(2,1)}), bf16[8,2,2,3584]{3,2,1,0:T(2,128)(2,1)S(1)}, u32[]{:S(2)}, u32[]{:S(2)}) async-start(bf16[8,2,2,3584]{3,2,1,0:T(2,128)(2,1)} %broadcast_in_dim.46), calls=%async_computation | async-start | bytes 458752 | tf_op jit(solution)/shard_map/all_to_all | solution.py:287
  17.3 63.2 %all-gather.2.cloned.1.call-start = ((), (), s32[]{:S(2)}) async-start(), calls=%async_computation.4 | async-start | bytes 3919872 | tf_op jit(solution)/shard_map/all_gather | solution.py:327
  28.0 8.2 %collective-permute-start.2 = (bf16[16,1792]{1,0:T(8,128)(2,1)S(1)}, bf16[16,1792]{1,0:T(8,128)(2,1)S(1)}, u32[]{:S(2)}, u32[]{:S(2)}) collective-permute-start(bf16[16,1792]{1,0:T(8,128)(2,1)S(1)} %get-tuple-element.146), channel_id=1, source_target_pairs={{0,48},{16,0},{32,16},{48,32},{1,49},{17,1},{33,17},{49,33},{2,50}... | collective-permute-start | bytes 172040 | tf_op jit(solution)/shard_map/ppermute | solution.py:282
  37.3 7.4 %collective-permute-start.3 = (bf16[4,16,1792]{2,1,0:T(8,128)(2,1)S(1)}, bf16[4,16,1792]{2,1,0:T(8,128)(2,1)S(1)}, u32[]{:S(2)}, u32[]{:S(2)}) collective-permute-start(bf16[4,16,1792]{2,1,0:T(8,128)(2,1)S(1)} %get-tuple-element.138), channel_id=1, source_target_pairs={{0,64},{64,128},{128,192},{192,0},{1,65},{65,129},{129,193},{193,1... | collective-permute-start | bytes 688136 | tf_op jit(solution)/shard_map/ppermute | solution.py:282
  37.8 12.7 %collective-permute-start.4 = (bf16[4,16,1792]{2,1,0:T(8,128)(2,1)S(1)}, bf16[4,16,1792]{2,1,0:T(8,128)(2,1)S(1)}, u32[]{:S(2)}, u32[]{:S(2)}) collective-permute-start(bf16[4,16,1792]{2,1,0:T(8,128)(2,1)S(1)} %get-tuple-element.138), channel_id=1, source_target_pairs={{0,128},{64,192},{128,0},{192,64},{1,129},{65,193},{129,1},{193,65... | collective-permute-start | bytes 688136 | tf_op jit(solution)/shard_map/ppermute | solution.py:282
  39.5 11.7 %collective-permute-start.5 = (bf16[4,16,1792]{2,1,0:T(8,128)(2,1)S(1)}, bf16[4,16,1792]{2,1,0:T(8,128)(2,1)S(1)}, u32[]{:S(2)}, u32[]{:S(2)}) collective-permute-start(bf16[4,16,1792]{2,1,0:T(8,128)(2,1)S(1)} %get-tuple-element.138), channel_id=1, source_target_pairs={{0,192},{64,0},{128,64},{192,128},{1,193},{65,1},{129,65},{193,129... | collective-permute-start | bytes 688136 | tf_op jit(solution)/shard_map/ppermute | solution.py:282
  40.6 10.6 %collective-permute-start.9 = (bf16[4,16,1792]{2,1,0:T(8,128)(2,1)S(1)}, bf16[4,16,1792]{2,1,0:T(8,128)(2,1)S(1)}, u32[]{:S(2)}, u32[]{:S(2)}) collective-permute-start(bf16[4,16,1792]{2,1,0:T(8,128)(2,1)S(1)} %get-tuple-element.140), channel_id=1, source_target_pairs={{0,16},{16,32},{32,48},{48,0},{1,17},{17,33},{33,49},{49,1},{2,18}... | collective-permute-start | bytes 688136 | tf_op jit(solution)/shard_map/ppermute | solution.py:282
  42.0 10.1 %collective-permute-start.10 = (bf16[4,16,1792]{2,1,0:T(8,128)(2,1)S(1)}, bf16[4,16,1792]{2,1,0:T(8,128)(2,1)S(1)}, u32[]{:S(2)}, u32[]{:S(2)}) collective-permute-start(bf16[4,16,1792]{2,1,0:T(8,128)(2,1)S(1)} %get-tuple-element.140), channel_id=1, source_target_pairs={{0,32},{16,48},{32,0},{48,16},{1,33},{17,49},{33,1},{49,17},{2,34}... | collective-permute-start | bytes 688136 | tf_op jit(solution)/shard_map/ppermute | solution.py:282
  44.8 9.8 %collective-permute-start.11 = (bf16[4,16,1792]{2,1,0:T(8,128)(2,1)S(1)}, bf16[4,16,1792]{2,1,0:T(8,128)(2,1)S(1)}, u32[]{:S(2)}, u32[]{:S(2)}) collective-permute-start(bf16[4,16,1792]{2,1,0:T(8,128)(2,1)S(1)} %get-tuple-element.140), channel_id=1, source_target_pairs={{0,48},{16,0},{32,16},{48,32},{1,49},{17,1},{33,17},{49,33},{2,50}... | collective-permute-start | bytes 688136 | tf_op jit(solution)/shard_map/ppermute | solution.py:282
  54.7 9.6 %collective-permute-start.12 = (bf16[256,3584]{1,0:T(8,128)(2,1)S(1)}, bf16[256,3584]{1,0:T(8,128)(2,1)}, u32[]{:S(2)}, u32[]{:S(2)}) collective-permute-start(bf16[256,3584]{1,0:T(8,128)(2,1)S(1)} %bitcast.68), channel_id=1, source_target_pairs={{0,8},{8,0},{1,9},{9,1},{2,10},{10,2},{3,11},{11,3},{4,12},{12,4},... | collective-permute-start | bytes 5505032 | tf_op jit(solution)/shard_map/ppermute | solution.py:282
  70.2 20.1 %all-to-all-start.1 = ((bf16[8,4,64,128]{3,2,1,0:T(8,128)(2,1)}), bf16[8,4,64,128]{3,2,1,0:T(8,128)(2,1)S(1)}, u32[]{:S(2)}, u32[]{:S(2)}) async-start(bf16[8,4,64,128]{3,2,1,0:T(8,128)(2,1)} %encode_early.1), calls=%async_computation.1 | async-start | bytes 1048576 | tf_op jit(solution)/shard_map/all_to_all | solution.py:372
  93.3 32.6 %all-to-all-start.2 = ((bf16[32,4,64,128]{3,2,1,0:T(8,128)(2,1)}), bf16[32,4,64,128]{3,2,1,0:T(8,128)(2,1)S(1)}, u32[]{:S(2)}, u32[]{:S(2)}) async-start(bf16[32,4,64,128]{3,2,1,0:T(8,128)(2,1)} %bitcast.76), calls=%async_computation.2 | async-start | bytes 4194304 | tf_op jit(solution)/shard_map/all_to_all | solution.py:344
  98.1 7.8 %collective-permute-start.13 = (bf16[4,64,128]{2,1,0:T(8,128)(2,1)S(1)}, bf16[4,64,128]{2,1,0:T(8,128)(2,1)S(1)}, u32[]{:S(2)}, u32[]{:S(2)}) collective-permute-start(bf16[4,64,128]{2,1,0:T(8,128)(2,1)S(1)} %get-tuple-element.96), channel_id=1, source_target_pairs={{0,1},{1,2},{2,3},{3,4},{4,5},{5,6},{6,7},{7,0},{8,9},{9,10},{10,1... | collective-permute-start | bytes 196616 | tf_op jit(solution)/shard_map/ppermute | solution.py:282
  99.2 9.7 %collective-permute-start.14 = (bf16[4,64,128]{2,1,0:T(8,128)(2,1)S(1)}, bf16[4,64,128]{2,1,0:T(8,128)(2,1)S(1)}, u32[]{:S(2)}, u32[]{:S(2)}) collective-permute-start(bf16[4,64,128]{2,1,0:T(8,128)(2,1)S(1)} %get-tuple-element.97), channel_id=1, source_target_pairs={{0,2},{1,3},{2,4},{3,5},{4,6},{5,7},{6,0},{7,1},{8,10},{9,11},{10,... | collective-permute-start | bytes 196616 | tf_op jit(solution)/shard_map/ppermute | solution.py:282
  99.2 10.9 %collective-permute-start.15 = (bf16[4,64,128]{2,1,0:T(8,128)(2,1)S(1)}, bf16[4,64,128]{2,1,0:T(8,128)(2,1)S(1)}, u32[]{:S(2)}, u32[]{:S(2)}) collective-permute-start(bf16[4,64,128]{2,1,0:T(8,128)(2,1)S(1)} %get-tuple-element.98), channel_id=1, source_target_pairs={{0,3},{1,4},{2,5},{3,6},{4,7},{5,0},{6,1},{7,2},{8,11},{9,12},{10,... | collective-permute-start | bytes 196616 | tf_op jit(solution)/shard_map/ppermute | solution.py:282
  101.6 11.3 %collective-permute-start.16 = (bf16[4,64,128]{2,1,0:T(8,128)(2,1)S(1)}, bf16[4,64,128]{2,1,0:T(8,128)(2,1)S(1)}, u32[]{:S(2)}, u32[]{:S(2)}) collective-permute-start(bf16[4,64,128]{2,1,0:T(8,128)(2,1)S(1)} %get-tuple-element.99), channel_id=1, source_target_pairs={{0,4},{1,5},{2,6},{3,7},{4,0},{5,1},{6,2},{7,3},{8,12},{9,13},{10,... | collective-permute-start | bytes 196616 | tf_op jit(solution)/shard_map/ppermute | solution.py:282
  104.7 8.3 %collective-permute-start.17 = (bf16[4,64,128]{2,1,0:T(8,128)(2,1)S(1)}, bf16[4,64,128]{2,1,0:T(8,128)(2,1)S(1)}, u32[]{:S(2)}, u32[]{:S(2)}) collective-permute-start(bf16[4,64,128]{2,1,0:T(8,128)(2,1)S(1)} %get-tuple-element.100), channel_id=1, source_target_pairs={{0,5},{1,6},{2,7},{3,0},{4,1},{5,2},{6,3},{7,4},{8,13},{9,14},{10,... | collective-permute-start | bytes 196616 | tf_op jit(solution)/shard_map/ppermute | solution.py:282
  105.9 11.5 %collective-permute-start.18 = (bf16[4,64,128]{2,1,0:T(8,128)(2,1)S(1)}, bf16[4,64,128]{2,1,0:T(8,128)(2,1)S(1)}, u32[]{:S(2)}, u32[]{:S(2)}) collective-permute-start(bf16[4,64,128]{2,1,0:T(8,128)(2,1)S(1)} %get-tuple-element.101), channel_id=1, source_target_pairs={{0,6},{1,7},{2,0},{3,1},{4,2},{5,3},{6,4},{7,5},{8,14},{9,15},{10,... | collective-permute-start | bytes 196616 | tf_op jit(solution)/shard_map/ppermute | solution.py:282
  108.9 8.6 %collective-permute-start.19 = (bf16[4,64,128]{2,1,0:T(8,128)(2,1)S(1)}, bf16[4,64,128]{2,1,0:T(8,128)(2,1)S(1)}, u32[]{:S(2)}, u32[]{:S(2)}) collective-permute-start(bf16[4,64,128]{2,1,0:T(8,128)(2,1)S(1)} %get-tuple-element.102), channel_id=1, source_target_pairs={{0,7},{1,0},{2,1},{3,2},{4,3},{5,4},{6,5},{7,6},{8,15},{9,8},{10,9... | collective-permute-start | bytes 196616 | tf_op jit(solution)/shard_map/ppermute | solution.py:282
  127.9 36.4 %all-to-all-start.3 = ((bf16[32,4,64,128]{3,2,1,0:T(8,128)(2,1)}), bf16[32,4,64,128]{3,2,1,0:T(8,128)(2,1)S(1)}, u32[]{:S(2)}, u32[]{:S(2)}) async-start(bf16[32,4,64,128]{3,2,1,0:T(8,128)(2,1)} %bitcast.77), calls=%async_computation.3 | async-start | bytes 4194304 | tf_op jit(solution)/shard_map/all_to_all | solution.py:344
  134.1 11.4 %collective-permute-start.20 = (bf16[16,64,128]{2,1,0:T(8,128)(2,1)}, bf16[16,64,128]{2,1,0:T(8,128)(2,1)S(1)}, u32[]{:S(2)}, u32[]{:S(2)}) collective-permute-start(bf16[16,64,128]{2,1,0:T(8,128)(2,1)} %get-tuple-element.115), channel_id=1, source_target_pairs={{0,2},{1,3},{2,4},{3,5},{4,6},{5,7},{6,0},{7,1},{8,10},{9,11},{10,... | collective-permute-start | bytes 786440 | tf_op jit(solution)/shard_map/ppermute | solution.py:282
  134.6 16.3 %collective-permute-start.21 = (bf16[16,64,128]{2,1,0:T(8,128)(2,1)}, bf16[16,64,128]{2,1,0:T(8,128)(2,1)S(1)}, u32[]{:S(2)}, u32[]{:S(2)}) collective-permute-start(bf16[16,64,128]{2,1,0:T(8,128)(2,1)} %get-tuple-element.116), channel_id=1, source_target_pairs={{0,6},{1,7},{2,0},{3,1},{4,2},{5,3},{6,4},{7,5},{8,14},{9,15},{10,... | collective-permute-start | bytes 786440 | tf_op jit(solution)/shard_map/ppermute | solution.py:282
  137.7 26.5 %collective-permute-start.22 = (bf16[16,64,128]{2,1,0:T(8,128)(2,1)}, bf16[16,64,128]{2,1,0:T(8,128)(2,1)S(1)}, u32[]{:S(2)}, u32[]{:S(2)}) collective-permute-start(bf16[16,64,128]{2,1,0:T(8,128)(2,1)} %get-tuple-element.117), channel_id=1, source_target_pairs={{0,3},{1,4},{2,5},{3,6},{4,7},{5,0},{6,1},{7,2},{8,11},{9,12},{10,... | collective-permute-start | bytes 786440 | tf_op jit(solution)/shard_map/ppermute | solution.py:282
  137.7 26.5 %collective-permute-start.23 = (bf16[16,64,128]{2,1,0:T(8,128)(2,1)S(1)}, bf16[16,64,128]{2,1,0:T(8,128)(2,1)S(1)}, u32[]{:S(2)}, u32[]{:S(2)}) collective-permute-start(bf16[16,64,128]{2,1,0:T(8,128)(2,1)S(1)} %copy-done.17), channel_id=1, source_target_pairs={{0,5},{1,6},{2,7},{3,0},{4,1},{5,2},{6,3},{7,4},{8,13},{9,14},{10,... | collective-permute-start | bytes 786440 | tf_op jit(solution)/shard_map/ppermute | solution.py:282
  168.3 45.8 %collective-permute-start.24 = (bf16[32,64,128]{2,1,0:T(8,128)(2,1)}, bf16[32,64,128]{2,1,0:T(8,128)(2,1)S(1)}, u32[]{:S(2)}, u32[]{:S(2)}) collective-permute-start(bf16[32,64,128]{2,1,0:T(8,128)(2,1)} %get-tuple-element.124), channel_id=1, source_target_pairs={{0,7},{1,0},{2,1},{3,2},{4,3},{5,4},{6,5},{7,6},{8,15},{9,8},{10,9... | collective-permute-start | bytes 1572872 | tf_op jit(solution)/shard_map/ppermute | solution.py:282
  172.1 27.4 %collective-permute-start.25 = (bf16[16,64,128]{2,1,0:T(8,128)(2,1)}, bf16[16,64,128]{2,1,0:T(8,128)(2,1)S(1)}, u32[]{:S(2)}, u32[]{:S(2)}) collective-permute-start(bf16[16,64,128]{2,1,0:T(8,128)(2,1)} %get-tuple-element.128), channel_id=1, source_target_pairs={{0,6},{1,7},{2,0},{3,1},{4,2},{5,3},{6,4},{7,5},{8,14},{9,15},{10,... | collective-permute-start | bytes 786440 | tf_op jit(solution)/shard_map/ppermute | solution.py:282
  174.5 42.4 %collective-permute-start.27 = (bf16[32,64,128]{2,1,0:T(8,128)(2,1)}, bf16[32,64,128]{2,1,0:T(8,128)(2,1)S(1)}, u32[]{:S(2)}, u32[]{:S(2)}) collective-permute-start(bf16[32,64,128]{2,1,0:T(8,128)(2,1)} %get-tuple-element.131), channel_id=1, source_target_pairs={{0,1},{1,2},{2,3},{3,4},{4,5},{5,6},{6,7},{7,0},{8,9},{9,10},{10,1... | collective-permute-start | bytes 1572872 | tf_op jit(solution)/shard_map/ppermute | solution.py:282
  175.6 38.5 %collective-permute-start.26 = (bf16[16,64,128]{2,1,0:T(8,128)(2,1)}, bf16[16,64,128]{2,1,0:T(8,128)(2,1)S(1)}, u32[]{:S(2)}, u32[]{:S(2)}) collective-permute-start(bf16[16,64,128]{2,1,0:T(8,128)(2,1)} %get-tuple-element.129), channel_id=1, source_target_pairs={{0,5},{1,6},{2,7},{3,0},{4,1},{5,2},{6,3},{7,4},{8,13},{9,14},{10,... | collective-permute-start | bytes 786440 | tf_op jit(solution)/shard_map/ppermute | solution.py:282
  176.8 40.0 %collective-permute-start.28 = (bf16[16,64,128]{2,1,0:T(8,128)(2,1)}, bf16[16,64,128]{2,1,0:T(8,128)(2,1)S(1)}, u32[]{:S(2)}, u32[]{:S(2)}) collective-permute-start(bf16[16,64,128]{2,1,0:T(8,128)(2,1)} %get-tuple-element.135), channel_id=1, source_target_pairs={{0,2},{1,3},{2,4},{3,5},{4,6},{5,7},{6,0},{7,1},{8,10},{9,11},{10,... | collective-permute-start | bytes 786440 | tf_op jit(solution)/shard_map/ppermute | solution.py:282
  199.5 17.3 %collective-permute-start.29 = (bf16[16,64,128]{2,1,0:T(8,128)(2,1)}, bf16[16,64,128]{2,1,0:T(8,128)(2,1)S(1)}, u32[]{:S(2)}, u32[]{:S(2)}) collective-permute-start(bf16[16,64,128]{2,1,0:T(8,128)(2,1)} %get-tuple-element.136), channel_id=1, source_target_pairs={{0,3},{1,4},{2,5},{3,6},{4,7},{5,0},{6,1},{7,2},{8,11},{9,12},{10,... | collective-permute-start | bytes 786440 | tf_op jit(solution)/shard_map/ppermute | solution.py:282
  216.7 12.0 %collective-permute-start.31 = (f32[8,128,128]{2,1,0:T(8,128)S(1)}, f32[8,128,128]{2,1,0:T(8,128)S(1)}, u32[]{:S(2)}, u32[]{:S(2)}) collective-permute-start(f32[8,128,128]{2,1,0:T(8,128)S(1)} %gram.7), channel_id=1, source_target_pairs={{0,7},{1,0},{2,1},{3,2},{4,3},{5,4},{6,5},{7,6},{8,15},{9,8},{10,9... | collective-permute-start | bytes 1572872 | tf_op jit(solution)/shard_map/ppermute | solution.py:282
  219.5 11.8 %collective-permute-start.30 = (f32[8,128,128]{2,1,0:T(8,128)S(1)}, f32[8,128,128]{2,1,0:T(8,128)S(1)}, u32[]{:S(2)}, u32[]{:S(2)}) collective-permute-start(f32[8,128,128]{2,1,0:T(8,128)S(1)} %gram.5), channel_id=1, source_target_pairs={{0,1},{1,2},{2,3},{3,4},{4,5},{5,6},{6,7},{7,0},{8,9},{9,10},{10,1... | collective-permute-start | bytes 1572872 | tf_op jit(solution)/shard_map/ppermute | solution.py:282
  (23 other events, 330.8 us)
Sparse Core Ops, SparseCore 0:
  28.0 52.3 all-gather.1
